TPU v7x, 32 devices: a whole 2x2x4 slice. The times are simulated.
32 devices in a mesh: dp: 8 (over z, y), tensor: 4 (over x, core).
Axes of the slice: x: 2, y: 2, z: 4, core: 2. Of those that a mesh axis runs over, the one named last changes fastest.
Arguments:
- tokens: bfloat16 [8192, 1152], P('dp'), may hold values from -6 to 6
- condition: bfloat16 [16, 1152], replicated, may hold values from -6 to 6
- latent_lengths: int32 [16], replicated, may hold values from 1 to 1024, as said below
- in_weight: bfloat16 [1152, 3, 1152], P(None, None, 'tensor'), may hold values from -0.1875 to 0.1875
- in_bias: bfloat16 [2, 1152], P(None, 'tensor'), may hold values from -3 to 3
- out_weight: bfloat16 [1152, 1152], P(None, 'tensor'), may hold values from -1.5 to 1.5
- out_bias: bfloat16 [1152], replicated, may hold values from -3 to 3
- up_weight: bfloat16 [1152, 4608], P(None, 'tensor'), may hold values from -0.1875 to 0.1875
- up_bias: bfloat16 [4608], P('tensor'), may hold values from -3 to 3
- down_weight: bfloat16 [1152, 4608], P(None, 'tensor'), may hold values from -0.09375 to 0.09375
- down_bias: bfloat16 [1152], replicated, may hold values from -3 to 3
- mod_weight: bfloat16 [1152, 6912], P(None, 'tensor'), may hold values from -0.1875 to 0.1875
- mod_bias: bfloat16 [6912], P('tensor'), may hold values from -3 to 3
- out_grad: bfloat16 [8192, 1152], P('dp'), may hold values from -6 to 6
Outputs:
- output: bfloat16 [8192, 1152], P(('dp', 'tensor'))
- grad_tokens: float32 [8192, 1152], P('dp', 'tensor')
- grad_condition: float32 [16, 1152], P('dp', 'tensor')
- grad_in_weight: float32 [1152, 3, 1152], P('dp', None, 'tensor')
- grad_in_bias: float32 [2, 1152], P(None, 'tensor')
- grad_out_weight: float32 [1152, 1152], P('dp', 'tensor')
- grad_out_bias: float32 [1152], replicated
- grad_up_weight: float32 [1152, 4608], P('dp', 'tensor')
- grad_up_bias: float32 [4608], P('tensor')
- grad_down_weight: float32 [1152, 4608], P('dp', 'tensor')
- grad_down_bias: float32 [1152], replicated
- grad_mod_weight: float32 [1152, 6912], P('dp', 'tensor')
- grad_mod_bias: float32 [6912], P('tensor')
Inputs may be any that keep to these rules, and one draw needn't show every extreme that they name: `latent_lengths`: lengths of the 16 latents in stream order; they sum to 8192.
All inputs are finite; a program needn't handle non-finite values.
Results may differ from a plain program's by a relative error of at most 0.017.
Values may be sent and summed in bfloat16 or wider, within the bound.
No kernel may reach another device: no remote copies, remote signals or barrier semaphores. Data moves between devices by JAX's collectives and lax.ppermute only.
A program may use at most 256 MiB of HBM per device.

v0:
```python
import functools
import math

import jax
import jax.numpy as jnp
from jax import lax
from jax.experimental import pallas as pl
from jax.experimental.pallas import tpu as pltpu
from jax.sharding import PartitionSpec as P

HD = 72
FACTOR = HD ** (-0.5)
LOG2E = math.log2(math.e)
NEG = -1e30
BQ = 256
BK = 256
F32 = jnp.float32
BF16 = jnp.bfloat16


def contract(a, b, dims):
    return lax.dot_general(a, b, (dims, ((), ())), preferred_element_type=F32)


def forward_kernel(bases, heads, last, bounds, span, query, mixed_in, top_in, total_in, *refs):
    segments = len(bases)
    keys = refs[:segments]
    values = refs[segments : 2 * segments]
    mixed_out, top_out, total_out, mixed = refs[2 * segments :]
    rows = query.shape[2]
    scale = FACTOR * LOG2E

    def query_block(i, _):
        own = pl.ds(pl.multiple_of(i * BQ, BQ), BQ)
        begin = span[0:1, own]
        end = span[1:2, own]
        for h in range(heads):
            mixed[h] = mixed_in[h, :, own]
        state = tuple(top_in[h, :, own] for h in range(heads)) + tuple(
            total_in[h, :, own] for h in range(heads)
        )
        for s, base in enumerate(bases):

            def key_block(j, state, s=s, base=base):
                k_at = pl.multiple_of(j * BK, BK)
                block = pl.ds(k_at, BK)
                place = lax.broadcasted_iota(jnp.int32, (BK, BQ), 0) + (k_at + base)
                allowed = (place >= begin) & (place < end)
                raws = [
                    contract(keys[s][h, :, block], query[h, :, own], ((0,), (0,)))
                    for h in range(heads)
                ]
                tops, totals, shrinks, lows = [], [], [], []
                for h in range(heads):
                    raw = jnp.where(allowed, raws[h] * scale, NEG)
                    top = jnp.maximum(state[h], jnp.max(raw, axis=0, keepdims=True))
                    probs = jnp.exp2(raw - top)
                    shrink = jnp.exp2(state[h] - top)
                    tops.append(top)
                    totals.append(state[heads + h] * shrink + jnp.sum(probs, axis=0, keepdims=True))
                    shrinks.append(shrink)
                    lows.append(probs.astype(BF16))
                for h in range(heads):
                    mixed[h] = mixed[h] * shrinks[h] + contract(
                        values[s][h, :, block], lows[h], ((1,), (0,))
                    )
                return tuple(tops) + tuple(totals)

            state = lax.fori_loop(bounds[s, 0, i], bounds[s, 1, i], key_block, state)
        for h in range(heads):
            top, total = state[h], state[heads + h]
            if last:
                mixed_out[h, :, own] = (mixed[h] / total).astype(BF16)
                top_out[h, :, own] = top + jnp.log2(total)
            else:
                mixed_out[h, :, own] = mixed[h]
                top_out[h, :, own] = top
            total_out[h, :, own] = total
        return 0

    lax.fori_loop(0, rows // BQ, query_block, 0)


def attend(bounds, span, query, carried, keys, values, bases, last):
    heads, hd, rows = query.shape
    vmem = pl.BlockSpec(memory_space=pltpu.VMEM)
    line = jax.ShapeDtypeStruct((heads, 1, rows), F32)
    return pl.pallas_call(
        functools.partial(forward_kernel, bases, heads, last),
        out_shape=(
            jax.ShapeDtypeStruct((heads, hd, rows), BF16 if last else F32),
            line,
            line,
        ),
        in_specs=[pl.BlockSpec(memory_space=pltpu.SMEM)] + [vmem] * (5 + 2 * len(bases)),
        out_specs=(vmem,) * 3,
        scratch_shapes=[pltpu.VMEM((heads, hd, BQ), F32)],
        compiler_params=pltpu.CompilerParams(vmem_limit_bytes=40 << 20),
        cost_estimate=pl.CostEstimate(flops=1 << 20, bytes_accessed=1 << 20, transcendentals=0),
    )(bounds, span, query, *carried, *keys, *values)


def tile_back(heads, allowed, keys, values, query, grad, logsum, delta):
    scale = FACTOR * LOG2E
    raws = [contract(keys[h], query[h], ((0,), (0,))) for h in range(heads)]
    grads = [contract(values[h], grad[h], ((0,), (0,))) for h in range(heads)]
    found = []
    for h in range(heads):
        raw = jnp.where(allowed, raws[h] * scale - logsum[h], NEG)
        probs = jnp.exp2(raw)
        found.append((probs.astype(BF16), (probs * (grads[h] - delta[h])).astype(BF16)))
    return found


def backward_kernel(bases, heads, bounds, span, query, grad, logsum, delta, *refs):
    segments = len(bases)
    keys = refs[:segments]
    values = refs[segments : 2 * segments]
    grad_query, grad_keys, grad_values, sum_query, sum_keys, sum_values = refs[2 * segments :]
    sum_query[...] = jnp.zeros_like(sum_query)
    for s, base in enumerate(bases):

        def key_block(j, _, s=s, base=base):
            k_at = pl.multiple_of(j * BK, BK)
            block = pl.ds(k_at, BK)
            place = lax.broadcasted_iota(jnp.int32, (BK, BQ), 0) + (k_at + base)
            if base == 0:
                sum_keys[...] = jnp.zeros_like(sum_keys)
                sum_values[...] = jnp.zeros_like(sum_values)

            def query_block(i, _):
                own = pl.ds(pl.multiple_of(i * BQ, BQ), BQ)
                allowed = (place >= span[0:1, own]) & (place < span[1:2, own])
                q = [query[h, :, own] for h in range(heads)]
                g = [grad[h, :, own] for h in range(heads)]
                k = [keys[s][h, :, block] for h in range(heads)]
                found = tile_back(
                    heads,
                    allowed,
                    k,
                    [values[s][h, :, block] for h in range(heads)],
                    q,
                    g,
                    [logsum[h, :, own] for h in range(heads)],
                    [delta[h, :, own] for h in range(heads)],
                )
                for h in range(heads):
                    probs, grad_raw = found[h]
                    if base == 0:
                        sum_values[h] += contract(g[h], probs, ((1,), (1,)))
                        sum_keys[h] += contract(q[h], grad_raw, ((1,), (1,)))
                    sum_query[h, :, own] += contract(k[h], grad_raw, ((1,), (0,)))
                return 0

            lax.fori_loop(bounds[s, 0, j], bounds[s, 1, j], query_block, 0)
            if base == 0:
                for h in range(heads):
                    grad_keys[h, :, block] = sum_keys[h]
                    grad_values[h, :, block] = sum_values[h]
            return 0

        lax.fori_loop(0, keys[s].shape[2] // BK, key_block, 0)
    grad_query[...] = (sum_query[...] * FACTOR).astype(BF16)


def attend_back(bounds, span, query, grad, logsum, delta, keys, values, bases):
    heads, hd, rows = query.shape
    vmem = pl.BlockSpec(memory_space=pltpu.VMEM)
    full = jax.ShapeDtypeStruct((heads, hd, rows), F32)
    return pl.pallas_call(
        functools.partial(backward_kernel, bases, heads),
        out_shape=(jax.ShapeDtypeStruct((heads, hd, rows), BF16), full, full),
        in_specs=[pl.BlockSpec(memory_space=pltpu.SMEM)] + [vmem] * (5 + 2 * len(bases)),
        out_specs=(vmem,) * 3,
        scratch_shapes=[
            pltpu.VMEM((heads, hd, rows), F32),
            pltpu.VMEM((heads, hd, BK), F32),
            pltpu.VMEM((heads, hd, BK), F32),
        ],
        compiler_params=pltpu.CompilerParams(vmem_limit_bytes=44 << 20),
        cost_estimate=pl.CostEstimate(flops=1 << 20, bytes_accessed=1 << 20, transcendentals=0),
    )(bounds, span, query, grad, logsum, delta, *keys, *values)


def others_kernel(segments, heads, bounds, keys, values, keys_in, values_in, *refs):
    spans, query, grad, logsum, delta = (refs[n * segments : (n + 1) * segments] for n in range(5))
    grad_keys, grad_values, sum_keys, sum_values = refs[5 * segments :]

    def key_block(j, _):
        k_at = pl.multiple_of(j * BK, BK)
        block = pl.ds(k_at, BK)
        place = lax.broadcasted_iota(jnp.int32, (BK, BQ), 0) + k_at
        for h in range(heads):
            sum_keys[h] = keys_in[h, :, block]
            sum_values[h] = values_in[h, :, block]
        for s in range(segments):

            def query_block(i, _, s=s):
                own = pl.ds(pl.multiple_of(i * BQ, BQ), BQ)
                allowed = (place >= spans[s][0:1, own]) & (place < spans[s][1:2, own])
                q = [query[s][h, :, own] for h in range(heads)]
                g = [grad[s][h, :, own] for h in range(heads)]
                found = tile_back(
                    heads,
                    allowed,
                    [keys[h, :, block] for h in range(heads)],
                    [values[h, :, block] for h in range(heads)],
                    q,
                    g,
                    [logsum[s][h, :, own] for h in range(heads)],
                    [delta[s][h, :, own] for h in range(heads)],
                )
                for h in range(heads):
                    probs, grad_raw = found[h]
                    sum_values[h] += contract(g[h], probs, ((1,), (1,)))
                    sum_keys[h] += contract(q[h], grad_raw, ((1,), (1,)))
                return 0

            lax.fori_loop(bounds[s, 0, j], bounds[s, 1, j], query_block, 0)
        for h in range(heads):
            grad_keys[h, :, block] = (sum_keys[h] * FACTOR).astype(BF16)
            grad_values[h, :, block] = sum_values[h].astype(BF16)
        return 0

    lax.fori_loop(0, keys.shape[2] // BK, key_block, 0)


def others_back(bounds, keys, values, keys_in, values_in, spans, query, grad, logsum, delta):
    heads, hd, rows = keys.shape
    segments = len(query)
    vmem = pl.BlockSpec(memory_space=pltpu.VMEM)
    shape = jax.ShapeDtypeStruct((heads, hd, rows), BF16)
    return pl.pallas_call(
        functools.partial(others_kernel, segments, heads),
        out_shape=(shape, shape),
        in_specs=[pl.BlockSpec(memory_space=pltpu.SMEM)] + [vmem] * (4 + 5 * segments),
        out_specs=(vmem, vmem),
        scratch_shapes=[pltpu.VMEM((heads, hd, BK), F32), pltpu.VMEM((heads, hd, BK), F32)],
        compiler_params=pltpu.CompilerParams(vmem_limit_bytes=40 << 20),
        cost_estimate=pl.CostEstimate(flops=1 << 20, bytes_accessed=1 << 20, transcendentals=0),
    )(bounds, keys, values, keys_in, values_in, *spans, *query, *grad, *logsum, *delta)


def swap(value, axis, bit):
    return lax.ppermute(value, axis, [(i, i ^ bit) for i in range(lax.axis_size(axis))])


def shift(value, axis, distance):
    devices = range(lax.axis_size(axis))
    return lax.ppermute(value, axis, [(i, i + distance) for i in devices if i + distance in devices])


def bits_of(axis):
    size = lax.axis_size(axis)
    return [1 << b for b in range(size.bit_length() - 1)]


def bit_set(axis, bit):
    return (lax.axis_index(axis) & bit) != 0


def sum_all(value, axis):
    for bit in bits_of(axis):
        value = value + swap(value, axis, bit)
    return value


def after(anchor, *values):
    held = values if anchor is None else lax.optimization_barrier((anchor, *values))[1:]
    return held[0] if len(values) == 1 else held


def in_order(mine, other, upper, dim=0):
    return jnp.where(
        upper, jnp.stack([other, mine], axis=dim), jnp.stack([mine, other], axis=dim)
    )


def gather_tensor(value):
    pair = in_order(value, swap(value, "tensor", 2), bit_set("tensor", 2))
    quad = in_order(pair, swap(pair, "tensor", 1), bit_set("tensor", 1), dim=1)
    return quad.reshape((4 * value.shape[0],) + value.shape[1:])


def scatter_tensor(partial):
    n = partial.shape[0] // 4
    core = lax.axis_index("tensor") % 2
    across = lax.axis_index("tensor") // 2
    parts = partial.astype(BF16).reshape((2, 2, n) + partial.shape[1:])
    kept = lax.dynamic_index_in_dim(parts, core, 1, keepdims=False)
    sent = lax.dynamic_index_in_dim(parts, 1 - core, 1, keepdims=False)
    come = swap(sent, "tensor", 1)
    come = after((yield sent), come)
    half = kept.astype(F32) + come.astype(F32)
    half_low = half.astype(BF16)
    stay = lax.dynamic_index_in_dim(half, across, 0, keepdims=False)
    leave = lax.dynamic_index_in_dim(half_low, 1 - across, 0, keepdims=False)
    come = swap(leave, "tensor", 2)
    come = after((yield leave), come)
    return stay + come.astype(F32)


def scatter_data(partials):
    joined = jnp.concatenate([partial.astype(BF16) for partial in partials], axis=1)
    found = lax.psum_scatter(joined, "dp", scatter_dimension=0, tiled=True).astype(F32)
    cuts, at = [], 0
    for partial in partials[:-1]:
        at += partial.shape[1]
        cuts.append(at)
    return jnp.split(found, cuts, axis=1)


def finish(steps, anchor=None):
    try:
        while True:
            steps.send(anchor)
    except StopIteration as end:
        return end.value


def layer_norm(value):
    center = value - jnp.mean(value, axis=-1, keepdims=True)
    spread = jnp.mean(center * center, axis=-1, keepdims=True)
    return center * lax.rsqrt(spread + 1e-06)


def gelu_tanh(value):
    return jax.nn.gelu(value, approximate=True)


def onehot_sum(select, values, form):
    upper = values.astype(BF16)
    lower = (values - upper.astype(F32)).astype(BF16)
    first = jnp.einsum(form, select, upper, preferred_element_type=F32)
    return first + jnp.einsum(form, select, lower, preferred_element_type=F32)


def on_device(
    tokens,
    condition,
    latent_lengths,
    in_weight,
    in_bias,
    out_weight,
    out_bias,
    up_weight,
    up_bias,
    down_weight,
    down_bias,
    mod_weight,
    mod_bias,
    out_grad,
):
    rows, width = tokens.shape
    latents = condition.shape[0]
    local_width = in_weight.shape[2]
    heads = local_width // HD
    data_size = lax.axis_size("dp")
    data_index = lax.axis_index("dp")
    tensor_index = lax.axis_index("tensor")
    quarter = rows // 4
    row_start = tensor_index * quarter

    def mine(value):
        return lax.dynamic_slice_in_dim(value, row_start, quarter, 0)

    places = jnp.arange(latents, dtype=jnp.int32)
    earlier = places[None, :] < places[:, None]
    starts = jnp.sum(jnp.where(earlier, latent_lengths[None, :], 0), axis=1)
    ends = starts + latent_lengths
    first_row = data_index * rows
    own_places = first_row + jnp.arange(rows, dtype=jnp.int32)

    def span_of(at):
        inside = (at[:, None] >= starts[None, :]) & (at[:, None] < ends[None, :])
        begin = jnp.sum(jnp.where(inside, starts[None, :] - first_row, 0), axis=1)
        end = jnp.sum(jnp.where(inside, ends[None, :] - first_row, 0), axis=1)
        return begin, end, inside

    bases = (-rows, 0, rows)
    windows = [span_of(own_places + base) for base in bases]
    spans = [jnp.stack(window[:2]) for window in windows]
    selects = [window[2].astype(BF16) for window in windows]
    begin, end = windows[1][:2]
    span, select = spans[1], selects[1]
    select_mine = mine(select)
    forward_bounds, backward_bounds, other_bounds = [], [], []
    for base in bases:
        low = jnp.clip(begin[::BQ] - base, 0, rows) // BK
        high = (jnp.clip(end[BQ - 1 :: BQ] - base, 0, rows) + BK - 1) // BK
        forward_bounds.append(jnp.stack([low, high]))
        key_at = first_row + base + jnp.arange(rows // BK, dtype=jnp.int32) * BK
        low = jnp.clip(span_of(key_at)[0], 0, rows) // BQ
        high = (jnp.clip(span_of(key_at + BK - 1)[1], 0, rows) + BQ - 1) // BQ
        valid = (key_at >= 0) & (key_at < rows * data_size)
        backward_bounds.append(jnp.where(valid[None, :], jnp.stack([low, high]), 0))
        low = jnp.clip(begin[::BK] - base, 0, rows) // BQ
        high = (jnp.clip(end[BK - 1 :: BK] - base, 0, rows) + BQ - 1) // BQ
        other_bounds.append(jnp.stack([low, high]))
    backward_bounds = jnp.stack(backward_bounds)
    other_bounds = jnp.stack([other_bounds[0], other_bounds[2]])

    tokens_mine = mine(tokens)
    behind_tokens = gather_tensor(shift(tokens_mine, "dp", 1))
    ahead_tokens = gather_tensor(shift(tokens_mine, "dp", -1))

    cond_full = condition.astype(F32)
    silu_cond = jax.nn.silu(cond_full).astype(BF16)
    mod_local = (
        jnp.dot(silu_cond, mod_weight, preferred_element_type=F32) + mod_bias.astype(F32)
    ).astype(BF16)
    modulation = gather_tensor(mod_local[None])
    modulation = modulation.transpose(1, 0, 2).reshape(latents, 6 * width)

    def spread(chosen, first, count):
        return jnp.dot(
            chosen,
            modulation[:, first * width : (first + count) * width],
            preferred_element_type=BF16,
        )

    others = spread(select_mine, 2, 4).astype(F32)
    gate_a, shift_m, scale_m, gate_m = (others[:, i * width : (i + 1) * width] for i in range(4))
    gate_m_all = spread(select, 5, 1).astype(F32)

    bias_full = in_bias.astype(F32)
    proj_bias = jnp.stack([bias_full[0], jnp.zeros_like(bias_full[0]), bias_full[1]])

    def entry_of(rows_of, chosen):
        shift_scale = spread(chosen, 0, 2)
        scale = shift_scale[:, width:].astype(F32)
        value = rows_of.astype(F32)
        center = value - jnp.mean(value, axis=-1, keepdims=True)
        inverse = lax.rsqrt(jnp.mean(center * center, axis=-1, keepdims=True) + 1e-06)
        normed = center * inverse
        entry = (normed * (1.0 + scale) + shift_scale[:, :width].astype(F32)).astype(BF16)
        return entry, normed, inverse

    def project(entry):
        found = jnp.einsum("dcf,td->cft", in_weight, entry, preferred_element_type=F32)
        found = (found + proj_bias[:, :, None]).astype(BF16)
        return found.reshape(3, heads, HD, rows)

    entry, normed, inverse = entry_of(tokens, select)
    normed_turned, inverse = normed.T, inverse.T
    own = project(entry)
    sides = [
        project(entry_of(behind_tokens, selects[0])[0]),
        project(entry_of(ahead_tokens, selects[2])[0]),
    ]
    query = own[0]
    line = jnp.zeros((heads, 1, rows), F32)
    carried = attend(
        jnp.stack([forward_bounds[1]]),
        span,
        query,
        (jnp.zeros((heads, HD, rows), F32), line + NEG, line),
        [own[1]],
        [own[2]],
        (0,),
        False,
    )
    attended, logsum, _ = attend(
        jnp.stack([forward_bounds[0], forward_bounds[2]]),
        span,
        query,
        carried,
        [side[1] for side in sides],
        [side[2] for side in sides],
        (-rows, rows),
        True,
    )
    attended_flat = attended.reshape(local_width, rows)
    attn_part = lax.dot_general(
        attended_flat, out_weight, (((0,), (1,)), ((), ())), preferred_element_type=F32
    )
    attn_steps = scatter_tensor(attn_part)
    next(attn_steps)
    branch = finish(attn_steps) + out_bias.astype(F32)

    middle = tokens_mine.astype(F32) + gate_a * branch
    normed_m, norm_back_m = jax.vjp(layer_norm, middle)
    entry_m = gather_tensor((normed_m * (1.0 + scale_m) + shift_m).astype(BF16))
    hidden_pre = jnp.dot(entry_m, up_weight, preferred_element_type=F32) + up_bias.astype(F32)
    hidden_full, gelu_back = jax.vjp(gelu_tanh, hidden_pre)
    hidden = hidden_full.astype(BF16)
    grad_out = out_grad.astype(F32)
    grad_branch_m = (gate_m_all * grad_out).astype(BF16)
    grad_hidden = jnp.einsum("td,df->tf", grad_branch_m, down_weight, preferred_element_type=F32)
    grad_pre = gelu_back(grad_hidden)[0].astype(BF16)
    grad_down_w = jnp.einsum("td,tf->df", grad_branch_m, hidden, preferred_element_type=F32)
    entry_part = jnp.einsum("tf,df->td", grad_pre, up_weight, preferred_element_type=F32)
    entry_steps = scatter_tensor(entry_part)
    grad_pre = after(next(entry_steps), grad_pre)
    grad_out_mine = mine(out_grad).astype(F32)
    grad_up_w = jnp.einsum("td,tf->df", entry_m, grad_pre, preferred_element_type=F32)
    sum_down_w, sum_up_w = scatter_data([grad_down_w, grad_up_w])
    grad_entry_m = finish(entry_steps)
    grad_down_b = jnp.sum(grad_branch_m.astype(F32), axis=0)
    grad_up_b = jnp.sum(grad_pre.astype(F32), axis=0)
    grad_middle = grad_out_mine + norm_back_m(grad_entry_m * (1.0 + scale_m))[0]
    grad_gate_a = grad_middle * branch
    grad_branch_mine = (gate_a * grad_middle).astype(BF16)
    grad_out_b = jnp.sum(grad_branch_mine.astype(F32), axis=0)
    grad_branch = gather_tensor(grad_branch_mine)
    grad_attended = lax.dot_general(
        out_weight, grad_branch, (((0,), (1,)), ((), ())), preferred_element_type=F32
    ).astype(BF16)

    mlp_part = jnp.einsum(
        "tf,df->td",
        after(grad_branch_mine, hidden),
        down_weight,
        preferred_element_type=F32,
    )
    mlp_steps = scatter_tensor(mlp_part)
    next(mlp_steps)

    grad_heads = grad_attended.reshape(heads, HD, rows)
    delta = jnp.sum(grad_heads.astype(F32) * attended.astype(F32), axis=1, keepdims=True)
    stats = jnp.stack([logsum, delta])
    side_grads = [shift(grad_heads, "dp", 1), shift(grad_heads, "dp", -1)]
    side_stats = [shift(stats, "dp", 1), shift(stats, "dp", -1)]
    grad_query, part_keys, part_values = attend_back(
        backward_bounds,
        span,
        query,
        grad_heads,
        logsum,
        delta,
        [sides[0][1], own[1], sides[1][1]],
        [sides[0][2], own[2], sides[1][2]],
        bases,
    )
    mlp_steps.send(grad_heads)
    branch_m = finish(mlp_steps, grad_query) + down_bias.astype(F32)
    output = (middle + gate_m * branch_m).astype(BF16)
    grad_gate_m = grad_out_mine * branch_m
    grad_out_w = lax.dot_general(
        grad_branch, attended_flat, (((0,), (1,)), ((), ())), preferred_element_type=F32
    )
    grad_keys, grad_values = others_back(
        other_bounds,
        own[1],
        own[2],
        part_keys,
        part_values,
        [spans[0], spans[2]],
        [side[0] for side in sides],
        side_grads,
        [side[0] for side in side_stats],
        [side[1] for side in side_stats],
    )
    grad_proj = [x.reshape(local_width, rows) for x in (grad_query, grad_keys, grad_values)]
    grad_q_w, grad_k_w, grad_v_w = (
        lax.dot_general(entry, x, (((0,), (1,)), ((), ())), preferred_element_type=F32)
        for x in grad_proj
    )
    sum_out_w, sum_q_w = scatter_data([grad_out_w, grad_q_w])
    sum_k_w, sum_v_w = scatter_data([grad_k_w, grad_v_w])
    grad_proj = after((grad_k_w, grad_v_w), *grad_proj)
    grad_in_b = jnp.stack([jnp.sum(grad_proj[c].astype(F32), axis=1) for c in (0, 2)])
    grad_entry = lax.dot_general(
        in_weight.reshape(width, 3 * local_width),
        jnp.concatenate(grad_proj, axis=0),
        (((1,), (0,)), ((), ())),
        preferred_element_type=F32,
    )

    scale_turned = lax.dot_general(
        modulation[:, width : 2 * width],
        select,
        (((0,), (1,)), ((), ())),
        preferred_element_type=BF16,
    ).astype(F32)
    scaled = grad_entry * (1.0 + scale_turned)
    input_part = (
        scaled
        - jnp.mean(scaled, axis=0, keepdims=True)
        - normed_turned * jnp.mean(scaled * normed_turned, axis=0, keepdims=True)
    ) * inverse

    split_terms = jnp.concatenate([grad_entry, grad_entry * normed_turned], axis=0)
    kept_terms = jnp.concatenate(
        [grad_gate_a, grad_entry_m, grad_entry_m * normed_m, grad_gate_m], axis=1
    )
    per_latent = jnp.concatenate(
        [onehot_sum(select, split_terms, "tl,mt->lm"), onehot_sum(select_mine, kept_terms, "tl,tm->lm")],
        axis=1,
    )
    columns_here = mod_weight.shape[1]
    arranged = per_latent.reshape(latents, 4, columns_here).transpose(1, 0, 2)

    out_b_row = jnp.pad(grad_out_b, (0, columns_here - width))[None]

    def for_device(flip):
        chosen = lax.dynamic_index_in_dim(arranged, tensor_index ^ flip, 0, keepdims=False)
        return jnp.concatenate([chosen, out_b_row])

    given = [for_device(flip) for flip in range(4)]
    come = [swap(given[flip], "tensor", flip) for flip in (1, 2, 3)]
    placed = lax.dynamic_update_slice_in_dim(
        jnp.zeros((width, rows), F32), grad_middle.T, row_start, 1
    )
    tokens_steps = scatter_tensor(input_part + placed)
    tokens_sent = next(tokens_steps)
    come = after(tokens_sent, *come)
    small = (given[0] + come[0]) + (come[1] + come[2])
    small = jnp.concatenate(
        [small]
        + [
            jnp.pad(value, (0, columns_here - value.shape[0]))[None]
            for value in (grad_in_b.reshape(-1), grad_up_b, grad_down_b)
        ]
    )
    tokens_sent = tokens_steps.send(small)
    for place, bit in enumerate(bits_of("dp")):
        come = swap(small, "dp", bit)
        if place == 0:
            come = after(tokens_sent, come)
        small = small + come
    grad_mod = small[:latents].astype(BF16)
    sum_out_b = small[latents, :width]
    sum_in_b = small[latents + 1, : 2 * local_width]
    sum_up_b = small[latents + 2, : grad_up_b.shape[0]]
    sum_down_b = small[latents + 3, :width]
    own_width = width // data_size
    own_silu = lax.dynamic_slice_in_dim(silu_cond, data_index * own_width, own_width, 1)
    grad_mod_w = jnp.einsum("ld,lm->dm", own_silu, grad_mod, preferred_element_type=F32)
    grad_mod_b = jnp.sum(grad_mod.astype(F32), axis=0)
    own_count = latents // data_size
    own_grad_mod = lax.dynamic_slice_in_dim(grad_mod, data_index * own_count, own_count, 0)
    own_cond = lax.dynamic_slice_in_dim(cond_full, data_index * own_count, own_count, 0)
    silu_grad = jnp.einsum("lm,dm->ld", own_grad_mod, mod_weight, preferred_element_type=F32)
    cond_part = jax.vjp(jax.nn.silu, own_cond)[1](silu_grad)[0]
    cond_parts = cond_part.reshape(own_count, 4, width // 4).transpose(1, 0, 2)
    grad_cond = lax.dynamic_index_in_dim(cond_parts, tensor_index, 0, keepdims=False)
    for bit in (1, 2, 3):
        grad_cond = grad_cond + swap(
            lax.dynamic_index_in_dim(cond_parts, tensor_index ^ bit, 0, keepdims=False),
            "tensor",
            bit,
        )

    grad_tokens = finish(tokens_steps, grad_mod_w).T
    sum_in_w = jnp.stack([sum_q_w, sum_k_w, sum_v_w], axis=1)
    return (
        output,
        grad_tokens,
        grad_cond,
        sum_in_w,
        sum_in_b.reshape(2, local_width),
        sum_out_w,
        sum_out_b,
        sum_up_w,
        sum_up_b,
        sum_down_w,
        sum_down_b,
        grad_mod_w,
        grad_mod_b,
    )


def solution(mesh):
    placed = (
        P("dp", None),
        P(),
        P(),
        P(None, None, "tensor"),
        P(None, "tensor"),
        P(None, "tensor"),
        P(),
        P(None, "tensor"),
        P("tensor"),
        P(None, "tensor"),
        P(),
        P(None, "tensor"),
        P("tensor"),
        P("dp", None),
    )
    return jax.shard_map(
        on_device,
        mesh=mesh,
        in_specs=placed,
        out_specs=(
            P(("dp", "tensor"), None),
            P("dp", "tensor"),
            P("dp", "tensor"),
            P("dp", None, "tensor"),
            P(None, "tensor"),
            P("dp", "tensor"),
            P(),
            P("dp", "tensor"),
            P("tensor"),
            P("dp", "tensor"),
            P(),
            P("dp", "tensor"),
            P("tensor"),
        ),
        check_vma=False,
    )
```

profile of v0, /device:TPU:0, one launch (start us, length us, event | category | flops | bytes accessed | tf_op | source)
XLA Modules:
  0.0 513.1 jit_solution(14105305175340060675)
XLA Ops:
  9.3 5.7 %collective-permute-start.2 = (bf16[256,1152]{1,0:T(8,128)(2,1)}, bf16[256,1152]{1,0:T(8,128)(2,1)}, u32[]{:S(2)}, u32[]{:S(2)}) collective-permute-start(bf16[256,1152]{1,0:T(8,128)(2,1)} %constant_dynamic-slice_fusion.10), channel_id=1, source_target_pairs={{0,4},{4,8},{8,12},{12,16},{16,20},{20,24},{24,28},{1,5},{5,9},{9,... | collective-permute-start | bytes 1769480 | tf_op jit(solution)/shard_map/ppermute | solution.py:250
  17.0 3.3 fusion.42
  35.6 2.5 fusion.43
  41.2 9.8 %collective-permute-done.6 = bf16[256,1152]{1,0:T(8,128)(2,1)S(1)} collective-permute-done((bf16[256,1152]{1,0:T(8,128)(2,1)S(1)}, bf16[256,1152]{1,0:T(8,128)(2,1)S(1)}, u32[]{:S(2)}, u32[]{:S(2)}) %collective-permute-start.6) | collective-permute-done | bytes 589856 | tf_op jit(solution)/shard_map/ppermute | solution.py:245
  51.6 9.1 %shard_map.237 = (f32[4,72,1024]{2,1,0:T(8,128)S(1)}, f32[4,1,1024]{2,1,0:T(1,128)S(1)}, f32[4,1,1024]{2,1,0:T(1,128)S(1)}) custom-call(s32[1,2,4]{2,1,0:T(2,128)S(1)} %add_bitcast_fusion.2.bounds, s32[2,1024]{1,0:T(2,128)S(1)} %pad_add_fusion.span, bf16[4,72,1024]{2,1,0:T(8,128)(2,1)S(1)} %bitcast.368, f32[4,72,1024]{2,1,0:T(8,128)S(1)} %broadcast_in_dim.212.mixed_in, ...), custom_call_target="tpu_custom_call" | custom-call | flops 1048576 | bytes 1048576 | tf_op jit(solution)/shard_map/pallas_call | solution.py:88
  73.1 2.5 fusion.44
  78.5 2.5 fusion.45
  81.9 3.5 shard_map.238
  90.0 2.8 collective-permute-done.8
  98.4 14.4 %collective-permute-done.9 = bf16[256,1152]{1,0:T(8,128)(2,1)} collective-permute-done((bf16[256,1152]{1,0:T(8,128)(2,1)}, bf16[256,1152]{1,0:T(8,128)(2,1)}, u32[]{:S(2)}, u32[]{:S(2)}) %collective-permute-start.9) | collective-permute-done | bytes 589856 | tf_op jit(solution)/shard_map/ppermute | solution.py:245
  116.0 14.2 %collective-permute-done.10 = bf16[256,1152]{1,0:T(8,128)(2,1)S(1)} collective-permute-done((bf16[256,1152]{1,0:T(8,128)(2,1)S(1)}, bf16[256,1152]{1,0:T(8,128)(2,1)S(1)}, u32[]{:S(2)}, u32[]{:S(2)}) %collective-permute-start.10) | collective-permute-done | bytes 589856 | tf_op jit(solution)/shard_map/ppermute | solution.py:245
  132.3 3.5 fusion.133
  136.4 6.7 %multiply_convert_fusion = (bf16[1024,1152]{1,0:T(8,128)(2,1)}, bf16[1024,1152]{1,0:T(8,128)(2,1)S(1)}) fusion(f32[1024,1152]{1,0:T(8,128)S(1)} %fusion.133, f32[1152]{0:T(1024)S(1)} %convert_element_type.326, bf16[1024,1152]{1,0:T(8,128)(2,1)S(1)} %bitcast.428, bf16[1152,1152]{1,0:T(8,128)(2,1)S(1)} %copy-done), kind=kOutput, calls=%fused_computation.48 | convolution fusion | flops 2745040896 | bytes 14455296 | tf_op jit(solution)/shard_map/dot_general | solution.py:484
  143.2 4.0 convolution_convert_fusion.5
  149.7 3.1 collective-permute-done.12
  156.4 14.9 %collective-permute-done.13 = bf16[256,1152]{1,0:T(8,128)(2,1)} collective-permute-done((bf16[256,1152]{1,0:T(8,128)(2,1)S(1)}, bf16[256,1152]{1,0:T(8,128)(2,1)}, u32[]{:S(2)}, u32[]{:S(2)}) %collective-permute-start.13) | collective-permute-done | bytes 589856 | tf_op jit(solution)/shard_map/ppermute | solution.py:245
  171.3 2.8 multiply_multiply_fusion.2
  178.1 3.4 convert_reduce_fusion.5
  182.4 13.7 %collective-permute-done.14 = bf16[256,1152]{1,0:T(8,128)(2,1)S(1)} collective-permute-done((bf16[256,1152]{1,0:T(8,128)(2,1)S(1)}, bf16[256,1152]{1,0:T(8,128)(2,1)S(1)}, u32[]{:S(2)}, u32[]{:S(2)}) %collective-permute-start.14) | collective-permute-done | bytes 589856 | tf_op jit(solution)/shard_map/ppermute | solution.py:245
  196.7 2.5 collective-permute-done.15
  203.7 14.3 %shard_map.239 = (bf16[4,72,1024]{2,1,0:T(8,128)(2,1)S(1)}, f32[4,72,1024]{2,1,0:T(8,128)S(1)}, f32[4,72,1024]{2,1,0:T(8,128)S(1)}) custom-call(s32[3,2,4]{2,1,0:T(2,128)S(1)} %pad_add_fusion.3.bounds, s32[2,1024]{1,0:T(2,128)S(1)} %pad_add_fusion.span, bf16[4,72,1024]{2,1,0:T(8,128)(2,1)S(1)} %bitcast.370, bf16[4,72,1024]{2,1,0:T(8,128)(2,1)S(1)} %bitcast.380, ...), custom_call_target="tpu_custom_call" | custom-call | flops 1048576 | bytes 1048576 | tf_op jit(solution)/shard_map/pallas_call | solution.py:170
  220.4 2.6 copy.83
  224.6 16.4 %collective-permute-start.18 = (bf16[4,72,1024]{2,1,0:T(8,128)(2,1)S(1)}, bf16[4,72,1024]{2,1,0:T(8,128)(2,1)S(1)}, u32[]{:S(2)}, u32[]{:S(2)}) collective-permute-start(bf16[4,72,1024]{2,1,0:T(8,128)(2,1)S(1)} %bitcast.382), channel_id=1, source_target_pairs={{0,4},{4,8},{8,12},{12,16},{16,20},{20,24},{24,28},{1,5},{5,9},{9,... | collective-permute-start | bytes 1769480 | tf_op jit(solution)/shard_map/ppermute | solution.py:250
  242.7 7.3 %convolution_convert_fusion.1 = bf16[1152,1152]{0,1:T(8,128)(2,1)} fusion(bf16[1024,1152]{1,0:T(8,128)(2,1)} %copy-done.50, bf16[1024,1152]{1,0:T(8,128)(2,1)} %get-tuple-element.40), kind=kOutput, calls=%fused_computation.4 | convolution fusion | flops 2719236096 | bytes 7372800 | tf_op jit(solution)/shard_map/td,tf->df/dot_general | solution.py:491
  249.9 10.8 %collective-permute-start.20 = (f32[2,4,1,1024]{3,2,1,0:T(1,128)S(1)}, f32[2,4,1,1024]{3,2,1,0:T(1,128)S(1)}, u32[]{:S(2)}, u32[]{:S(2)}) collective-permute-start(f32[2,4,1,1024]{3,2,1,0:T(1,128)S(1)} %pad_maximum_fusion.12), channel_id=1, source_target_pairs={{0,4},{4,8},{8,12},{12,16},{16,20},{20,24},{24,28},{1,5},{5,9},{9,... | collective-permute-start | bytes 98312 | tf_op jit(solution)/shard_map/ppermute | solution.py:250
  260.8 9.1 %collective-permute-done.20 = f32[2,4,1,1024]{3,2,1,0:T(1,128)S(1)} collective-permute-done((f32[2,4,1,1024]{3,2,1,0:T(1,128)S(1)}, f32[2,4,1,1024]{3,2,1,0:T(1,128)S(1)}, u32[]{:S(2)}, u32[]{:S(2)}) %collective-permute-start.20) | collective-permute-done | bytes 32800 | tf_op jit(solution)/shard_map/ppermute | solution.py:250
  270.0 3.4 shard_map.240
  277.2 5.8 %convolution_convert_fusion = bf16[1152,1152]{0,1:T(8,128)(2,1)S(1)} fusion(bf16[1024,1152]{1,0:T(8,128)(2,1)} %bitcast.429, bf16[1024,1152]{1,0:T(8,128)(2,1)} %copy-done.48), kind=kOutput, calls=%fused_computation.3 | convolution fusion | flops 2719236096 | bytes 7372800 | tf_op jit(solution)/shard_map/td,tf->df/dot_general | solution.py:496
  283.0 4.2 convolution_convert_fusion.4
  289.7 2.8 pad_maximum_fusion.1
  292.5 8.6 %copy.87 = bf16[1152,2304]{1,0:T(8,128)(2,1)} copy(bf16[1152,2304]{0,1:T(8,128)(2,1)} %pad_maximum_fusion.1) | data formatting | bytes 10616832
  306.9 3.0 convolution_bitcast_fusion
  312.1 9.2 %collective-permute-done.17 = bf16[256,1152]{1,0:T(8,128)(2,1)S(1)} collective-permute-done((bf16[256,1152]{1,0:T(8,128)(2,1)S(1)}, bf16[256,1152]{1,0:T(8,128)(2,1)S(1)}, u32[]{:S(2)}, u32[]{:S(2)}) %collective-permute-start.17) | collective-permute-done | bytes 589856 | tf_op jit(solution)/shard_map/ppermute | solution.py:245
  322.1 2.9 fusion.7
  328.1 4.5 copy.77
  332.7 3.3 convert_multiply_fusion
  336.0 2.9 fusion.52
  347.4 3.4 collective-permute-done.24
  350.8 4.4 collective-permute-done.23
  356.2 5.8 %collective-permute-start.26 = (f32[20,1728]{1,0:T(8,128)S(1)}, f32[20,1728]{1,0:T(8,128)S(1)}, u32[]{:S(2)}, u32[]{:S(2)}) collective-permute-start(f32[20,1728]{1,0:T(8,128)S(1)} %pad_maximum_fusion.11), channel_id=1, source_target_pairs={{0,4},{4,0},{8,12},{12,8},{16,20},{20,16},{24,28},{28,24},{1,5},{5... | collective-permute-start | bytes 414728 | tf_op jit(solution)/shard_map/ppermute | solution.py:245
  366.1 9.5 %collective-permute-start.27 = (f32[20,1728]{1,0:T(8,128)S(1)}, f32[20,1728]{1,0:T(8,128)S(1)}, u32[]{:S(2)}, u32[]{:S(2)}) collective-permute-start(f32[20,1728]{1,0:T(8,128)S(1)} %fusion.167), channel_id=1, source_target_pairs={{0,8},{4,12},{8,0},{12,4},{16,24},{20,28},{24,16},{28,20},{1,9},{5... | collective-permute-start | bytes 414728 | tf_op jit(solution)/shard_map/ppermute | solution.py:245
  375.6 6.3 %collective-permute-done.27 = f32[20,1728]{1,0:T(8,128)S(1)} collective-permute-done((f32[20,1728]{1,0:T(8,128)S(1)}, f32[20,1728]{1,0:T(8,128)S(1)}, u32[]{:S(2)}, u32[]{:S(2)}) %collective-permute-start.27) | collective-permute-done | bytes 138272 | tf_op jit(solution)/shard_map/ppermute | solution.py:245
  381.9 4.6 collective-permute-start.28
  388.4 3.4 collective-permute-done.28
  393.3 2.7 fusion.91
  408.5 87.7 %reduce-scatter.14.cloned.1.call-done = bf16[144,2304]{1,0:T(8,128)(2,1)} async-done(((bf16[1152,2304]{1,0:T(8,128)(2,1)}), bf16[144,2304]{1,0:T(8,128)(2,1)}) %reduce-scatter.14.cloned.1.call-update) | async-done | bytes 663568
  498.5 3.0 fusion.131
  501.5 2.4 copy.81
  (416 shorter events, 128.0 us)
Async XLA Ops:
  7.2 129.2 %copy-start = (bf16[1152,1152]{1,0:T(8,128)(2,1)S(1)}, bf16[1152,1152]{1,0:T(8,128)(2,1)}, u32[]{:S(2)}) copy-start(bf16[1152,1152]{1,0:T(8,128)(2,1)} %param.21) | copy-start | bytes 7962628
  7.2 396.9 %reduce-scatter.10.cloned.1.call-start = ((), (), s32[]{:S(2)}) async-start(), calls=%async_computation.3 | async-start | bytes 1658880
  9.3 30.4 %collective-permute-start.2 = (bf16[256,1152]{1,0:T(8,128)(2,1)}, bf16[256,1152]{1,0:T(8,128)(2,1)}, u32[]{:S(2)}, u32[]{:S(2)}) collective-permute-start(bf16[256,1152]{1,0:T(8,128)(2,1)} %constant_dynamic-slice_fusion.10), channel_id=1, source_target_pairs={{0,4},{4,8},{8,12},{12,16},{16,20},{20,24},{24,28},{1,5},{5,9},{9,... | collective-permute-start | bytes 1769480 | tf_op jit(solution)/shard_map/ppermute | solution.py:250
  15.0 19.7 %collective-permute-start.5 = (bf16[256,1152]{1,0:T(8,128)(2,1)}, bf16[256,1152]{1,0:T(8,128)(2,1)S(1)}, u32[]{:S(2)}, u32[]{:S(2)}) collective-permute-start(bf16[256,1152]{1,0:T(8,128)(2,1)} %constant_dynamic-slice_fusion.10), channel_id=1, source_target_pairs={{4,0},{8,4},{12,8},{16,12},{20,16},{24,20},{28,24},{5,1},{9,5},{13... | collective-permute-start | bytes 1769480 | tf_op jit(solution)/shard_map/ppermute | solution.py:250
  20.3 5.9 %collective-permute-start = (bf16[1,16,1728]{2,1,0:T(8,128)(2,1)S(1)}, bf16[1,16,1728]{2,1,0:T(8,128)(2,1)S(1)}, u32[]{:S(2)}, u32[]{:S(2)}) collective-permute-start(bf16[1,16,1728]{2,1,0:T(8,128)(2,1)S(1)} %bitcast.436), channel_id=1, source_target_pairs={{0,2},{1,3},{2,0},{3,1},{4,6},{5,7},{6,4},{7,5},{8,10},{9,11},{10,... | collective-permute-start | bytes 165896 | tf_op jit(solution)/shard_map/ppermute | solution.py:245
  26.3 1.4 collective-permute-start.1
  34.7 16.3 %copy-start.43 = (bf16[256,1152]{1,0:T(8,128)(2,1)}, bf16[256,1152]{1,0:T(8,128)(2,1)S(1)}, u32[]{:S(2)}) copy-start(bf16[256,1152]{1,0:T(8,128)(2,1)S(1)} %collective-permute-done.5) | copy-start | bytes 1769476
  34.8 16.2 %collective-permute-start.6 = (bf16[256,1152]{1,0:T(8,128)(2,1)S(1)}, bf16[256,1152]{1,0:T(8,128)(2,1)S(1)}, u32[]{:S(2)}, u32[]{:S(2)}) collective-permute-start(bf16[256,1152]{1,0:T(8,128)(2,1)S(1)} %collective-permute-done.5), channel_id=1, source_target_pairs={{0,2},{1,3},{2,0},{3,1},{4,6},{5,7},{6,4},{7,5},{8,10},{9,11},{10,... | collective-permute-start | bytes 1769480 | tf_op jit(solution)/shard_map/ppermute | solution.py:245
  39.7 23.1 %collective-permute-start.3 = (bf16[256,1152]{1,0:T(8,128)(2,1)}, bf16[256,1152]{1,0:T(8,128)(2,1)S(1)}, u32[]{:S(2)}, u32[]{:S(2)}) collective-permute-start(bf16[256,1152]{1,0:T(8,128)(2,1)} %collective-permute-done.2), channel_id=1, source_target_pairs={{0,2},{1,3},{2,0},{3,1},{4,6},{5,7},{6,4},{7,5},{8,10},{9,11},{10,... | collective-permute-start | bytes 1769480 | tf_op jit(solution)/shard_map/ppermute | solution.py:245
  51.2 14.9 %collective-permute-start.7 = (bf16[2,256,1152]{2,1,0:T(8,128)(2,1)S(1)}, bf16[2,256,1152]{2,1,0:T(8,128)(2,1)S(1)}, u32[]{:S(2)}, u32[]{:S(2)}) collective-permute-start(bf16[2,256,1152]{2,1,0:T(8,128)(2,1)S(1)} %maximum_select_fusion.6), channel_id=1, source_target_pairs={{0,1},{1,0},{2,3},{3,2},{4,5},{5,4},{6,7},{7,6},{8,9},{9,8},{10,11... | collective-permute-start | bytes 3538952 | tf_op jit(solution)/shard_map/ppermute | solution.py:245
  51.4 30.5 %copy-start.4 = (bf16[1,288,1024]{2,1,0:T(8,128)(2,1)}, bf16[1,288,1024]{2,1,0:T(8,128)(2,1)S(1)}, u32[]{:S(2)}) copy-start(bf16[1,288,1024]{2,1,0:T(8,128)(2,1)S(1)} %get-tuple-element.162) | copy-start | bytes 1769476
  64.3 2.9 collective-permute-start.4
  89.5 3.3 collective-permute-start.8
  96.9 15.9 %collective-permute-start.9 = (bf16[256,1152]{1,0:T(8,128)(2,1)}, bf16[256,1152]{1,0:T(8,128)(2,1)}, u32[]{:S(2)}, u32[]{:S(2)}) collective-permute-start(bf16[256,1152]{1,0:T(8,128)(2,1)} %fusion.69), channel_id=1, source_target_pairs={{0,2},{1,3},{2,0},{3,1},{4,6},{5,7},{6,4},{7,5},{8,10},{9,11},{10,... | collective-permute-start | bytes 1769480 | tf_op jit(solution)/shard_map/ppermute | solution.py:245
  98.4 16.4 %copy-start.31 = (f32[256,4608]{1,0:T(8,128)}, f32[256,4608]{1,0:T(8,128)S(1)}, u32[]{:S(2)}) copy-start(f32[256,4608]{1,0:T(8,128)S(1)} %convolution_convert_fusion.2) | copy-start | bytes 14155780
  114.8 15.7 %copy-start.65 = (f32[256]{0:T(256)}, f32[256]{0:T(256)S(1)}, u32[]{:S(2)}) copy-start(f32[256]{0:T(256)S(1)} %multiply_reduce_fusion.4) | copy-start | bytes 3076
  114.8 15.8 %copy-start.39 = (bf16[1024,1152]{1,0:T(8,128)(2,1)S(1)}, bf16[1024,1152]{1,0:T(8,128)(2,1)}, u32[]{:S(2)}) copy-start(bf16[1024,1152]{1,0:T(8,128)(2,1)} %param.27) | copy-start | bytes 7077892
  115.5 14.8 %collective-permute-start.10 = (bf16[256,1152]{1,0:T(8,128)(2,1)S(1)}, bf16[256,1152]{1,0:T(8,128)(2,1)S(1)}, u32[]{:S(2)}, u32[]{:S(2)}) collective-permute-start(bf16[256,1152]{1,0:T(8,128)(2,1)S(1)} %fusion.60), channel_id=1, source_target_pairs={{0,2},{1,3},{2,0},{3,1},{4,6},{5,7},{6,4},{7,5},{8,10},{9,11},{10,... | collective-permute-start | bytes 1769480 | tf_op jit(solution)/shard_map/ppermute | solution.py:245
  130.5 5.5 %collective-permute-start.11 = (bf16[2,256,1152]{2,1,0:T(8,128)(2,1)S(1)}, bf16[2,256,1152]{2,1,0:T(8,128)(2,1)S(1)}, u32[]{:S(2)}, u32[]{:S(2)}) collective-permute-start(bf16[2,256,1152]{2,1,0:T(8,128)(2,1)S(1)} %maximum_select_fusion.8), channel_id=1, source_target_pairs={{0,1},{1,0},{2,3},{3,2},{4,5},{5,4},{6,7},{7,6},{8,9},{9,8},{10,11... | collective-permute-start | bytes 3538952 | tf_op jit(solution)/shard_map/ppermute | solution.py:245
  149.7 3.1 collective-permute-start.12
  149.7 21.6 %copy-start.29 = (f32[256,1152]{1,0:T(8,128)S(1)}, f32[256,1152]{1,0:T(8,128)}, u32[]{:S(2)}) copy-start(f32[256,1152]{1,0:T(8,128)} %copy-done.28) | copy-start | bytes 3538948
  149.7 21.6 %copy-start.62 = (f32[256]{0:T(256)S(1)}, f32[256]{0:T(256)}, u32[]{:S(2)}) copy-start(f32[256]{0:T(256)} %copy-done.61) | copy-start | bytes 3076
  155.7 15.5 %collective-permute-start.13 = (bf16[256,1152]{1,0:T(8,128)(2,1)S(1)}, bf16[256,1152]{1,0:T(8,128)(2,1)}, u32[]{:S(2)}, u32[]{:S(2)}) collective-permute-start(bf16[256,1152]{1,0:T(8,128)(2,1)S(1)} %fusion.70), channel_id=1, source_target_pairs={{0,2},{1,3},{2,0},{3,1},{4,6},{5,7},{6,4},{7,5},{8,10},{9,11},{10,... | collective-permute-start | bytes 1769480 | tf_op jit(solution)/shard_map/ppermute | solution.py:245
  181.5 14.5 %collective-permute-start.14 = (bf16[256,1152]{1,0:T(8,128)(2,1)S(1)}, bf16[256,1152]{1,0:T(8,128)(2,1)S(1)}, u32[]{:S(2)}, u32[]{:S(2)}) collective-permute-start(bf16[256,1152]{1,0:T(8,128)(2,1)S(1)} %get-tuple-element.140), channel_id=1, source_target_pairs={{0,2},{1,3},{2,0},{3,1},{4,6},{5,7},{6,4},{7,5},{8,10},{9,11},{10,... | collective-permute-start | bytes 1769480 | tf_op jit(solution)/shard_map/ppermute | solution.py:245
  196.3 2.9 collective-permute-start.15
  223.1 183.0 %reduce-scatter.12.cloned.1.call-start = ((), (), s32[]{:S(2)}) async-start(), calls=%async_computation.4 | async-start | bytes 1658880
  223.3 46.6 %collective-permute-start.19 = (bf16[4,72,1024]{2,1,0:T(8,128)(2,1)S(1)}, bf16[4,72,1024]{2,1,0:T(8,128)(2,1)S(1)}, u32[]{:S(2)}, u32[]{:S(2)}) collective-permute-start(bf16[4,72,1024]{2,1,0:T(8,128)(2,1)S(1)} %bitcast.381), channel_id=1, source_target_pairs={{4,0},{8,4},{12,8},{16,12},{20,16},{24,20},{28,24},{5,1},{9,5},{13... | collective-permute-start | bytes 1769480 | tf_op jit(solution)/shard_map/ppermute | solution.py:250
  224.6 45.3 %collective-permute-start.18 = (bf16[4,72,1024]{2,1,0:T(8,128)(2,1)S(1)}, bf16[4,72,1024]{2,1,0:T(8,128)(2,1)S(1)}, u32[]{:S(2)}, u32[]{:S(2)}) collective-permute-start(bf16[4,72,1024]{2,1,0:T(8,128)(2,1)S(1)} %bitcast.382), channel_id=1, source_target_pairs={{0,4},{4,8},{8,12},{12,16},{16,20},{20,24},{24,28},{1,5},{5,9},{9,... | collective-permute-start | bytes 1769480 | tf_op jit(solution)/shard_map/ppermute | solution.py:250
  241.1 19.7 %collective-permute-start.21 = (f32[2,4,1,1024]{3,2,1,0:T(1,128)S(1)}, f32[2,4,1,1024]{3,2,1,0:T(1,128)S(1)}, u32[]{:S(2)}, u32[]{:S(2)}) collective-permute-start(f32[2,4,1,1024]{3,2,1,0:T(1,128)S(1)} %pad_maximum_fusion.12), channel_id=1, source_target_pairs={{4,0},{8,4},{12,8},{16,12},{20,16},{24,20},{28,24},{5,1},{9,5},{13... | collective-permute-start | bytes 98312 | tf_op jit(solution)/shard_map/ppermute | solution.py:250
  242.6 27.3 %copy-start.14 = (bf16[1,288,1024]{2,1,0:T(8,128)(2,1)S(1)}, bf16[1,288,1024]{2,1,0:T(8,128)(2,1)}, u32[]{:S(2)}) copy-start(bf16[1,288,1024]{2,1,0:T(8,128)(2,1)} %get-tuple-element.157) | copy-start | bytes 1769476
  242.6 27.3 %copy-start.15 = (bf16[1,288,1024]{2,1,0:T(8,128)(2,1)S(1)}, bf16[1,288,1024]{2,1,0:T(8,128)(2,1)}, u32[]{:S(2)}) copy-start(bf16[1,288,1024]{2,1,0:T(8,128)(2,1)} %get-tuple-element.154) | copy-start | bytes 1769476
  242.7 27.3 %copy-start.17 = (f32[4,72,1024]{2,1,0:T(8,128)S(1)}, f32[4,72,1024]{2,1,0:T(8,128)}, u32[]{:S(2)}) copy-start(f32[4,72,1024]{2,1,0:T(8,128)} %copy-done.16) | copy-start | bytes 3538948
  249.9 20.0 %collective-permute-start.20 = (f32[2,4,1,1024]{3,2,1,0:T(1,128)S(1)}, f32[2,4,1,1024]{3,2,1,0:T(1,128)S(1)}, u32[]{:S(2)}, u32[]{:S(2)}) collective-permute-start(f32[2,4,1,1024]{3,2,1,0:T(1,128)S(1)} %pad_maximum_fusion.12), channel_id=1, source_target_pairs={{0,4},{4,8},{8,12},{12,16},{16,20},{20,24},{24,28},{1,5},{5,9},{9,... | collective-permute-start | bytes 98312 | tf_op jit(solution)/shard_map/ppermute | solution.py:250
  277.1 219.1 %reduce-scatter.14.cloned.1.call-start = ((), (), s32[]{:S(2)}) async-start(), calls=%async_computation.5 | async-start | bytes 5971968
  289.7 13.6 %collective-permute-start.16 = (bf16[2,256,1152]{2,1,0:T(8,128)(2,1)}, bf16[2,256,1152]{2,1,0:T(8,128)(2,1)}, u32[]{:S(2)}, u32[]{:S(2)}) collective-permute-start(bf16[2,256,1152]{2,1,0:T(8,128)(2,1)} %dynamic-slice_bitcast_fusion.1), channel_id=1, source_target_pairs={{0,1},{1,0},{2,3},{3,2},{4,5},{5,4},{6,7},{7,6},{8,9},{9,8},{10,11... | collective-permute-start | bytes 3538952 | tf_op jit(solution)/shard_map/ppermute | solution.py:245
  305.5 15.8 %collective-permute-start.17 = (bf16[256,1152]{1,0:T(8,128)(2,1)S(1)}, bf16[256,1152]{1,0:T(8,128)(2,1)S(1)}, u32[]{:S(2)}, u32[]{:S(2)}) collective-permute-start(bf16[256,1152]{1,0:T(8,128)(2,1)S(1)} %fusion.71), channel_id=1, source_target_pairs={{0,2},{1,3},{2,0},{3,1},{4,6},{5,7},{6,4},{7,5},{8,10},{9,11},{10,... | collective-permute-start | bytes 1769480 | tf_op jit(solution)/shard_map/ppermute | solution.py:245
  344.5 17.5 %collective-permute-start.25 = (bf16[2,288,1024]{2,1,0:T(8,128)(2,1)S(1)}, bf16[2,288,1024]{2,1,0:T(8,128)(2,1)}, u32[]{:S(2)}, u32[]{:S(2)}) collective-permute-start(bf16[2,288,1024]{2,1,0:T(8,128)(2,1)S(1)} %dynamic-slice_bitcast_fusion), channel_id=1, source_target_pairs={{0,1},{1,0},{2,3},{3,2},{4,5},{5,4},{6,7},{7,6},{8,9},{9,8},{10,11... | collective-permute-start | bytes 3538952 | tf_op jit(solution)/shard_map/ppermute | solution.py:245
  344.7 6.1 %collective-permute-start.24 = (f32[17,1728]{1,0:T(8,128)S(1)}, f32[17,1728]{1,0:T(8,128)S(1)}, u32[]{:S(2)}, u32[]{:S(2)}) collective-permute-start(f32[17,1728]{1,0:T(8,128)S(1)} %get-tuple-element.179), channel_id=1, source_target_pairs={{0,3},{1,2},{2,1},{3,0},{4,7},{5,6},{6,5},{7,4},{8,11},{9,10},{10,... | collective-permute-start | bytes 352520 | tf_op jit(solution)/shard_map/ppermute | solution.py:245
  345.2 5.6 %collective-permute-start.22 = (f32[17,1728]{1,0:T(8,128)S(1)}, f32[17,1728]{1,0:T(8,128)S(1)}, u32[]{:S(2)}, u32[]{:S(2)}) collective-permute-start(f32[17,1728]{1,0:T(8,128)S(1)} %get-tuple-element.180), channel_id=1, source_target_pairs={{0,1},{1,0},{2,3},{3,2},{4,5},{5,4},{6,7},{7,6},{8,9},{9,8},{10,11... | collective-permute-start | bytes 352520 | tf_op jit(solution)/shard_map/ppermute | solution.py:245
  345.3 9.9 %collective-permute-start.23 = (f32[17,1728]{1,0:T(8,128)S(1)}, f32[17,1728]{1,0:T(8,128)}, u32[]{:S(2)}, u32[]{:S(2)}) collective-permute-start(f32[17,1728]{1,0:T(8,128)S(1)} %get-tuple-element.181), channel_id=1, source_target_pairs={{0,2},{1,3},{2,0},{3,1},{4,6},{5,7},{6,4},{7,5},{8,10},{9,11},{10,... | collective-permute-start | bytes 352520 | tf_op jit(solution)/shard_map/ppermute | solution.py:245
  356.2 30.3 %copy-start.57 = (bf16[16,1152]{1,0:T(8,128)(2,1)S(1)}, bf16[16,1152]{1,0:T(8,128)(2,1)}, u32[]{:S(2)}) copy-start(bf16[16,1152]{1,0:T(8,128)(2,1)} %param.15) | copy-start | bytes 110596
  356.2 9.8 %collective-permute-start.26 = (f32[20,1728]{1,0:T(8,128)S(1)}, f32[20,1728]{1,0:T(8,128)S(1)}, u32[]{:S(2)}, u32[]{:S(2)}) collective-permute-start(f32[20,1728]{1,0:T(8,128)S(1)} %pad_maximum_fusion.11), channel_id=1, source_target_pairs={{0,4},{4,0},{8,12},{12,8},{16,20},{20,16},{24,28},{28,24},{1,5},{5... | collective-permute-start | bytes 414728 | tf_op jit(solution)/shard_map/ppermute | solution.py:245
  366.1 15.8 %collective-permute-start.27 = (f32[20,1728]{1,0:T(8,128)S(1)}, f32[20,1728]{1,0:T(8,128)S(1)}, u32[]{:S(2)}, u32[]{:S(2)}) collective-permute-start(f32[20,1728]{1,0:T(8,128)S(1)} %fusion.167), channel_id=1, source_target_pairs={{0,8},{4,12},{8,0},{12,4},{16,24},{20,28},{24,16},{28,20},{1,9},{5... | collective-permute-start | bytes 414728 | tf_op jit(solution)/shard_map/ppermute | solution.py:245
  381.9 9.8 %collective-permute-start.28 = (f32[20,1728]{1,0:T(8,128)S(1)}, f32[20,1728]{1,0:T(8,128)}, u32[]{:S(2)}, u32[]{:S(2)}) collective-permute-start(f32[20,1728]{1,0:T(8,128)S(1)} %add.664), channel_id=1, source_target_pairs={{0,16},{4,20},{8,24},{12,28},{16,0},{20,4},{24,8},{28,12},{1,17},{... | collective-permute-start | bytes 414728 | tf_op jit(solution)/shard_map/ppermute | solution.py:245
  386.6 15.2 %collective-permute-start.29 = (bf16[288,1024]{1,0:T(8,128)(2,1)S(1)}, bf16[288,1024]{1,0:T(8,128)(2,1)}, u32[]{:S(2)}, u32[]{:S(2)}) collective-permute-start(bf16[288,1024]{1,0:T(8,128)(2,1)S(1)} %fusion.72), channel_id=1, source_target_pairs={{0,2},{1,3},{2,0},{3,1},{4,6},{5,7},{6,4},{7,5},{8,10},{9,11},{10,... | collective-permute-start | bytes 1769480 | tf_op jit(solution)/shard_map/ppermute | solution.py:245
  396.8 3.9 collective-permute-start.30
  396.8 3.9 collective-permute-start.31
  398.2 3.0 collective-permute-start.32
  (75 other events, 295.4 us)
Sparse Core Ops, SparseCore 0:
  223.2 94.7 reduce-scatter.9
  321.5 65.6 reduce-scatter.11
  390.8 105.3 reduce-scatter.13
where the time goes:
time: 523 us; the launch traced here: 513 us
  waiting for transfers between devices  205 us (39%)
  starting transfers between devices  70.1 us (13%)
  matrix products  68.9 us (13%)
  other arithmetic  62.5 us (12%)
  local copies, waits for them, and re-layouts  60.6 us (12%)
  Pallas kernels  30.2 us (6%)
  between operations  15.9 us (3%)
    ppermute x27, waiting for transfers between devices, swap(): lax.ppermute(value, axis, [(i, i ^ bit) for i in range(lax.axis_size(axis...  106 us
    unnamed x6, waiting for transfers between devices  87.7 us
    unnamed x195, local copies, waits for them, and re-layouts  38.1 us
    ppermute x6, starting transfers between devices, shift(): lax.ppermute(value, axis, [(i, i + distance) for i in devices if i + dist...  37.1 us
    ppermute x27, starting transfers between devices, swap(): lax.ppermute(value, axis, [(i, i ^ bit) for i in range(lax.axis_size(axis...  33 us
    pallas_call x1, Pallas kernels, attend_back(): pl.pallas_call(functools.partial(backward_kernel, bases, heads), out_shap...  14.3 us
    pallas_call x2, Pallas kernels, attend(): pl.pallas_call(functools.partial(forward_kernel, bases, heads, last), out...  12.5 us
    ppermute x6, waiting for transfers between devices, shift(): lax.ppermute(value, axis, [(i, i + distance) for i in devices if i + dist...  10.7 us
  transfers between devices with their start and end apart: 36, of which 20 were waited for; matrix products, arithmetic and copies ran while one was open for 22% of the time, Pallas kernels for 2%

commit v1 on v0

--- a/solution.py
+++ b/solution.py
@@ -14,6 +14,7 @@
 NEG = -1e30
 BQ = 256
 BK = 256
+COST = pl.CostEstimate(flops=18 << 30, bytes_accessed=24 << 20, transcendentals=1 << 22)
 F32 = jnp.float32
 BF16 = jnp.bfloat16
 
@@ -96,7 +97,7 @@
         out_specs=(vmem,) * 3,
         scratch_shapes=[pltpu.VMEM((heads, hd, BQ), F32)],
         compiler_params=pltpu.CompilerParams(vmem_limit_bytes=40 << 20),
-        cost_estimate=pl.CostEstimate(flops=1 << 20, bytes_accessed=1 << 20, transcendentals=0),
+        cost_estimate=COST,
     )(bounds, span, query, *carried, *keys, *values)
 
 
@@ -178,7 +179,7 @@
             pltpu.VMEM((heads, hd, BK), F32),
         ],
         compiler_params=pltpu.CompilerParams(vmem_limit_bytes=44 << 20),
-        cost_estimate=pl.CostEstimate(flops=1 << 20, bytes_accessed=1 << 20, transcendentals=0),
+        cost_estimate=COST,
     )(bounds, span, query, grad, logsum, delta, *keys, *values)
 
 
@@ -237,7 +238,7 @@
         out_specs=(vmem, vmem),
         scratch_shapes=[pltpu.VMEM((heads, hd, BK), F32), pltpu.VMEM((heads, hd, BK), F32)],
         compiler_params=pltpu.CompilerParams(vmem_limit_bytes=40 << 20),
-        cost_estimate=pl.CostEstimate(flops=1 << 20, bytes_accessed=1 << 20, transcendentals=0),
+        cost_estimate=COST,
     )(bounds, keys, values, keys_in, values_in, *spans, *query, *grad, *logsum, *delta)
 
 
@@ -279,7 +280,7 @@
 def gather_tensor(value):
     pair = in_order(value, swap(value, "tensor", 2), bit_set("tensor", 2))
     quad = in_order(pair, swap(pair, "tensor", 1), bit_set("tensor", 1), dim=1)
-    return quad.reshape((4 * value.shape[0],) + value.shape[1:])
+    return lax.optimization_barrier(quad.reshape((4 * value.shape[0],) + value.shape[1:]))
 
 
 def scatter_tensor(partial):
@@ -300,14 +301,34 @@
     return stay + come.astype(F32)
 
 
+def scatter_data_steps(partial):
+    size = lax.axis_size("dp")
+    index = lax.axis_index("dp")
+    bits = bits_of("dp")
+    count = len(bits)
+    rest = (partial.shape[0] // size,) + partial.shape[1:]
+    held = partial.astype(BF16).reshape((2,) * count + rest)
+    left = list(reversed(bits))
+    for bit in [1] + bits[:0:-1]:
+        axis = left.index(bit)
+        mine = (index // bit) % 2
+        kept = lax.dynamic_index_in_dim(held, mine, axis, keepdims=False)
+        sent = lax.dynamic_index_in_dim(held, 1 - mine, axis, keepdims=False).astype(BF16)
+        come = swap(sent, "dp", bit)
+        come = after((yield sent), come)
+        held = kept.astype(F32) + come.astype(F32)
+        left.remove(bit)
+    return held
+
+
 def scatter_data(partials):
     joined = jnp.concatenate([partial.astype(BF16) for partial in partials], axis=1)
-    found = lax.psum_scatter(joined, "dp", scatter_dimension=0, tiled=True).astype(F32)
+    found = lax.psum_scatter(joined, "dp", scatter_dimension=0, tiled=True)
     cuts, at = [], 0
     for partial in partials[:-1]:
         at += partial.shape[1]
         cuts.append(at)
-    return jnp.split(found, cuts, axis=1)
+    return joined, lambda anchor: jnp.split(after(anchor, found).astype(F32), cuts, axis=1)
 
 
 def finish(steps, anchor=None):
@@ -494,8 +515,8 @@
     grad_pre = after(next(entry_steps), grad_pre)
     grad_out_mine = mine(out_grad).astype(F32)
     grad_up_w = jnp.einsum("td,tf->df", entry_m, grad_pre, preferred_element_type=F32)
-    sum_down_w, sum_up_w = scatter_data([grad_down_w, grad_up_w])
-    grad_entry_m = finish(entry_steps)
+    wide_sent, wide_sums = scatter_data([grad_down_w, grad_up_w])
+    grad_entry_m = finish(entry_steps, wide_sent)
     grad_down_b = jnp.sum(grad_branch_m.astype(F32), axis=0)
     grad_up_b = jnp.sum(grad_pre.astype(F32), axis=0)
     grad_middle = grad_out_mine + norm_back_m(grad_entry_m * (1.0 + scale_m))[0]
@@ -556,9 +577,12 @@
         lax.dot_general(entry, x, (((0,), (1,)), ((), ())), preferred_element_type=F32)
         for x in grad_proj
     )
-    sum_out_w, sum_q_w = scatter_data([grad_out_w, grad_q_w])
-    sum_k_w, sum_v_w = scatter_data([grad_k_w, grad_v_w])
-    grad_proj = after((grad_k_w, grad_v_w), *grad_proj)
+    early_steps = scatter_data_steps(jnp.concatenate([grad_out_w, grad_q_w], axis=1))
+    next(early_steps)
+    early_sent = early_steps.send(grad_keys)
+    late_steps = scatter_data_steps(jnp.concatenate([grad_k_w, grad_v_w], axis=1))
+    late_sent = next(late_steps)
+    grad_proj = after((late_sent, early_sent), *grad_proj)
     grad_in_b = jnp.stack([jnp.sum(grad_proj[c].astype(F32), axis=1) for c in (0, 2)])
     grad_entry = lax.dot_general(
         in_weight.reshape(width, 3 * local_width),
@@ -613,7 +637,8 @@
             for value in (grad_in_b.reshape(-1), grad_up_b, grad_down_b)
         ]
     )
-    tokens_sent = tokens_steps.send(small)
+    late_sent = late_steps.send(tokens_sent)
+    tokens_sent = tokens_steps.send(late_sent)
     for place, bit in enumerate(bits_of("dp")):
         come = swap(small, "dp", bit)
         if place == 0:
@@ -643,7 +668,13 @@
         )
 
     grad_tokens = finish(tokens_steps, grad_mod_w).T
-    sum_in_w = jnp.stack([sum_q_w, sum_k_w, sum_v_w], axis=1)
+    sum_down_w, sum_up_w = wide_sums(grad_mod_w)
+    early = finish(early_steps, tokens_sent)
+    late = finish(late_steps, small)
+    sum_out_w = early[:, :local_width]
+    sum_in_w = jnp.stack(
+        [early[:, local_width:], late[:, :local_width], late[:, local_width:]], axis=1
+    )
     return (
         output,
         grad_tokens,

time: 523 us -> 423 us (0.81); the launches traced: 513 us -> 418 us
  waiting for transfers between devices: 205 us -> 98.1 us
  Pallas kernels: 30.2 us -> 38.4 us
  starting transfers between devices: 70.1 us -> 63.5 us
    unnamed x6 -> x2, waiting for transfers between devices: 87.7 us -> 0.02 us
    ppermute x27 -> x33, waiting for transfers between devices: 106 us -> 92.8 us  [swap(): lax.ppermute(value, axis, [(i, i ^ bit) for i in range(lax.axis_size(axis...]
    ppermute x6, starting transfers between devices: 37.1 us -> 24.8 us  [shift(): lax.ppermute(value, axis, [(i, i + distance) for i in devices if i + dist...]
    unnamed x195 -> x224, local copies, waits for them, and re-layouts: 38.1 us -> 27.2 us
    dot_general x0 -> x2, local copies, waits for them, and re-layouts: none -> 6.97 us  [the longest x1 4.46 us: on_device(): lax.dot_general(grad_branch, attended_flat, (((0,), (1,)), ((), ())), pre...]
    select_n x13 -> x15, other arithmetic: 5.1 us -> 11.9 us  [in_order(): jnp.where(upper, jnp.stack([other, mine], axis=dim), jnp.stack([mine, oth...]
    ppermute x27 -> x33, starting transfers between devices: 33 us -> 38.7 us  [swap(): lax.ppermute(value, axis, [(i, i ^ bit) for i in range(lax.axis_size(axis...]
    ppermute x6, waiting for transfers between devices: 10.7 us -> 5.33 us  [shift(): lax.ppermute(value, axis, [(i, i + distance) for i in devices if i + dist...]
  transfers between devices with their start and end apart: 36 -> 40, of which waited for: 20 -> 17; matrix products, arithmetic and copies ran while one was open for 22% -> 33% of each run, Pallas kernels for 2% -> 8%
where the time goes in v1:
time: 423 us; the launch traced here: 418 us
  waiting for transfers between devices  98.1 us (23%)
  matrix products  74 us (17%)
  other arithmetic  64.9 us (15%)
  starting transfers between devices  63.5 us (15%)
  local copies, waits for them, and re-layouts  63.1 us (15%)
  Pallas kernels  38.4 us (9%)
  between operations  16.3 us (4%)
    ppermute x33, waiting for transfers between devices, swap(): lax.ppermute(value, axis, [(i, i ^ bit) for i in range(lax.axis_size(axis...  92.8 us
    ppermute x33, starting transfers between devices, swap(): lax.ppermute(value, axis, [(i, i ^ bit) for i in range(lax.axis_size(axis...  38.7 us
    unnamed x224, local copies, waits for them, and re-layouts  27.2 us
    ppermute x6, starting transfers between devices, shift(): lax.ppermute(value, axis, [(i, i + distance) for i in devices if i + dist...  24.8 us
    pallas_call x1, Pallas kernels, attend_back(): pl.pallas_call(functools.partial(backward_kernel, bases, heads), out_shap...  16.8 us
    pallas_call x2, Pallas kernels, attend(): pl.pallas_call(functools.partial(forward_kernel, bases, heads, last), out...  14.6 us
    select_n x15, other arithmetic, in_order(): jnp.where(upper, jnp.stack([other, mine], axis=dim), jnp.stack([mine, oth...  11.9 us
    dot_general x3, matrix products, project(): jnp.einsum('dcf,td->cft', in_weight, entry, preferred_element_type=F32)  9.85 us
  transfers between devices with their start and end apart: 40, of which 17 were waited for; matrix products, arithmetic and copies ran while one was open for 33% of the time, Pallas kernels for 8%

profile of v1, /device:TPU:0, one launch (start us, length us, event | category | flops | bytes accessed | tf_op | source)
XLA Modules:
  0.0 418.4 jit_solution(5325014060435882531)
XLA Ops:
  9.3 5.7 %collective-permute-start.2 = (bf16[256,1152]{1,0:T(8,128)(2,1)}, bf16[256,1152]{1,0:T(8,128)(2,1)}, u32[]{:S(2)}, u32[]{:S(2)}) collective-permute-start(bf16[256,1152]{1,0:T(8,128)(2,1)} %constant_dynamic-slice_fusion.12), channel_id=1, source_target_pairs={{0,4},{4,8},{8,12},{12,16},{16,20},{20,24},{24,28},{1,5},{5,9},{9,... | collective-permute-start | bytes 1769480 | tf_op jit(solution)/shard_map/ppermute | solution.py:251
  17.0 3.3 fusion.60
  31.7 2.5 fusion.61
  34.4 5.3 %collective-permute-done.2 = bf16[256,1152]{1,0:T(8,128)(2,1)} collective-permute-done((bf16[256,1152]{1,0:T(8,128)(2,1)}, bf16[256,1152]{1,0:T(8,128)(2,1)}, u32[]{:S(2)}, u32[]{:S(2)}) %collective-permute-start.2) | collective-permute-done | bytes 589856 | tf_op jit(solution)/shard_map/ppermute | solution.py:251
  41.4 9.1 %shard_map.237 = (f32[4,72,1024]{2,1,0:T(8,128)S(1)}, f32[4,1,1024]{2,1,0:T(1,128)S(1)}, f32[4,1,1024]{2,1,0:T(1,128)S(1)}) custom-call(s32[1,2,4]{2,1,0:T(2,128)S(1)} %add_bitcast_fusion.2.bounds, s32[2,1024]{1,0:T(2,128)S(1)} %pad_add_fusion.span, bf16[4,72,1024]{2,1,0:T(8,128)(2,1)S(1)} %bitcast.384, f32[4,72,1024]{2,1,0:T(8,128)S(1)} %broadcast_in_dim.212.mixed_in, ...), custom_call_target="tpu_custom_call" | custom-call | flops 19327352832 | bytes 25165824 | tf_op jit(solution)/shard_map/pallas_call | solution.py:89
  51.1 5.1 %collective-permute-done.3 = bf16[256,1152]{1,0:T(8,128)(2,1)S(1)} collective-permute-done((bf16[256,1152]{1,0:T(8,128)(2,1)}, bf16[256,1152]{1,0:T(8,128)(2,1)S(1)}, u32[]{:S(2)}, u32[]{:S(2)}) %collective-permute-start.3) | collective-permute-done | bytes 589856 | tf_op jit(solution)/shard_map/ppermute | solution.py:246
  60.8 6.0 %collective-permute-done.6 = bf16[256,1152]{1,0:T(8,128)(2,1)S(1)} collective-permute-done((bf16[256,1152]{1,0:T(8,128)(2,1)}, bf16[256,1152]{1,0:T(8,128)(2,1)S(1)}, u32[]{:S(2)}, u32[]{:S(2)}) %collective-permute-start.6) | collective-permute-done | bytes 589856 | tf_op jit(solution)/shard_map/ppermute | solution.py:246
  74.5 3.4 fusion.62
  78.8 4.0 fusion.63
  83.8 5.6 %shard_map.238 = (bf16[4,72,1024]{2,1,0:T(8,128)(2,1)S(1)}, f32[4,1,1024]{2,1,0:T(1,128)S(1)}, f32[4,1,1024]{2,1,0:T(1,128)}) custom-call(s32[2,2,4]{2,1,0:T(2,128)S(1)} %pad_add_fusion.4.bounds, s32[2,1024]{1,0:T(2,128)S(1)} %pad_add_fusion.span, bf16[4,72,1024]{2,1,0:T(8,128)(2,1)S(1)} %bitcast.385, f32[4,72,1024]{2,1,0:T(8,128)S(1)} %get-tuple-element.45.mixed_in, ...), custom_call_target="tpu_custom_call" | custom-call | flops 19327352832 | bytes 25165824 | tf_op jit(solution)/shard_map/pallas_call | solution.py:89
  103.9 12.9 %collective-permute-done.9 = bf16[256,1152]{1,0:T(8,128)(2,1)} collective-permute-done((bf16[256,1152]{1,0:T(8,128)(2,1)}, bf16[256,1152]{1,0:T(8,128)(2,1)}, u32[]{:S(2)}, u32[]{:S(2)}) %collective-permute-start.9) | collective-permute-done | bytes 589856 | tf_op jit(solution)/shard_map/ppermute | solution.py:246
  122.3 11.9 %collective-permute-done.10 = bf16[256,1152]{1,0:T(8,128)(2,1)S(1)} collective-permute-done((bf16[256,1152]{1,0:T(8,128)(2,1)S(1)}, bf16[256,1152]{1,0:T(8,128)(2,1)S(1)}, u32[]{:S(2)}, u32[]{:S(2)}) %collective-permute-start.10) | collective-permute-done | bytes 589856 | tf_op jit(solution)/shard_map/ppermute | solution.py:246
  136.2 3.5 fusion.166
  140.3 5.8 %multiply_convert_fusion = (bf16[1024,1152]{1,0:T(8,128)(2,1)S(1)}, bf16[1024,1152]{1,0:T(8,128)(2,1)S(1)}) fusion(f32[1024,1152]{1,0:T(8,128)S(1)} %fusion.166, f32[1152]{0:T(1024)S(1)} %convert_element_type.348, bf16[1024,1152]{1,0:T(8,128)(2,1)S(1)} %bitcast.438, bf16[1152,1152]{1,0:T(8,128)(2,1)S(1)} %copy-done), kind=kOutput, calls=%fused_computation.54 | convolution fusion | flops 2745040896 | bytes 14455296 | tf_op jit(solution)/shard_map/dot_general | solution.py:505
  146.2 3.8 convolution_convert_fusion.5
  150.2 3.4 convolution_convert_fusion.1
  153.6 3.4 convolution_convert_fusion
  157.0 2.8 pad_maximum_fusion.1
  163.9 13.5 %collective-permute-done.13 = bf16[256,1152]{1,0:T(8,128)(2,1)} collective-permute-done((bf16[256,1152]{1,0:T(8,128)(2,1)S(1)}, bf16[256,1152]{1,0:T(8,128)(2,1)}, u32[]{:S(2)}, u32[]{:S(2)}) %collective-permute-start.13) | collective-permute-done | bytes 589856 | tf_op jit(solution)/shard_map/ppermute | solution.py:246
  177.4 2.8 multiply_multiply_fusion.2
  184.3 3.6 convert_reduce_fusion.7
  190.1 2.5 copy.99
  192.6 8.7 %copy.116 = bf16[1152,2304]{1,0:T(8,128)(2,1)} copy(bf16[1152,2304]{0,1:T(8,128)(2,1)} %pad_maximum_fusion.1) | data formatting | bytes 10616832
  205.1 5.7 %convolution_convert_fusion.4 = bf16[1024,1152]{1,0:T(8,128)(2,1)S(1)} fusion(bf16[1024,1152]{1,0:T(8,128)(2,1)S(1)} %copy-done.104, bf16[1152,1152]{1,0:T(8,128)(2,1)} %param.23), kind=kOutput, calls=%fused_computation.60 | convolution fusion | flops 2719088640 | bytes 7372800 | tf_op jit(solution)/shard_map/tf,df->td/dot_general | solution.py:531
  219.5 9.0 %collective-permute-start.20 = (f32[2,4,1,1024]{3,2,1,0:T(1,128)S(1)}, f32[2,4,1,1024]{3,2,1,0:T(1,128)S(1)}, u32[]{:S(2)}, u32[]{:S(2)}) collective-permute-start(f32[2,4,1,1024]{3,2,1,0:T(1,128)S(1)} %pad_maximum_fusion.10), channel_id=1, source_target_pairs={{0,4},{4,8},{8,12},{12,16},{16,20},{20,24},{24,28},{1,5},{5,9},{9,... | collective-permute-start | bytes 98312 | tf_op jit(solution)/shard_map/ppermute | solution.py:251
  229.8 6.3 %collective-permute-start.18 = (bf16[4,72,1024]{2,1,0:T(8,128)(2,1)}, bf16[4,72,1024]{2,1,0:T(8,128)(2,1)}, u32[]{:S(2)}, u32[]{:S(2)}) collective-permute-start(bf16[4,72,1024]{2,1,0:T(8,128)(2,1)} %bitcast.71.grad), channel_id=1, source_target_pairs={{0,4},{4,8},{8,12},{12,16},{16,20},{20,24},{24,28},{1,5},{5,9},{9,... | collective-permute-start | bytes 1769480 | tf_op jit(solution)/shard_map/ppermute | solution.py:251
  238.9 4.5 %copy.100 = bf16[1152,1024]{1,0:T(8,128)(2,1)} copy(bf16[1152,1024]{0,1:T(8,128)(2,1)} %bitcast.419) | data formatting | bytes 4718592 | tf_op jit(solution)/shard_map/dot_general | solution.py:560
  245.5 16.8 %shard_map.239 = (bf16[4,72,1024]{2,1,0:T(8,128)(2,1)S(1)}, f32[4,72,1024]{2,1,0:T(8,128)S(1)}, f32[4,72,1024]{2,1,0:T(8,128)S(1)}) custom-call(s32[3,2,4]{2,1,0:T(2,128)S(1)} %pad_add_fusion.3.bounds, s32[2,1024]{1,0:T(2,128)S(1)} %pad_add_fusion.span, bf16[4,72,1024]{2,1,0:T(8,128)(2,1)S(1)} %bitcast.386, bf16[4,72,1024]{2,1,0:T(8,128)(2,1)} %bitcast.71.grad, ...), custom_call_target="tpu_custom_call" | custom-call | flops 19327352832 | bytes 25165824 | tf_op jit(solution)/shard_map/pallas_call | solution.py:171
  266.0 6.2 %collective-permute-start.22 = (bf16[2,2,144,576]{3,2,1,0:T(8,128)(2,1)S(1)}, bf16[2,2,144,576]{3,2,1,0:T(8,128)(2,1)S(1)}, u32[]{:S(2)}, u32[]{:S(2)}) collective-permute-start(bf16[2,2,144,576]{3,2,1,0:T(8,128)(2,1)S(1)} %fusion.93), channel_id=1, source_target_pairs={{0,4},{4,0},{8,12},{12,8},{16,20},{20,16},{24,28},{28,24},{1,5},{5... | collective-permute-start | bytes 1990664 | tf_op jit(solution)/shard_map/ppermute | solution.py:246
  272.3 7.0 %shard_map.240 = (bf16[4,72,1024]{2,1,0:T(8,128)(2,1)S(1)}, bf16[4,72,1024]{2,1,0:T(8,128)(2,1)S(1)}) custom-call(s32[2,2,4]{2,1,0:T(2,128)S(1)} %pad_add_fusion.4.bounds, bf16[4,72,1024]{2,1,0:T(8,128)(2,1)S(1)} %bitcast.383, bf16[4,72,1024]{2,1,0:T(8,128)(2,1)S(1)} %bitcast.380, f32[4,72,1024]{2,1,0:T(8,128)S(1)} %get-tuple-element.57.keys_in, ...), custom_call_target="tpu_custom_call" | custom-call | flops 19327352832 | bytes 25165824 | tf_op jit(solution)/shard_map/pallas_call | solution.py:234
  283.3 5.8 %collective-permute-start.23 = (bf16[2,2,144,576]{3,2,1,0:T(8,128)(2,1)}, bf16[2,2,144,576]{3,2,1,0:T(8,128)(2,1)}, u32[]{:S(2)}, u32[]{:S(2)}) collective-permute-start(bf16[2,2,144,576]{3,2,1,0:T(8,128)(2,1)} %fusion.99), channel_id=1, source_target_pairs={{0,4},{4,0},{8,12},{12,8},{16,20},{20,16},{24,28},{28,24},{1,5},{5... | collective-permute-start | bytes 1990664 | tf_op jit(solution)/shard_map/ppermute | solution.py:246
  289.1 2.6 convert_multiply_fusion
  293.3 4.6 %collective-permute-done.22 = bf16[2,2,144,576]{3,2,1,0:T(8,128)(2,1)S(1)} collective-permute-done((bf16[2,2,144,576]{3,2,1,0:T(8,128)(2,1)S(1)}, bf16[2,2,144,576]{3,2,1,0:T(8,128)(2,1)S(1)}, u32[]{:S(2)}, u32[]{:S(2)}) %collective-permute-start.22) | collective-permute-done | bytes 663584 | tf_op jit(solution)/shard_map/ppermute | solution.py:246
  299.5 2.9 convolution_bitcast_fusion
  304.3 3.0 fusion.11
  309.3 3.1 copy.104
  312.4 5.1 %fusion.7 = f32[16,2304]{1,0:T(8,128)S(1)} fusion(f32[1152,1024]{0,1:T(8,128)} %get-tuple-element.183, f32[1152,1024]{0,1:T(8,128)} %copy-done.21, s32[1024]{0:T(1024)S(1)} %iota_add_fusion, s32[16]{0:T(128)S(1)} %copy-done.71, s32[16]{0:T(128)S(1)} %select_reduce_fusion.6), kind=kOutput, calls=%fused_computation.21 | convolution fusion | flops 84983808 | bytes 9588864 | tf_op jit(solution)/shard_map/tl,mt->lm/dot_general | solution.py:355
  317.8 3.2 fusion.36
  324.0 2.9 constant_dynamic-slice_fusion.9
  334.7 3.1 collective-permute-start.35
  347.4 7.0 %collective-permute-done.35 = bf16[2,144,576]{2,1,0:T(8,128)(2,1)S(1)} collective-permute-done((bf16[2,144,576]{2,1,0:T(8,128)(2,1)}, bf16[2,144,576]{2,1,0:T(8,128)(2,1)S(1)}, u32[]{:S(2)}, u32[]{:S(2)}) %collective-permute-start.35) | collective-permute-done | bytes 331808 | tf_op jit(solution)/shard_map/ppermute | solution.py:246
  358.7 7.3 %collective-permute-done.29 = f32[20,1728]{1,0:T(8,128)S(1)} collective-permute-done((f32[20,1728]{1,0:T(8,128)S(1)}, f32[20,1728]{1,0:T(8,128)S(1)}, u32[]{:S(2)}, u32[]{:S(2)}) %collective-permute-start.29) | collective-permute-done | bytes 138272 | tf_op jit(solution)/shard_map/ppermute | solution.py:246
  369.6 14.0 %collective-permute-done.30 = f32[20,1728]{1,0:T(8,128)S(1)} collective-permute-done((f32[20,1728]{1,0:T(8,128)S(1)}, f32[20,1728]{1,0:T(8,128)S(1)}, u32[]{:S(2)}, u32[]{:S(2)}) %collective-permute-start.30) | collective-permute-done | bytes 138272 | tf_op jit(solution)/shard_map/ppermute | solution.py:246
  385.7 3.4 fusion.127
  395.3 3.6 collective-permute-done.38
  403.4 3.0 fusion.163
  406.4 2.4 copy.106
  408.9 2.4 copy.105
  (458 shorter events, 138.7 us)
Async XLA Ops:
  7.2 133.2 %copy-start = (bf16[1152,1152]{1,0:T(8,128)(2,1)S(1)}, bf16[1152,1152]{1,0:T(8,128)(2,1)}, u32[]{:S(2)}) copy-start(bf16[1152,1152]{1,0:T(8,128)(2,1)} %param.21) | copy-start | bytes 7962628
  7.2 393.9 %reduce-scatter.4.cloned.1.call-start = ((), (), s32[]{:S(2)}) async-start(), calls=%async_computation.1 | async-start | bytes 5971968
  9.3 30.4 %collective-permute-start.2 = (bf16[256,1152]{1,0:T(8,128)(2,1)}, bf16[256,1152]{1,0:T(8,128)(2,1)}, u32[]{:S(2)}, u32[]{:S(2)}) collective-permute-start(bf16[256,1152]{1,0:T(8,128)(2,1)} %constant_dynamic-slice_fusion.12), channel_id=1, source_target_pairs={{0,4},{4,8},{8,12},{12,16},{16,20},{20,24},{24,28},{1,5},{5,9},{9,... | collective-permute-start | bytes 1769480 | tf_op jit(solution)/shard_map/ppermute | solution.py:251
  15.0 35.4 %collective-permute-start.5 = (bf16[256,1152]{1,0:T(8,128)(2,1)}, bf16[256,1152]{1,0:T(8,128)(2,1)}, u32[]{:S(2)}, u32[]{:S(2)}) collective-permute-start(bf16[256,1152]{1,0:T(8,128)(2,1)} %constant_dynamic-slice_fusion.12), channel_id=1, source_target_pairs={{4,0},{8,4},{12,8},{16,12},{20,16},{24,20},{28,24},{5,1},{9,5},{13... | collective-permute-start | bytes 1769480 | tf_op jit(solution)/shard_map/ppermute | solution.py:251
  20.3 6.0 %collective-permute-start = (bf16[1,16,1728]{2,1,0:T(8,128)(2,1)S(1)}, bf16[1,16,1728]{2,1,0:T(8,128)(2,1)S(1)}, u32[]{:S(2)}, u32[]{:S(2)}) collective-permute-start(bf16[1,16,1728]{2,1,0:T(8,128)(2,1)S(1)} %bitcast.447), channel_id=1, source_target_pairs={{0,2},{1,3},{2,0},{3,1},{4,6},{5,7},{6,4},{7,5},{8,10},{9,11},{10,... | collective-permute-start | bytes 165896 | tf_op jit(solution)/shard_map/ppermute | solution.py:246
  24.2 278.2 %copy-start.70 = (s32[16]{0:T(128)}, s32[16]{0:T(128)S(1)}, u32[]{:S(2)}) copy-start(s32[16]{0:T(128)S(1)} %get-tuple-element.177) | copy-start | bytes 196
  26.3 1.4 collective-permute-start.1
  34.4 49.4 %copy-start.4 = (bf16[1,288,1024]{2,1,0:T(8,128)(2,1)}, bf16[1,288,1024]{2,1,0:T(8,128)(2,1)S(1)}, u32[]{:S(2)}) copy-start(bf16[1,288,1024]{2,1,0:T(8,128)(2,1)S(1)} %get-tuple-element.193) | copy-start | bytes 1769476
  39.7 16.5 %collective-permute-start.3 = (bf16[256,1152]{1,0:T(8,128)(2,1)}, bf16[256,1152]{1,0:T(8,128)(2,1)S(1)}, u32[]{:S(2)}, u32[]{:S(2)}) collective-permute-start(bf16[256,1152]{1,0:T(8,128)(2,1)} %collective-permute-done.2), channel_id=1, source_target_pairs={{0,2},{1,3},{2,0},{3,1},{4,6},{5,7},{6,4},{7,5},{8,10},{9,11},{10,... | collective-permute-start | bytes 1769480 | tf_op jit(solution)/shard_map/ppermute | solution.py:246
  50.5 16.3 %collective-permute-start.6 = (bf16[256,1152]{1,0:T(8,128)(2,1)}, bf16[256,1152]{1,0:T(8,128)(2,1)S(1)}, u32[]{:S(2)}, u32[]{:S(2)}) collective-permute-start(bf16[256,1152]{1,0:T(8,128)(2,1)} %collective-permute-done.5), channel_id=1, source_target_pairs={{0,2},{1,3},{2,0},{3,1},{4,6},{5,7},{6,4},{7,5},{8,10},{9,11},{10,... | collective-permute-start | bytes 1769480 | tf_op jit(solution)/shard_map/ppermute | solution.py:246
  57.7 13.6 %collective-permute-start.4 = (bf16[2,256,1152]{2,1,0:T(8,128)(2,1)S(1)}, bf16[2,256,1152]{2,1,0:T(8,128)(2,1)S(1)}, u32[]{:S(2)}, u32[]{:S(2)}) collective-permute-start(bf16[2,256,1152]{2,1,0:T(8,128)(2,1)S(1)} %maximum_select_fusion.4), channel_id=1, source_target_pairs={{0,1},{1,0},{2,3},{3,2},{4,5},{5,4},{6,7},{7,6},{8,9},{9,8},{10,11... | collective-permute-start | bytes 3538952 | tf_op jit(solution)/shard_map/ppermute | solution.py:246
  68.2 4.6 %collective-permute-start.7 = (bf16[2,256,1152]{2,1,0:T(8,128)(2,1)S(1)}, bf16[2,256,1152]{2,1,0:T(8,128)(2,1)S(1)}, u32[]{:S(2)}, u32[]{:S(2)}) collective-permute-start(bf16[2,256,1152]{2,1,0:T(8,128)(2,1)S(1)} %maximum_select_fusion.6), channel_id=1, source_target_pairs={{0,1},{1,0},{2,3},{3,2},{4,5},{5,4},{6,7},{7,6},{8,9},{9,8},{10,11... | collective-permute-start | bytes 3538952 | tf_op jit(solution)/shard_map/ppermute | solution.py:246
  93.4 3.3 collective-permute-start.8
  100.9 15.9 %collective-permute-start.9 = (bf16[256,1152]{1,0:T(8,128)(2,1)}, bf16[256,1152]{1,0:T(8,128)(2,1)}, u32[]{:S(2)}, u32[]{:S(2)}) collective-permute-start(bf16[256,1152]{1,0:T(8,128)(2,1)} %fusion.101), channel_id=1, source_target_pairs={{0,2},{1,3},{2,0},{3,1},{4,6},{5,7},{6,4},{7,5},{8,10},{9,11},{10,... | collective-permute-start | bytes 1769480 | tf_op jit(solution)/shard_map/ppermute | solution.py:246
  103.9 31.6 %copy-start.28 = (f32[256,4608]{1,0:T(8,128)}, f32[256,4608]{1,0:T(8,128)S(1)}, u32[]{:S(2)}) copy-start(f32[256,4608]{1,0:T(8,128)S(1)} %convolution_convert_fusion.2) | copy-start | bytes 14155780
  119.5 14.8 %collective-permute-start.10 = (bf16[256,1152]{1,0:T(8,128)(2,1)S(1)}, bf16[256,1152]{1,0:T(8,128)(2,1)S(1)}, u32[]{:S(2)}, u32[]{:S(2)}) collective-permute-start(bf16[256,1152]{1,0:T(8,128)(2,1)S(1)} %fusion.84), channel_id=1, source_target_pairs={{0,2},{1,3},{2,0},{3,1},{4,6},{5,7},{6,4},{7,5},{8,10},{9,11},{10,... | collective-permute-start | bytes 1769480 | tf_op jit(solution)/shard_map/ppermute | solution.py:246
  134.5 5.5 %collective-permute-start.11 = (bf16[2,256,1152]{2,1,0:T(8,128)(2,1)S(1)}, bf16[2,256,1152]{2,1,0:T(8,128)(2,1)S(1)}, u32[]{:S(2)}, u32[]{:S(2)}) collective-permute-start(bf16[2,256,1152]{2,1,0:T(8,128)(2,1)S(1)} %maximum_select_fusion.8), channel_id=1, source_target_pairs={{0,1},{1,0},{2,3},{3,2},{4,5},{5,4},{6,7},{7,6},{8,9},{9,8},{10,11... | collective-permute-start | bytes 3538952 | tf_op jit(solution)/shard_map/ppermute | solution.py:246
  150.2 9.7 %collective-permute-start.12 = (bf16[2,256,1152]{2,1,0:T(8,128)(2,1)S(1)}, bf16[2,256,1152]{2,1,0:T(8,128)(2,1)S(1)}, u32[]{:S(2)}, u32[]{:S(2)}) collective-permute-start(bf16[2,256,1152]{2,1,0:T(8,128)(2,1)S(1)} %dynamic-slice_bitcast_fusion.2), channel_id=1, source_target_pairs={{0,1},{1,0},{2,3},{3,2},{4,5},{5,4},{6,7},{7,6},{8,9},{9,8},{10,11... | collective-permute-start | bytes 3538952 | tf_op jit(solution)/shard_map/ppermute | solution.py:246
  159.8 17.6 %copy-start.26 = (f32[256,1152]{1,0:T(8,128)S(1)}, f32[256,1152]{1,0:T(8,128)}, u32[]{:S(2)}) copy-start(f32[256,1152]{1,0:T(8,128)} %copy-done.25) | copy-start | bytes 3538948
  161.6 15.9 %collective-permute-start.13 = (bf16[256,1152]{1,0:T(8,128)(2,1)S(1)}, bf16[256,1152]{1,0:T(8,128)(2,1)}, u32[]{:S(2)}, u32[]{:S(2)}) collective-permute-start(bf16[256,1152]{1,0:T(8,128)(2,1)S(1)} %fusion.102), channel_id=1, source_target_pairs={{0,2},{1,3},{2,0},{3,1},{4,6},{5,7},{6,4},{7,5},{8,10},{9,11},{10,... | collective-permute-start | bytes 1769480 | tf_op jit(solution)/shard_map/ppermute | solution.py:246
  187.9 15.3 %collective-permute-start.14 = (bf16[256,1152]{1,0:T(8,128)(2,1)}, bf16[256,1152]{1,0:T(8,128)(2,1)}, u32[]{:S(2)}, u32[]{:S(2)}) collective-permute-start(bf16[256,1152]{1,0:T(8,128)(2,1)} %get-tuple-element.171), channel_id=1, source_target_pairs={{0,2},{1,3},{2,0},{3,1},{4,6},{5,7},{6,4},{7,5},{8,10},{9,11},{10,... | collective-permute-start | bytes 1769480 | tf_op jit(solution)/shard_map/ppermute | solution.py:246
  205.0 8.5 %collective-permute-start.15 = (bf16[2,256,1152]{2,1,0:T(8,128)(2,1)S(1)}, bf16[2,256,1152]{2,1,0:T(8,128)(2,1)S(1)}, u32[]{:S(2)}, u32[]{:S(2)}) collective-permute-start(bf16[2,256,1152]{2,1,0:T(8,128)(2,1)S(1)} %maximum_select_fusion.10), channel_id=1, source_target_pairs={{0,1},{1,0},{2,3},{3,2},{4,5},{5,4},{6,7},{7,6},{8,9},{9,8},{10,11... | collective-permute-start | bytes 3538952 | tf_op jit(solution)/shard_map/ppermute | solution.py:246
  210.9 25.2 %collective-permute-start.16 = (bf16[2,256,1152]{2,1,0:T(8,128)(2,1)S(1)}, bf16[2,256,1152]{2,1,0:T(8,128)(2,1)S(1)}, u32[]{:S(2)}, u32[]{:S(2)}) collective-permute-start(bf16[2,256,1152]{2,1,0:T(8,128)(2,1)S(1)} %dynamic-slice_bitcast_fusion.1), channel_id=1, source_target_pairs={{0,1},{1,0},{2,3},{3,2},{4,5},{5,4},{6,7},{7,6},{8,9},{9,8},{10,11... | collective-permute-start | bytes 3538952 | tf_op jit(solution)/shard_map/ppermute | solution.py:246
  218.2 47.7 %collective-permute-start.21 = (f32[2,4,1,1024]{3,2,1,0:T(1,128)S(1)}, f32[2,4,1,1024]{3,2,1,0:T(1,128)S(1)}, u32[]{:S(2)}, u32[]{:S(2)}) collective-permute-start(f32[2,4,1,1024]{3,2,1,0:T(1,128)S(1)} %pad_maximum_fusion.10), channel_id=1, source_target_pairs={{4,0},{8,4},{12,8},{16,12},{20,16},{24,20},{28,24},{5,1},{9,5},{13... | collective-permute-start | bytes 98312 | tf_op jit(solution)/shard_map/ppermute | solution.py:251
  219.5 52.7 %collective-permute-start.20 = (f32[2,4,1,1024]{3,2,1,0:T(1,128)S(1)}, f32[2,4,1,1024]{3,2,1,0:T(1,128)S(1)}, u32[]{:S(2)}, u32[]{:S(2)}) collective-permute-start(f32[2,4,1,1024]{3,2,1,0:T(1,128)S(1)} %pad_maximum_fusion.10), channel_id=1, source_target_pairs={{0,4},{4,8},{8,12},{12,16},{16,20},{20,24},{24,28},{1,5},{5,9},{9,... | collective-permute-start | bytes 98312 | tf_op jit(solution)/shard_map/ppermute | solution.py:251
  228.5 43.7 %collective-permute-start.19 = (bf16[4,72,1024]{2,1,0:T(8,128)(2,1)}, bf16[4,72,1024]{2,1,0:T(8,128)(2,1)}, u32[]{:S(2)}, u32[]{:S(2)}) collective-permute-start(bf16[4,72,1024]{2,1,0:T(8,128)(2,1)} %bitcast.71.grad), channel_id=1, source_target_pairs={{4,0},{8,4},{12,8},{16,12},{20,16},{24,20},{28,24},{5,1},{9,5},{13... | collective-permute-start | bytes 1769480 | tf_op jit(solution)/shard_map/ppermute | solution.py:251
  229.8 42.4 %collective-permute-start.18 = (bf16[4,72,1024]{2,1,0:T(8,128)(2,1)}, bf16[4,72,1024]{2,1,0:T(8,128)(2,1)}, u32[]{:S(2)}, u32[]{:S(2)}) collective-permute-start(bf16[4,72,1024]{2,1,0:T(8,128)(2,1)} %bitcast.71.grad), channel_id=1, source_target_pairs={{0,4},{4,8},{8,12},{12,16},{16,20},{20,24},{24,28},{1,5},{5,9},{9,... | collective-permute-start | bytes 1769480 | tf_op jit(solution)/shard_map/ppermute | solution.py:251
  237.4 34.8 %collective-permute-start.17 = (bf16[256,1152]{1,0:T(8,128)(2,1)}, bf16[256,1152]{1,0:T(8,128)(2,1)}, u32[]{:S(2)}, u32[]{:S(2)}) collective-permute-start(bf16[256,1152]{1,0:T(8,128)(2,1)} %fusion.103), channel_id=1, source_target_pairs={{0,2},{1,3},{2,0},{3,1},{4,6},{5,7},{6,4},{7,5},{8,10},{9,11},{10,... | collective-permute-start | bytes 1769480 | tf_op jit(solution)/shard_map/ppermute | solution.py:246
  245.5 16.9 %copy-start.56 = (bf16[1152,1024]{1,0:T(8,128)(2,1)S(1)}, bf16[1152,1024]{1,0:T(8,128)(2,1)}, u32[]{:S(2)}) copy-start(bf16[1152,1024]{1,0:T(8,128)(2,1)} %copy.100) | copy-start | bytes 7077892
  262.4 37.1 %copy-start.19 = (bf16[4,72,1024]{2,1,0:T(8,128)(2,1)}, bf16[4,72,1024]{2,1,0:T(8,128)(2,1)S(1)}, u32[]{:S(2)}) copy-start(bf16[4,72,1024]{2,1,0:T(8,128)(2,1)S(1)} %get-tuple-element.55) | copy-start | bytes 1769476
  266.0 32.0 %collective-permute-start.22 = (bf16[2,2,144,576]{3,2,1,0:T(8,128)(2,1)S(1)}, bf16[2,2,144,576]{3,2,1,0:T(8,128)(2,1)S(1)}, u32[]{:S(2)}, u32[]{:S(2)}) collective-permute-start(bf16[2,2,144,576]{3,2,1,0:T(8,128)(2,1)S(1)} %fusion.93), channel_id=1, source_target_pairs={{0,4},{4,0},{8,12},{12,8},{16,20},{20,16},{24,28},{28,24},{1,5},{5... | collective-permute-start | bytes 1990664 | tf_op jit(solution)/shard_map/ppermute | solution.py:246
  283.3 59.2 %collective-permute-start.23 = (bf16[2,2,144,576]{3,2,1,0:T(8,128)(2,1)}, bf16[2,2,144,576]{3,2,1,0:T(8,128)(2,1)}, u32[]{:S(2)}, u32[]{:S(2)}) collective-permute-start(bf16[2,2,144,576]{3,2,1,0:T(8,128)(2,1)} %fusion.99), channel_id=1, source_target_pairs={{0,4},{4,0},{8,12},{12,8},{16,20},{20,16},{24,28},{28,24},{1,5},{5... | collective-permute-start | bytes 1990664 | tf_op jit(solution)/shard_map/ppermute | solution.py:246
  327.7 7.0 %collective-permute-start.27 = (f32[17,1728]{1,0:T(8,128)}, f32[17,1728]{1,0:T(8,128)}, u32[]{:S(2)}, u32[]{:S(2)}) collective-permute-start(f32[17,1728]{1,0:T(8,128)} %get-tuple-element.212), channel_id=1, source_target_pairs={{0,3},{1,2},{2,1},{3,0},{4,7},{5,6},{6,5},{7,4},{8,11},{9,10},{10,... | collective-permute-start | bytes 352520 | tf_op jit(solution)/shard_map/ppermute | solution.py:246
  327.7 10.1 %collective-permute-start.25 = (f32[17,1728]{1,0:T(8,128)}, f32[17,1728]{1,0:T(8,128)}, u32[]{:S(2)}, u32[]{:S(2)}) collective-permute-start(f32[17,1728]{1,0:T(8,128)} %get-tuple-element.213), channel_id=1, source_target_pairs={{0,1},{1,0},{2,3},{3,2},{4,5},{5,4},{6,7},{7,6},{8,9},{9,8},{10,11... | collective-permute-start | bytes 352520 | tf_op jit(solution)/shard_map/ppermute | solution.py:246
  329.3 9.1 %collective-permute-start.26 = (f32[17,1728]{1,0:T(8,128)}, f32[17,1728]{1,0:T(8,128)}, u32[]{:S(2)}, u32[]{:S(2)}) collective-permute-start(f32[17,1728]{1,0:T(8,128)} %get-tuple-element.214), channel_id=1, source_target_pairs={{0,2},{1,3},{2,0},{3,1},{4,6},{5,7},{6,4},{7,5},{8,10},{9,11},{10,... | collective-permute-start | bytes 352520 | tf_op jit(solution)/shard_map/ppermute | solution.py:246
  331.3 14.0 %collective-permute-start.24 = (bf16[2,288,1024]{2,1,0:T(8,128)(2,1)}, bf16[2,288,1024]{2,1,0:T(8,128)(2,1)S(1)}, u32[]{:S(2)}, u32[]{:S(2)}) collective-permute-start(bf16[2,288,1024]{2,1,0:T(8,128)(2,1)} %dynamic-slice_bitcast_fusion), channel_id=1, source_target_pairs={{0,1},{1,0},{2,3},{3,2},{4,5},{5,4},{6,7},{7,6},{8,9},{9,8},{10,11... | collective-permute-start | bytes 3538952 | tf_op jit(solution)/shard_map/ppermute | solution.py:246
  334.7 19.7 %collective-permute-start.35 = (bf16[2,144,576]{2,1,0:T(8,128)(2,1)}, bf16[2,144,576]{2,1,0:T(8,128)(2,1)S(1)}, u32[]{:S(2)}, u32[]{:S(2)}) collective-permute-start(bf16[2,144,576]{2,1,0:T(8,128)(2,1)} %fusion.105), channel_id=1, source_target_pairs={{0,16},{4,20},{8,24},{12,28},{16,0},{20,4},{24,8},{28,12},{1,17},{... | collective-permute-start | bytes 995336 | tf_op jit(solution)/shard_map/ppermute | solution.py:246
  340.3 14.1 %collective-permute-start.28 = (f32[20,1728]{1,0:T(8,128)S(1)}, f32[20,1728]{1,0:T(8,128)S(1)}, u32[]{:S(2)}, u32[]{:S(2)}) collective-permute-start(f32[20,1728]{1,0:T(8,128)S(1)} %pad_maximum_fusion.9), channel_id=1, source_target_pairs={{0,4},{4,0},{8,12},{12,8},{16,20},{20,16},{24,28},{28,24},{1,5},{5... | collective-permute-start | bytes 414728 | tf_op jit(solution)/shard_map/ppermute | solution.py:246
  354.5 11.4 %collective-permute-start.29 = (f32[20,1728]{1,0:T(8,128)S(1)}, f32[20,1728]{1,0:T(8,128)S(1)}, u32[]{:S(2)}, u32[]{:S(2)}) collective-permute-start(f32[20,1728]{1,0:T(8,128)S(1)} %fusion.196), channel_id=1, source_target_pairs={{0,8},{4,12},{8,0},{12,4},{16,24},{20,28},{24,16},{28,20},{1,9},{5... | collective-permute-start | bytes 414728 | tf_op jit(solution)/shard_map/ppermute | solution.py:246
  354.7 14.1 %collective-permute-start.36 = (bf16[144,576]{1,0:T(8,128)(2,1)S(1)}, bf16[144,576]{1,0:T(8,128)(2,1)S(1)}, u32[]{:S(2)}, u32[]{:S(2)}) collective-permute-start(bf16[144,576]{1,0:T(8,128)(2,1)S(1)} %fusion.107), channel_id=1, source_target_pairs={{0,8},{4,12},{8,0},{12,4},{16,24},{20,28},{24,16},{28,20},{1,9},{5... | collective-permute-start | bytes 497672 | tf_op jit(solution)/shard_map/ppermute | solution.py:246
  357.4 26.2 %collective-permute-start.37 = (bf16[2,144,576]{2,1,0:T(8,128)(2,1)S(1)}, bf16[2,144,576]{2,1,0:T(8,128)(2,1)S(1)}, u32[]{:S(2)}, u32[]{:S(2)}) collective-permute-start(bf16[2,144,576]{2,1,0:T(8,128)(2,1)S(1)} %copy-done.59), channel_id=1, source_target_pairs={{0,16},{4,20},{8,24},{12,28},{16,0},{20,4},{24,8},{28,12},{1,17},{... | collective-permute-start | bytes 995336 | tf_op jit(solution)/shard_map/ppermute | solution.py:246
  358.0 42.0 %collective-permute-start.31 = (bf16[288,1024]{1,0:T(8,128)(2,1)S(1)}, bf16[288,1024]{1,0:T(8,128)(2,1)S(1)}, u32[]{:S(2)}, u32[]{:S(2)}) collective-permute-start(bf16[288,1024]{1,0:T(8,128)(2,1)S(1)} %fusion.104), channel_id=1, source_target_pairs={{0,2},{1,3},{2,0},{3,1},{4,6},{5,7},{6,4},{7,5},{8,10},{9,11},{10,... | collective-permute-start | bytes 1769480 | tf_op jit(solution)/shard_map/ppermute | solution.py:246
  365.9 17.6 %collective-permute-start.30 = (f32[20,1728]{1,0:T(8,128)S(1)}, f32[20,1728]{1,0:T(8,128)S(1)}, u32[]{:S(2)}, u32[]{:S(2)}) collective-permute-start(f32[20,1728]{1,0:T(8,128)S(1)} %add.728), channel_id=1, source_target_pairs={{0,16},{4,20},{8,24},{12,28},{16,0},{20,4},{24,8},{28,12},{1,17},{... | collective-permute-start | bytes 414728 | tf_op jit(solution)/shard_map/ppermute | solution.py:246
  369.6 22.2 %copy-start.49 = (f32[2,2,144,576]{3,2,1,0:T(8,128)S(1)}, f32[2,2,144,576]{3,2,1,0:T(8,128)}, u32[]{:S(2)}) copy-start(f32[2,2,144,576]{3,2,1,0:T(8,128)} %copy-done.48) | copy-start | bytes 3981316
  389.9 4.9 %collective-permute-start.32 = (f32[2,288]{1,0:T(2,128)S(1)}, f32[2,288]{1,0:T(2,128)S(1)}, u32[]{:S(2)}, u32[]{:S(2)}) collective-permute-start(f32[2,288]{1,0:T(2,128)S(1)} %bitcast.466), channel_id=1, source_target_pairs={{0,1},{1,0},{2,3},{3,2},{4,5},{5,4},{6,7},{7,6},{8,9},{9,8},{10,11... | collective-permute-start | bytes 6920 | tf_op jit(solution)/shard_map/ppermute | solution.py:246
  390.0 4.8 %collective-permute-start.33 = (f32[2,288]{1,0:T(2,128)S(1)}, f32[2,288]{1,0:T(2,128)S(1)}, u32[]{:S(2)}, u32[]{:S(2)}) collective-permute-start(f32[2,288]{1,0:T(2,128)S(1)} %bitcast.465), channel_id=1, source_target_pairs={{0,2},{1,3},{2,0},{3,1},{4,6},{5,7},{6,4},{7,5},{8,10},{9,11},{10,... | collective-permute-start | bytes 6920 | tf_op jit(solution)/shard_map/ppermute | solution.py:246
  390.7 4.0 collective-permute-start.34
  391.9 7.0 %collective-permute-start.38 = (bf16[144,576]{1,0:T(8,128)(2,1)S(1)}, bf16[144,576]{1,0:T(8,128)(2,1)S(1)}, u32[]{:S(2)}, u32[]{:S(2)}) collective-permute-start(bf16[144,576]{1,0:T(8,128)(2,1)S(1)} %fusion.108), channel_id=1, source_target_pairs={{0,8},{4,12},{8,0},{12,4},{16,24},{20,28},{24,16},{28,20},{1,9},{5... | collective-permute-start | bytes 497672 | tf_op jit(solution)/shard_map/ppermute | solution.py:246
  (99 other events, 485.4 us)
Sparse Core Ops, SparseCore 0:
  202.5 135.7 reduce-scatter.3

commit v2 on v1

--- a/solution.py
+++ b/solution.py
@@ -301,7 +301,7 @@
     return stay + come.astype(F32)
 
 
-def scatter_data_steps(partial):
+def scatter_data(partial):
     size = lax.axis_size("dp")
     index = lax.axis_index("dp")
     bits = bits_of("dp")
@@ -318,17 +318,9 @@
         come = after((yield sent), come)
         held = kept.astype(F32) + come.astype(F32)
         left.remove(bit)
+        if left:
+            held = held.astype(BF16)
     return held
-
-
-def scatter_data(partials):
-    joined = jnp.concatenate([partial.astype(BF16) for partial in partials], axis=1)
-    found = lax.psum_scatter(joined, "dp", scatter_dimension=0, tiled=True)
-    cuts, at = [], 0
-    for partial in partials[:-1]:
-        at += partial.shape[1]
-        cuts.append(at)
-    return joined, lambda anchor: jnp.split(after(anchor, found).astype(F32), cuts, axis=1)
 
 
 def finish(steps, anchor=None):
@@ -515,7 +507,8 @@
     grad_pre = after(next(entry_steps), grad_pre)
     grad_out_mine = mine(out_grad).astype(F32)
     grad_up_w = jnp.einsum("td,tf->df", entry_m, grad_pre, preferred_element_type=F32)
-    wide_sent, wide_sums = scatter_data([grad_down_w, grad_up_w])
+    down_steps, up_steps = scatter_data(grad_down_w), scatter_data(grad_up_w)
+    wide_sent = next(down_steps), next(up_steps)
     grad_entry_m = finish(entry_steps, wide_sent)
     grad_down_b = jnp.sum(grad_branch_m.astype(F32), axis=0)
     grad_up_b = jnp.sum(grad_pre.astype(F32), axis=0)
@@ -554,9 +547,6 @@
         bases,
     )
     mlp_steps.send(grad_heads)
-    branch_m = finish(mlp_steps, grad_query) + down_bias.astype(F32)
-    output = (middle + gate_m * branch_m).astype(BF16)
-    grad_gate_m = grad_out_mine * branch_m
     grad_out_w = lax.dot_general(
         grad_branch, attended_flat, (((0,), (1,)), ((), ())), preferred_element_type=F32
     )
@@ -572,17 +562,21 @@
         [side[0] for side in side_stats],
         [side[1] for side in side_stats],
     )
+    branch_m = finish(mlp_steps, grad_keys) + down_bias.astype(F32)
+    output = (middle + gate_m * branch_m).astype(BF16)
+    grad_gate_m = grad_out_mine * branch_m
+    down_steps.send(grad_keys)
     grad_proj = [x.reshape(local_width, rows) for x in (grad_query, grad_keys, grad_values)]
     grad_q_w, grad_k_w, grad_v_w = (
         lax.dot_general(entry, x, (((0,), (1,)), ((), ())), preferred_element_type=F32)
         for x in grad_proj
     )
-    early_steps = scatter_data_steps(jnp.concatenate([grad_out_w, grad_q_w], axis=1))
+    early_steps = scatter_data(jnp.concatenate([grad_out_w, grad_q_w], axis=1))
     next(early_steps)
-    early_sent = early_steps.send(grad_keys)
-    late_steps = scatter_data_steps(jnp.concatenate([grad_k_w, grad_v_w], axis=1))
+    up_steps.send(grad_keys)
+    late_steps = scatter_data(jnp.concatenate([grad_k_w, grad_v_w], axis=1))
     late_sent = next(late_steps)
-    grad_proj = after((late_sent, early_sent), *grad_proj)
+    grad_proj = after(late_sent, *grad_proj)
     grad_in_b = jnp.stack([jnp.sum(grad_proj[c].astype(F32), axis=1) for c in (0, 2)])
     grad_entry = lax.dot_general(
         in_weight.reshape(width, 3 * local_width),
@@ -637,13 +631,17 @@
             for value in (grad_in_b.reshape(-1), grad_up_b, grad_down_b)
         ]
     )
-    late_sent = late_steps.send(tokens_sent)
+    early_steps.send(tokens_sent)
+    late_sent = late_steps.send(input_part)
     tokens_sent = tokens_steps.send(late_sent)
     for place, bit in enumerate(bits_of("dp")):
         come = swap(small, "dp", bit)
         if place == 0:
             come = after(tokens_sent, come)
         small = small + come
+        if place == 0:
+            tokens_come = finish(tokens_steps, small)
+    small = after(tokens_come, small)
     grad_mod = small[:latents].astype(BF16)
     sum_out_b = small[latents, :width]
     sum_in_b = small[latents + 1, : 2 * local_width]
@@ -667,9 +665,10 @@
             bit,
         )
 
-    grad_tokens = finish(tokens_steps, grad_mod_w).T
-    sum_down_w, sum_up_w = wide_sums(grad_mod_w)
-    early = finish(early_steps, tokens_sent)
+    grad_tokens = tokens_come.T
+    sum_down_w = finish(down_steps, tokens_come)
+    sum_up_w = finish(up_steps, small)
+    early = finish(early_steps, small)
     late = finish(late_steps, small)
     sum_out_w = early[:, :local_width]
     sum_in_w = jnp.stack(

time: 423 us -> 474 us (1.12)
  waiting for transfers between devices: 98.1 us -> 174 us
  local copies, waits for them, and re-layouts: 63.1 us -> 45.1 us
  between operations: 16.3 us -> 2.9 us
  other arithmetic: 64.9 us -> 74.8 us
  matrix products: 74 us -> 65.4 us
    ppermute x33 -> x39, waiting for transfers between devices: 92.8 us -> 147 us  [swap(): lax.ppermute(value, axis, [(i, i ^ bit) for i in range(lax.axis_size(axis...]
    ppermute x6, waiting for transfers between devices: 5.33 us -> 27.1 us  [shift(): lax.ppermute(value, axis, [(i, i + distance) for i in devices if i + dist...]
    unnamed x224 -> x203, local copies, waits for them, and re-layouts: 27.2 us -> 11.3 us
    convert_element_type x1 -> x9, other arithmetic: 0.6 us -> 9.83 us  [the longest x8 9.82 us: scatter_data(): held = held.astype(BF16)]
    ppermute x33 -> x39, starting transfers between devices: 38.7 us -> 45.4 us  [swap(): lax.ppermute(value, axis, [(i, i ^ bit) for i in range(lax.axis_size(axis...]
    squeeze x0 -> x10, local copies, waits for them, and re-layouts: none -> 5.37 us  [scatter_data(): lax.dynamic_index_in_dim(held, 1 - mine, axis, keepdims=False).astype(BF16)]
  transfers between devices with their start and end apart: 40 -> 45, of which waited for: 17 -> 19; matrix products, arithmetic and copies ran while one was open for 33% -> 28% of each run, Pallas kernels for 8% -> 7%
where the time goes in v2:
time: 474 us; the launch traced here: 467 us
  waiting for transfers between devices  174 us (37%)
  other arithmetic  74.8 us (16%)
  starting transfers between devices  66.5 us (14%)
  matrix products  65.4 us (14%)
  local copies, waits for them, and re-layouts  45.1 us (10%)
  Pallas kernels  38.5 us (8%)
    ppermute x39, waiting for transfers between devices, swap(): lax.ppermute(value, axis, [(i, i ^ bit) for i in range(lax.axis_size(axis...  147 us
    ppermute x39, starting transfers between devices, swap(): lax.ppermute(value, axis, [(i, i ^ bit) for i in range(lax.axis_size(axis...  45.4 us
    ppermute x6, waiting for transfers between devices, shift(): lax.ppermute(value, axis, [(i, i + distance) for i in devices if i + dist...  27.1 us
    ppermute x6, starting transfers between devices, shift(): lax.ppermute(value, axis, [(i, i + distance) for i in devices if i + dist...  21 us
    pallas_call x1, Pallas kernels, attend_back(): pl.pallas_call(functools.partial(backward_kernel, bases, heads), out_shap...  16.8 us
    pallas_call x2, Pallas kernels, attend(): pl.pallas_call(functools.partial(forward_kernel, bases, heads, last), out...  14.6 us
    select_n x15, other arithmetic, in_order(): jnp.where(upper, jnp.stack([other, mine], axis=dim), jnp.stack([mine, oth...  11.7 us
    unnamed x203, local copies, waits for them, and re-layouts  11.3 us
  transfers between devices with their start and end apart: 45, of which 19 were waited for; matrix products, arithmetic and copies ran while one was open for 28% of the time, Pallas kernels for 7%

profile of v2, /device:TPU:0, one launch (start us, length us, event | category | flops | bytes accessed | tf_op | source)
XLA Modules:
  0.0 467.3 jit_solution(4423515819608631862)
XLA Ops:
  2.8 5.7 %collective-permute-start.2 = (bf16[256,1152]{1,0:T(8,128)(2,1)}, bf16[256,1152]{1,0:T(8,128)(2,1)}, u32[]{:S(2)}, u32[]{:S(2)}) collective-permute-start(bf16[256,1152]{1,0:T(8,128)(2,1)} %constant_dynamic-slice_fusion.12), channel_id=1, source_target_pairs={{0,4},{4,8},{8,12},{12,16},{16,20},{20,24},{24,28},{1,5},{5,9},{9,... | collective-permute-start | bytes 1769480 | tf_op jit(solution)/shard_map/ppermute | solution.py:251
  10.5 3.3 fusion.62
  15.9 2.4 fusion.27
  25.1 2.5 fusion.63
  27.8 5.4 %collective-permute-done.2 = bf16[256,1152]{1,0:T(8,128)(2,1)} collective-permute-done((bf16[256,1152]{1,0:T(8,128)(2,1)}, bf16[256,1152]{1,0:T(8,128)(2,1)}, u32[]{:S(2)}, u32[]{:S(2)}) %collective-permute-start.2) | collective-permute-done | bytes 589856 | tf_op jit(solution)/shard_map/ppermute | solution.py:251
  34.8 9.1 %shard_map.237 = (f32[4,72,1024]{2,1,0:T(8,128)S(1)}, f32[4,1,1024]{2,1,0:T(1,128)S(1)}, f32[4,1,1024]{2,1,0:T(1,128)S(1)}) custom-call(s32[1,2,4]{2,1,0:T(2,128)S(1)} %add_bitcast_fusion.2.bounds, s32[2,1024]{1,0:T(2,128)S(1)} %pad_add_fusion.span, bf16[4,72,1024]{2,1,0:T(8,128)(2,1)S(1)} %bitcast.420, f32[4,72,1024]{2,1,0:T(8,128)S(1)} %broadcast_in_dim.212.mixed_in, ...), custom_call_target="tpu_custom_call" | custom-call | flops 19327352832 | bytes 25165824 | tf_op jit(solution)/shard_map/pallas_call | solution.py:89
  44.5 5.1 %collective-permute-done.3 = bf16[256,1152]{1,0:T(8,128)(2,1)S(1)} collective-permute-done((bf16[256,1152]{1,0:T(8,128)(2,1)}, bf16[256,1152]{1,0:T(8,128)(2,1)S(1)}, u32[]{:S(2)}, u32[]{:S(2)}) %collective-permute-start.3) | collective-permute-done | bytes 589856 | tf_op jit(solution)/shard_map/ppermute | solution.py:246
  54.2 6.0 %collective-permute-done.6 = bf16[256,1152]{1,0:T(8,128)(2,1)S(1)} collective-permute-done((bf16[256,1152]{1,0:T(8,128)(2,1)}, bf16[256,1152]{1,0:T(8,128)(2,1)S(1)}, u32[]{:S(2)}, u32[]{:S(2)}) %collective-permute-start.6) | collective-permute-done | bytes 589856 | tf_op jit(solution)/shard_map/ppermute | solution.py:246
  67.9 3.4 fusion.64
  72.3 3.9 fusion.65
  77.2 5.6 %shard_map.238 = (bf16[4,72,1024]{2,1,0:T(8,128)(2,1)S(1)}, f32[4,1,1024]{2,1,0:T(1,128)S(1)}, f32[4,1,1024]{2,1,0:T(1,128)}) custom-call(s32[2,2,4]{2,1,0:T(2,128)S(1)} %pad_add_fusion.4.bounds, s32[2,1024]{1,0:T(2,128)S(1)} %pad_add_fusion.span, bf16[4,72,1024]{2,1,0:T(8,128)(2,1)S(1)} %bitcast.421, f32[4,72,1024]{2,1,0:T(8,128)S(1)} %get-tuple-element.51.mixed_in, ...), custom_call_target="tpu_custom_call" | custom-call | flops 19327352832 | bytes 25165824 | tf_op jit(solution)/shard_map/pallas_call | solution.py:89
  97.8 12.4 %collective-permute-done.9 = bf16[256,1152]{1,0:T(8,128)(2,1)} collective-permute-done((bf16[256,1152]{1,0:T(8,128)(2,1)}, bf16[256,1152]{1,0:T(8,128)(2,1)}, u32[]{:S(2)}, u32[]{:S(2)}) %collective-permute-start.9) | collective-permute-done | bytes 589856 | tf_op jit(solution)/shard_map/ppermute | solution.py:246
  114.0 13.2 %collective-permute-done.10 = bf16[256,1152]{1,0:T(8,128)(2,1)S(1)} collective-permute-done((bf16[256,1152]{1,0:T(8,128)(2,1)S(1)}, bf16[256,1152]{1,0:T(8,128)(2,1)S(1)}, u32[]{:S(2)}, u32[]{:S(2)}) %collective-permute-start.10) | collective-permute-done | bytes 589856 | tf_op jit(solution)/shard_map/ppermute | solution.py:246
  129.2 3.5 fusion.168
  133.6 5.8 %fusion.34 = (bf16[1024,1152]{1,0:T(8,128)(2,1)S(1)}, bf16[1024,1152]{1,0:T(8,128)(2,1)S(1)}) fusion(f32[1024,1152]{1,0:T(8,128)S(1)} %fusion.168, f32[1152]{0:T(1024)S(1)} %copy-done.78, bf16[1024,1152]{1,0:T(8,128)(2,1)S(1)} %bitcast.476, bf16[1152,1152]{1,0:T(8,128)(2,1)S(1)} %copy-done), kind=kOutput, calls=%fused_computation.47 | convolution fusion | flops 2745040896 | bytes 14455296 | tf_op jit(solution)/shard_map/dot_general | solution.py:497
  139.5 3.8 convolution_convert_fusion.5
  143.4 3.3 convolution_convert_fusion.1
  148.0 3.3 convolution_convert_fusion
  154.9 14.1 %collective-permute-done.13 = bf16[256,1152]{1,0:T(8,128)(2,1)S(1)} collective-permute-done((bf16[256,1152]{1,0:T(8,128)(2,1)S(1)}, bf16[256,1152]{1,0:T(8,128)(2,1)S(1)}, u32[]{:S(2)}, u32[]{:S(2)}) %collective-permute-start.13) | collective-permute-done | bytes 589856 | tf_op jit(solution)/shard_map/ppermute | solution.py:246
  171.5 3.2 convert_reduce_fusion.7
  177.0 2.7 copy.83
  179.7 6.7 %collective-permute-start.42 = (bf16[2,2,144,1152]{3,2,1,0:T(8,128)(2,1)}, bf16[2,2,144,1152]{3,2,1,0:T(8,128)(2,1)}, u32[]{:S(2)}, u32[]{:S(2)}) collective-permute-start(bf16[2,2,144,1152]{3,2,1,0:T(8,128)(2,1)} %dynamic-slice_bitcast_fusion.1), channel_id=1, source_target_pairs={{0,4},{4,0},{8,12},{12,8},{16,20},{20,16},{24,28},{28,24},{1,5},{5... | collective-permute-start | bytes 3981320 | tf_op jit(solution)/shard_map/ppermute | solution.py:246
  191.8 5.2 %convolution_convert_fusion.4 = bf16[1024,1152]{1,0:T(8,128)(2,1)S(1)} fusion(bf16[1024,1152]{1,0:T(8,128)(2,1)} %copy-done.97, bf16[1152,1152]{1,0:T(8,128)(2,1)S(1)} %copy-done.92), kind=kOutput, calls=%fused_computation.59 | convolution fusion | flops 2719088640 | bytes 7372800 | tf_op jit(solution)/shard_map/tf,df->td/dot_general | solution.py:524
  204.1 10.0 %collective-permute-start.17 = (bf16[4,72,1024]{2,1,0:T(8,128)(2,1)}, bf16[4,72,1024]{2,1,0:T(8,128)(2,1)}, u32[]{:S(2)}, u32[]{:S(2)}) collective-permute-start(bf16[4,72,1024]{2,1,0:T(8,128)(2,1)} %bitcast.75.grad), channel_id=1, source_target_pairs={{0,4},{4,8},{8,12},{12,16},{16,20},{20,24},{24,28},{1,5},{5,9},{9,... | collective-permute-start | bytes 1769480 | tf_op jit(solution)/shard_map/ppermute | solution.py:251
  218.5 4.4 copy.86
  225.1 16.8 %shard_map.239 = (bf16[4,72,1024]{2,1,0:T(8,128)(2,1)S(1)}, f32[4,72,1024]{2,1,0:T(8,128)S(1)}, f32[4,72,1024]{2,1,0:T(8,128)S(1)}) custom-call(s32[3,2,4]{2,1,0:T(2,128)S(1)} %pad_add_fusion.3.bounds, s32[2,1024]{1,0:T(2,128)S(1)} %pad_add_fusion.span, bf16[4,72,1024]{2,1,0:T(8,128)(2,1)S(1)} %bitcast.422, bf16[4,72,1024]{2,1,0:T(8,128)(2,1)} %bitcast.75.grad, ...), custom_call_target="tpu_custom_call" | custom-call | flops 19327352832 | bytes 25165824 | tf_op jit(solution)/shard_map/pallas_call | solution.py:171
  246.6 10.5 %collective-permute-done.20 = f32[2,4,1,1024]{3,2,1,0:T(1,128)S(1)} collective-permute-done((f32[2,4,1,1024]{3,2,1,0:T(1,128)S(1)}, f32[2,4,1,1024]{3,2,1,0:T(1,128)S(1)}, u32[]{:S(2)}, u32[]{:S(2)}) %collective-permute-start.20) | collective-permute-done | bytes 32800 | tf_op jit(solution)/shard_map/ppermute | solution.py:251
  258.6 11.1 %collective-permute-done.19 = f32[2,4,1,1024]{3,2,1,0:T(1,128)S(1)} collective-permute-done((f32[2,4,1,1024]{3,2,1,0:T(1,128)S(1)}, f32[2,4,1,1024]{3,2,1,0:T(1,128)S(1)}, u32[]{:S(2)}, u32[]{:S(2)}) %collective-permute-start.19) | collective-permute-done | bytes 32800 | tf_op jit(solution)/shard_map/ppermute | solution.py:251
  270.3 3.7 collective-permute-start.34
  274.0 7.1 %shard_map.240 = (bf16[4,72,1024]{2,1,0:T(8,128)(2,1)S(1)}, bf16[4,72,1024]{2,1,0:T(8,128)(2,1)S(1)}) custom-call(s32[2,2,4]{2,1,0:T(2,128)S(1)} %pad_add_fusion.4.bounds, bf16[4,72,1024]{2,1,0:T(8,128)(2,1)S(1)} %bitcast.419, bf16[4,72,1024]{2,1,0:T(8,128)(2,1)S(1)} %bitcast.416, f32[4,72,1024]{2,1,0:T(8,128)S(1)} %get-tuple-element.61.keys_in, ...), custom_call_target="tpu_custom_call" | custom-call | flops 19327352832 | bytes 25165824 | tf_op jit(solution)/shard_map/pallas_call | solution.py:234
  283.5 2.6 convert_multiply_fusion
  296.1 3.2 collective-permute-start.22
  300.8 2.9 convolution_bitcast_fusion
  303.7 2.9 fusion.160
  306.6 3.2 fusion.11
  314.3 2.9 constant_dynamic-slice_fusion.10
  322.1 2.7 fusion.93
  324.8 4.0 convert_element_type.448
  328.8 2.8 copy.85
  332.9 2.7 collective-permute-start.43
  349.8 19.1 %collective-permute-done.29 = f32[20,1728]{1,0:T(8,128)S(1)} collective-permute-done((f32[20,1728]{1,0:T(8,128)S(1)}, f32[20,1728]{1,0:T(8,128)S(1)}, u32[]{:S(2)}, u32[]{:S(2)}) %collective-permute-start.29) | collective-permute-done | bytes 138272 | tf_op jit(solution)/shard_map/ppermute | solution.py:246
  369.0 2.6 collective-permute-start.30
  373.1 44.1 %collective-permute-done.30 = f32[20,1728]{1,0:T(8,128)S(1)} collective-permute-done((f32[20,1728]{1,0:T(8,128)S(1)}, f32[20,1728]{1,0:T(8,128)S(1)}, u32[]{:S(2)}, u32[]{:S(2)}) %collective-permute-start.30) | collective-permute-done | bytes 138272 | tf_op jit(solution)/shard_map/ppermute | solution.py:246
  424.0 11.3 %collective-permute-done.35 = bf16[2,144,576]{2,1,0:T(8,128)(2,1)S(1)} collective-permute-done((bf16[2,144,576]{2,1,0:T(8,128)(2,1)S(1)}, bf16[2,144,576]{2,1,0:T(8,128)(2,1)S(1)}, u32[]{:S(2)}, u32[]{:S(2)}) %collective-permute-start.35) | collective-permute-done | bytes 331808 | tf_op jit(solution)/shard_map/ppermute | solution.py:246
  436.1 2.7 fusion.130
  448.7 3.8 collective-permute-done.36
  454.2 5.5 %collective-permute-done.44 = bf16[144,1152]{1,0:T(8,128)(2,1)S(1)} collective-permute-done((bf16[144,1152]{1,0:T(8,128)(2,1)S(1)}, bf16[144,1152]{1,0:T(8,128)(2,1)S(1)}, u32[]{:S(2)}, u32[]{:S(2)}) %collective-permute-start.44) | collective-permute-done | bytes 331808 | tf_op jit(solution)/shard_map/ppermute | solution.py:246
  460.5 5.6 %collective-permute-done.41 = bf16[144,1152]{1,0:T(8,128)(2,1)S(1)} collective-permute-done((bf16[144,1152]{1,0:T(8,128)(2,1)S(1)}, bf16[144,1152]{1,0:T(8,128)(2,1)S(1)}, u32[]{:S(2)}, u32[]{:S(2)}) %collective-permute-start.41) | collective-permute-done | bytes 331808 | tf_op jit(solution)/shard_map/ppermute | solution.py:246
  (455 shorter events, 146.4 us)
Async XLA Ops:
  0.6 132.7 %copy-start = (bf16[1152,1152]{1,0:T(8,128)(2,1)S(1)}, bf16[1152,1152]{1,0:T(8,128)(2,1)}, u32[]{:S(2)}) copy-start(bf16[1152,1152]{1,0:T(8,128)(2,1)} %param.21) | copy-start | bytes 7962628
  2.8 30.4 %collective-permute-start.2 = (bf16[256,1152]{1,0:T(8,128)(2,1)}, bf16[256,1152]{1,0:T(8,128)(2,1)}, u32[]{:S(2)}, u32[]{:S(2)}) collective-permute-start(bf16[256,1152]{1,0:T(8,128)(2,1)} %constant_dynamic-slice_fusion.12), channel_id=1, source_target_pairs={{0,4},{4,8},{8,12},{12,16},{16,20},{20,24},{24,28},{1,5},{5,9},{9,... | collective-permute-start | bytes 1769480 | tf_op jit(solution)/shard_map/ppermute | solution.py:251
  8.5 35.4 %collective-permute-start.5 = (bf16[256,1152]{1,0:T(8,128)(2,1)}, bf16[256,1152]{1,0:T(8,128)(2,1)}, u32[]{:S(2)}, u32[]{:S(2)}) collective-permute-start(bf16[256,1152]{1,0:T(8,128)(2,1)} %constant_dynamic-slice_fusion.12), channel_id=1, source_target_pairs={{4,0},{8,4},{12,8},{16,12},{20,16},{24,20},{28,24},{5,1},{9,5},{13... | collective-permute-start | bytes 1769480 | tf_op jit(solution)/shard_map/ppermute | solution.py:251
  13.8 5.8 %collective-permute-start = (bf16[1,16,1728]{2,1,0:T(8,128)(2,1)S(1)}, bf16[1,16,1728]{2,1,0:T(8,128)(2,1)S(1)}, u32[]{:S(2)}, u32[]{:S(2)}) collective-permute-start(bf16[1,16,1728]{2,1,0:T(8,128)(2,1)S(1)} %bitcast.486), channel_id=1, source_target_pairs={{0,2},{1,3},{2,0},{3,1},{4,6},{5,7},{6,4},{7,5},{8,10},{9,11},{10,... | collective-permute-start | bytes 165896 | tf_op jit(solution)/shard_map/ppermute | solution.py:246
  15.9 111.7 %copy-start.73 = (s32[16]{0:T(128)}, s32[16]{0:T(128)S(1)}, u32[]{:S(2)}) copy-start(s32[16]{0:T(128)S(1)} %get-tuple-element.124) | copy-start | bytes 196
  19.6 1.4 collective-permute-start.1
  21.4 106.2 %copy-start.59 = (bf16[16,6912]{1,0:T(8,128)(2,1)}, bf16[16,6912]{1,0:T(8,128)(2,1)S(1)}, u32[]{:S(2)}) copy-start(bf16[16,6912]{1,0:T(8,128)(2,1)S(1)} %reshape.1193) | copy-start | bytes 663556
  33.2 16.5 %collective-permute-start.3 = (bf16[256,1152]{1,0:T(8,128)(2,1)}, bf16[256,1152]{1,0:T(8,128)(2,1)S(1)}, u32[]{:S(2)}, u32[]{:S(2)}) collective-permute-start(bf16[256,1152]{1,0:T(8,128)(2,1)} %collective-permute-done.2), channel_id=1, source_target_pairs={{0,2},{1,3},{2,0},{3,1},{4,6},{5,7},{6,4},{7,5},{8,10},{9,11},{10,... | collective-permute-start | bytes 1769480 | tf_op jit(solution)/shard_map/ppermute | solution.py:246
  43.9 16.3 %collective-permute-start.6 = (bf16[256,1152]{1,0:T(8,128)(2,1)}, bf16[256,1152]{1,0:T(8,128)(2,1)S(1)}, u32[]{:S(2)}, u32[]{:S(2)}) collective-permute-start(bf16[256,1152]{1,0:T(8,128)(2,1)} %collective-permute-done.5), channel_id=1, source_target_pairs={{0,2},{1,3},{2,0},{3,1},{4,6},{5,7},{6,4},{7,5},{8,10},{9,11},{10,... | collective-permute-start | bytes 1769480 | tf_op jit(solution)/shard_map/ppermute | solution.py:246
  51.1 13.6 %collective-permute-start.4 = (bf16[2,256,1152]{2,1,0:T(8,128)(2,1)S(1)}, bf16[2,256,1152]{2,1,0:T(8,128)(2,1)S(1)}, u32[]{:S(2)}, u32[]{:S(2)}) collective-permute-start(bf16[2,256,1152]{2,1,0:T(8,128)(2,1)S(1)} %maximum_select_fusion.4), channel_id=1, source_target_pairs={{0,1},{1,0},{2,3},{3,2},{4,5},{5,4},{6,7},{7,6},{8,9},{9,8},{10,11... | collective-permute-start | bytes 3538952 | tf_op jit(solution)/shard_map/ppermute | solution.py:246
  61.7 4.6 collective-permute-start.7
  86.8 3.3 collective-permute-start.8
  94.2 15.9 %collective-permute-start.9 = (bf16[256,1152]{1,0:T(8,128)(2,1)}, bf16[256,1152]{1,0:T(8,128)(2,1)}, u32[]{:S(2)}, u32[]{:S(2)}) collective-permute-start(bf16[256,1152]{1,0:T(8,128)(2,1)} %fusion.108), channel_id=1, source_target_pairs={{0,2},{1,3},{2,0},{3,1},{4,6},{5,7},{6,4},{7,5},{8,10},{9,11},{10,... | collective-permute-start | bytes 1769480 | tf_op jit(solution)/shard_map/ppermute | solution.py:246
  112.4 14.9 %collective-permute-start.10 = (bf16[256,1152]{1,0:T(8,128)(2,1)S(1)}, bf16[256,1152]{1,0:T(8,128)(2,1)S(1)}, u32[]{:S(2)}, u32[]{:S(2)}) collective-permute-start(bf16[256,1152]{1,0:T(8,128)(2,1)S(1)} %fusion.90), channel_id=1, source_target_pairs={{0,2},{1,3},{2,0},{3,1},{4,6},{5,7},{6,4},{7,5},{8,10},{9,11},{10,... | collective-permute-start | bytes 1769480 | tf_op jit(solution)/shard_map/ppermute | solution.py:246
  127.4 5.5 %collective-permute-start.11 = (bf16[2,256,1152]{2,1,0:T(8,128)(2,1)S(1)}, bf16[2,256,1152]{2,1,0:T(8,128)(2,1)S(1)}, u32[]{:S(2)}, u32[]{:S(2)}) collective-permute-start(bf16[2,256,1152]{2,1,0:T(8,128)(2,1)S(1)} %maximum_select_fusion.8), channel_id=1, source_target_pairs={{0,1},{1,0},{2,3},{3,2},{4,5},{5,4},{6,7},{7,6},{8,9},{9,8},{10,11... | collective-permute-start | bytes 3538952 | tf_op jit(solution)/shard_map/ppermute | solution.py:246
  143.3 9.3 %collective-permute-start.12 = (bf16[2,256,1152]{2,1,0:T(8,128)(2,1)S(1)}, bf16[2,256,1152]{2,1,0:T(8,128)(2,1)S(1)}, u32[]{:S(2)}, u32[]{:S(2)}) collective-permute-start(bf16[2,256,1152]{2,1,0:T(8,128)(2,1)S(1)} %dynamic-slice_bitcast_fusion.4), channel_id=1, source_target_pairs={{0,1},{1,0},{2,3},{3,2},{4,5},{5,4},{6,7},{7,6},{8,9},{9,8},{10,11... | collective-permute-start | bytes 3538952 | tf_op jit(solution)/shard_map/ppermute | solution.py:246
  153.3 15.8 %collective-permute-start.13 = (bf16[256,1152]{1,0:T(8,128)(2,1)S(1)}, bf16[256,1152]{1,0:T(8,128)(2,1)S(1)}, u32[]{:S(2)}, u32[]{:S(2)}) collective-permute-start(bf16[256,1152]{1,0:T(8,128)(2,1)S(1)} %fusion.109), channel_id=1, source_target_pairs={{0,2},{1,3},{2,0},{3,1},{4,6},{5,7},{6,4},{7,5},{8,10},{9,11},{10,... | collective-permute-start | bytes 1769480 | tf_op jit(solution)/shard_map/ppermute | solution.py:246
  174.6 15.3 %collective-permute-start.14 = (bf16[256,1152]{1,0:T(8,128)(2,1)}, bf16[256,1152]{1,0:T(8,128)(2,1)}, u32[]{:S(2)}, u32[]{:S(2)}) collective-permute-start(bf16[256,1152]{1,0:T(8,128)(2,1)} %get-tuple-element.118), channel_id=1, source_target_pairs={{0,2},{1,3},{2,0},{3,1},{4,6},{5,7},{6,4},{7,5},{8,10},{9,11},{10,... | collective-permute-start | bytes 1769480 | tf_op jit(solution)/shard_map/ppermute | solution.py:246
  179.7 101.4 %collective-permute-start.42 = (bf16[2,2,144,1152]{3,2,1,0:T(8,128)(2,1)}, bf16[2,2,144,1152]{3,2,1,0:T(8,128)(2,1)}, u32[]{:S(2)}, u32[]{:S(2)}) collective-permute-start(bf16[2,2,144,1152]{3,2,1,0:T(8,128)(2,1)} %dynamic-slice_bitcast_fusion.1), channel_id=1, source_target_pairs={{0,4},{4,0},{8,12},{12,8},{16,20},{20,16},{24,28},{28,24},{1,5},{5... | collective-permute-start | bytes 3981320 | tf_op jit(solution)/shard_map/ppermute | solution.py:246
  186.4 100.6 %collective-permute-start.39 = (bf16[2,2,144,1152]{3,2,1,0:T(8,128)(2,1)}, bf16[2,2,144,1152]{3,2,1,0:T(8,128)(2,1)}, u32[]{:S(2)}, u32[]{:S(2)}) collective-permute-start(bf16[2,2,144,1152]{3,2,1,0:T(8,128)(2,1)} %dynamic-slice_bitcast_fusion), channel_id=1, source_target_pairs={{0,4},{4,0},{8,12},{12,8},{16,20},{20,16},{24,28},{28,24},{1,5},{5... | collective-permute-start | bytes 3981320 | tf_op jit(solution)/shard_map/ppermute | solution.py:246
  191.7 7.8 %collective-permute-start.15 = (bf16[2,256,1152]{2,1,0:T(8,128)(2,1)S(1)}, bf16[2,256,1152]{2,1,0:T(8,128)(2,1)S(1)}, u32[]{:S(2)}, u32[]{:S(2)}) collective-permute-start(bf16[2,256,1152]{2,1,0:T(8,128)(2,1)S(1)} %maximum_select_fusion.10), channel_id=1, source_target_pairs={{0,1},{1,0},{2,3},{3,2},{4,5},{5,4},{6,7},{7,6},{8,9},{9,8},{10,11... | collective-permute-start | bytes 3538952 | tf_op jit(solution)/shard_map/ppermute | solution.py:246
  197.1 18.3 %collective-permute-start.16 = (bf16[2,256,1152]{2,1,0:T(8,128)(2,1)S(1)}, bf16[2,256,1152]{2,1,0:T(8,128)(2,1)S(1)}, u32[]{:S(2)}, u32[]{:S(2)}) collective-permute-start(bf16[2,256,1152]{2,1,0:T(8,128)(2,1)S(1)} %dynamic-slice_bitcast_fusion.3), channel_id=1, source_target_pairs={{0,1},{1,0},{2,3},{3,2},{4,5},{5,4},{6,7},{7,6},{8,9},{9,8},{10,11... | collective-permute-start | bytes 3538952 | tf_op jit(solution)/shard_map/ppermute | solution.py:246
  202.8 67.4 %collective-permute-start.18 = (bf16[4,72,1024]{2,1,0:T(8,128)(2,1)}, bf16[4,72,1024]{2,1,0:T(8,128)(2,1)}, u32[]{:S(2)}, u32[]{:S(2)}) collective-permute-start(bf16[4,72,1024]{2,1,0:T(8,128)(2,1)} %bitcast.75.grad), channel_id=1, source_target_pairs={{4,0},{8,4},{12,8},{16,12},{20,16},{24,20},{28,24},{5,1},{9,5},{13... | collective-permute-start | bytes 1769480 | tf_op jit(solution)/shard_map/ppermute | solution.py:251
  204.1 69.9 %collective-permute-start.17 = (bf16[4,72,1024]{2,1,0:T(8,128)(2,1)}, bf16[4,72,1024]{2,1,0:T(8,128)(2,1)}, u32[]{:S(2)}, u32[]{:S(2)}) collective-permute-start(bf16[4,72,1024]{2,1,0:T(8,128)(2,1)} %bitcast.75.grad), channel_id=1, source_target_pairs={{0,4},{4,8},{8,12},{12,16},{16,20},{20,24},{24,28},{1,5},{5,9},{9,... | collective-permute-start | bytes 1769480 | tf_op jit(solution)/shard_map/ppermute | solution.py:251
  217.2 40.0 %collective-permute-start.20 = (f32[2,4,1,1024]{3,2,1,0:T(1,128)S(1)}, f32[2,4,1,1024]{3,2,1,0:T(1,128)S(1)}, u32[]{:S(2)}, u32[]{:S(2)}) collective-permute-start(f32[2,4,1,1024]{3,2,1,0:T(1,128)S(1)} %pad_maximum_fusion.9), channel_id=1, source_target_pairs={{4,0},{8,4},{12,8},{16,12},{20,16},{24,20},{28,24},{5,1},{9,5},{13... | collective-permute-start | bytes 98312 | tf_op jit(solution)/shard_map/ppermute | solution.py:251
  257.1 12.6 %collective-permute-start.19 = (f32[2,4,1,1024]{3,2,1,0:T(1,128)S(1)}, f32[2,4,1,1024]{3,2,1,0:T(1,128)S(1)}, u32[]{:S(2)}, u32[]{:S(2)}) collective-permute-start(f32[2,4,1,1024]{3,2,1,0:T(1,128)S(1)} %pad_maximum_fusion.9), channel_id=1, source_target_pairs={{0,4},{4,8},{8,12},{12,16},{16,20},{20,24},{24,28},{1,5},{5,9},{9,... | collective-permute-start | bytes 98312 | tf_op jit(solution)/shard_map/ppermute | solution.py:251
  269.7 13.7 %collective-permute-start.21 = (bf16[256,1152]{1,0:T(8,128)(2,1)S(1)}, bf16[256,1152]{1,0:T(8,128)(2,1)S(1)}, u32[]{:S(2)}, u32[]{:S(2)}) collective-permute-start(bf16[256,1152]{1,0:T(8,128)(2,1)S(1)} %fusion.110), channel_id=1, source_target_pairs={{0,2},{1,3},{2,0},{3,1},{4,6},{5,7},{6,4},{7,5},{8,10},{9,11},{10,... | collective-permute-start | bytes 1769480 | tf_op jit(solution)/shard_map/ppermute | solution.py:246
  270.3 77.4 %collective-permute-start.34 = (bf16[2,2,144,576]{3,2,1,0:T(8,128)(2,1)}, bf16[2,2,144,576]{3,2,1,0:T(8,128)(2,1)}, u32[]{:S(2)}, u32[]{:S(2)}) collective-permute-start(bf16[2,2,144,576]{3,2,1,0:T(8,128)(2,1)} %fusion.98), channel_id=1, source_target_pairs={{0,4},{4,0},{8,12},{12,8},{16,20},{20,16},{24,28},{28,24},{1,5},{5... | collective-permute-start | bytes 1990664 | tf_op jit(solution)/shard_map/ppermute | solution.py:246
  296.1 26.0 %collective-permute-start.22 = (bf16[2,2,144,576]{3,2,1,0:T(8,128)(2,1)}, bf16[2,2,144,576]{3,2,1,0:T(8,128)(2,1)}, u32[]{:S(2)}, u32[]{:S(2)}) collective-permute-start(bf16[2,2,144,576]{3,2,1,0:T(8,128)(2,1)} %fusion.104), channel_id=1, source_target_pairs={{0,4},{4,0},{8,12},{12,8},{16,20},{20,16},{24,28},{28,24},{1,5},{5... | collective-permute-start | bytes 1990664 | tf_op jit(solution)/shard_map/ppermute | solution.py:246
  318.1 14.8 %collective-permute-start.26 = (f32[17,1728]{1,0:T(8,128)}, f32[17,1728]{1,0:T(8,128)}, u32[]{:S(2)}, u32[]{:S(2)}) collective-permute-start(f32[17,1728]{1,0:T(8,128)} %get-tuple-element.157), channel_id=1, source_target_pairs={{0,3},{1,2},{2,1},{3,0},{4,7},{5,6},{6,5},{7,4},{8,11},{9,10},{10,... | collective-permute-start | bytes 352520 | tf_op jit(solution)/shard_map/ppermute | solution.py:246
  318.1 17.5 %collective-permute-start.24 = (f32[17,1728]{1,0:T(8,128)}, f32[17,1728]{1,0:T(8,128)}, u32[]{:S(2)}, u32[]{:S(2)}) collective-permute-start(f32[17,1728]{1,0:T(8,128)} %get-tuple-element.158), channel_id=1, source_target_pairs={{0,1},{1,0},{2,3},{3,2},{4,5},{5,4},{6,7},{7,6},{8,9},{9,8},{10,11... | collective-permute-start | bytes 352520 | tf_op jit(solution)/shard_map/ppermute | solution.py:246
  319.3 16.6 %collective-permute-start.25 = (f32[17,1728]{1,0:T(8,128)}, f32[17,1728]{1,0:T(8,128)}, u32[]{:S(2)}, u32[]{:S(2)}) collective-permute-start(f32[17,1728]{1,0:T(8,128)} %get-tuple-element.159), channel_id=1, source_target_pairs={{0,2},{1,3},{2,0},{3,1},{4,6},{5,7},{6,4},{7,5},{8,10},{9,11},{10,... | collective-permute-start | bytes 352520 | tf_op jit(solution)/shard_map/ppermute | solution.py:246
  332.8 9.4 %collective-permute-start.23 = (bf16[2,288,1024]{2,1,0:T(8,128)(2,1)}, bf16[2,288,1024]{2,1,0:T(8,128)(2,1)}, u32[]{:S(2)}, u32[]{:S(2)}) collective-permute-start(bf16[2,288,1024]{2,1,0:T(8,128)(2,1)} %dynamic-slice_bitcast_fusion.2), channel_id=1, source_target_pairs={{0,1},{1,0},{2,3},{3,2},{4,5},{5,4},{6,7},{7,6},{8,9},{9,8},{10,11... | collective-permute-start | bytes 3538952 | tf_op jit(solution)/shard_map/ppermute | solution.py:246
  332.9 86.8 %collective-permute-start.43 = (bf16[2,144,1152]{2,1,0:T(8,128)(2,1)}, bf16[2,144,1152]{2,1,0:T(8,128)(2,1)}, u32[]{:S(2)}, u32[]{:S(2)}) collective-permute-start(bf16[2,144,1152]{2,1,0:T(8,128)(2,1)} %dynamic-slice_bitcast_fusion.6), channel_id=1, source_target_pairs={{0,16},{4,20},{8,24},{12,28},{16,0},{20,4},{24,8},{28,12},{1,17},{... | collective-permute-start | bytes 1990664 | tf_op jit(solution)/shard_map/ppermute | solution.py:246
  335.6 84.1 %collective-permute-start.40 = (bf16[2,144,1152]{2,1,0:T(8,128)(2,1)}, bf16[2,144,1152]{2,1,0:T(8,128)(2,1)}, u32[]{:S(2)}, u32[]{:S(2)}) collective-permute-start(bf16[2,144,1152]{2,1,0:T(8,128)(2,1)} %dynamic-slice_bitcast_fusion.7), channel_id=1, source_target_pairs={{0,16},{4,20},{8,24},{12,28},{16,0},{20,4},{24,8},{28,12},{1,17},{... | collective-permute-start | bytes 1990664 | tf_op jit(solution)/shard_map/ppermute | solution.py:246
  337.8 8.9 %collective-permute-start.27 = (f32[20,1728]{1,0:T(8,128)S(1)}, f32[20,1728]{1,0:T(8,128)S(1)}, u32[]{:S(2)}, u32[]{:S(2)}) collective-permute-start(f32[20,1728]{1,0:T(8,128)S(1)} %pad_maximum_fusion.8), channel_id=1, source_target_pairs={{0,4},{4,0},{8,12},{12,8},{16,20},{20,16},{24,28},{28,24},{1,5},{5... | collective-permute-start | bytes 414728 | tf_op jit(solution)/shard_map/ppermute | solution.py:246
  345.5 71.8 %collective-permute-start.28 = (bf16[288,1024]{1,0:T(8,128)(2,1)S(1)}, bf16[288,1024]{1,0:T(8,128)(2,1)}, u32[]{:S(2)}, u32[]{:S(2)}) collective-permute-start(bf16[288,1024]{1,0:T(8,128)(2,1)S(1)} %fusion.111), channel_id=1, source_target_pairs={{0,2},{1,3},{2,0},{3,1},{4,6},{5,7},{6,4},{7,5},{8,10},{9,11},{10,... | collective-permute-start | bytes 1769480 | tf_op jit(solution)/shard_map/ppermute | solution.py:246
  346.7 22.2 %collective-permute-start.29 = (f32[20,1728]{1,0:T(8,128)S(1)}, f32[20,1728]{1,0:T(8,128)S(1)}, u32[]{:S(2)}, u32[]{:S(2)}) collective-permute-start(f32[20,1728]{1,0:T(8,128)S(1)} %fusion.198), channel_id=1, source_target_pairs={{0,8},{4,12},{8,0},{12,4},{16,24},{20,28},{24,16},{28,20},{1,9},{5... | collective-permute-start | bytes 414728 | tf_op jit(solution)/shard_map/ppermute | solution.py:246
  347.7 76.1 %collective-permute-start.37 = (bf16[2,144,576]{2,1,0:T(8,128)(2,1)}, bf16[2,144,576]{2,1,0:T(8,128)(2,1)S(1)}, u32[]{:S(2)}, u32[]{:S(2)}) collective-permute-start(bf16[2,144,576]{2,1,0:T(8,128)(2,1)} %dynamic-slice_bitcast_fusion.9), channel_id=1, source_target_pairs={{0,16},{4,20},{8,24},{12,28},{16,0},{20,4},{24,8},{28,12},{1,17},{... | collective-permute-start | bytes 995336 | tf_op jit(solution)/shard_map/ppermute | solution.py:246
  369.0 48.2 %collective-permute-start.30 = (f32[20,1728]{1,0:T(8,128)S(1)}, f32[20,1728]{1,0:T(8,128)S(1)}, u32[]{:S(2)}, u32[]{:S(2)}) collective-permute-start(f32[20,1728]{1,0:T(8,128)S(1)} %add.764), channel_id=1, source_target_pairs={{0,16},{4,20},{8,24},{12,28},{16,0},{20,4},{24,8},{28,12},{1,17},{... | collective-permute-start | bytes 414728 | tf_op jit(solution)/shard_map/ppermute | solution.py:246
  417.3 18.0 %collective-permute-start.35 = (bf16[2,144,576]{2,1,0:T(8,128)(2,1)S(1)}, bf16[2,144,576]{2,1,0:T(8,128)(2,1)S(1)}, u32[]{:S(2)}, u32[]{:S(2)}) collective-permute-start(bf16[2,144,576]{2,1,0:T(8,128)(2,1)S(1)} %dynamic-slice_bitcast_fusion.8), channel_id=1, source_target_pairs={{0,16},{4,20},{8,24},{12,28},{16,0},{20,4},{24,8},{28,12},{1,17},{... | collective-permute-start | bytes 995336 | tf_op jit(solution)/shard_map/ppermute | solution.py:246
  439.0 5.5 %collective-permute-start.31 = (f32[2,288]{1,0:T(2,128)S(1)}, f32[2,288]{1,0:T(2,128)S(1)}, u32[]{:S(2)}, u32[]{:S(2)}) collective-permute-start(f32[2,288]{1,0:T(2,128)S(1)} %bitcast.505), channel_id=1, source_target_pairs={{0,1},{1,0},{2,3},{3,2},{4,5},{5,4},{6,7},{7,6},{8,9},{9,8},{10,11... | collective-permute-start | bytes 6920 | tf_op jit(solution)/shard_map/ppermute | solution.py:246
  439.1 5.6 %collective-permute-start.32 = (f32[2,288]{1,0:T(2,128)S(1)}, f32[2,288]{1,0:T(2,128)S(1)}, u32[]{:S(2)}, u32[]{:S(2)}) collective-permute-start(f32[2,288]{1,0:T(2,128)S(1)} %bitcast.504), channel_id=1, source_target_pairs={{0,2},{1,3},{2,0},{3,1},{4,6},{5,7},{6,4},{7,5},{8,10},{9,11},{10,... | collective-permute-start | bytes 6920 | tf_op jit(solution)/shard_map/ppermute | solution.py:246
  440.3 6.4 %collective-permute-start.33 = (f32[2,288]{1,0:T(2,128)S(1)}, f32[2,288]{1,0:T(2,128)S(1)}, u32[]{:S(2)}, u32[]{:S(2)}) collective-permute-start(f32[2,288]{1,0:T(2,128)S(1)} %bitcast.503), channel_id=1, source_target_pairs={{0,3},{1,2},{2,1},{3,0},{4,7},{5,6},{6,5},{7,4},{8,11},{9,10},{10,... | collective-permute-start | bytes 6920 | tf_op jit(solution)/shard_map/ppermute | solution.py:246
  441.0 7.5 %collective-permute-start.38 = (bf16[144,576]{1,0:T(8,128)(2,1)S(1)}, bf16[144,576]{1,0:T(8,128)(2,1)S(1)}, u32[]{:S(2)}, u32[]{:S(2)}) collective-permute-start(bf16[144,576]{1,0:T(8,128)(2,1)S(1)} %dynamic-slice_bitcast_fusion.12), channel_id=1, source_target_pairs={{0,8},{4,12},{8,0},{12,4},{16,24},{20,28},{24,16},{28,20},{1,9},{5... | collective-permute-start | bytes 497672 | tf_op jit(solution)/shard_map/ppermute | solution.py:246
  441.1 11.4 %collective-permute-start.36 = (bf16[144,576]{1,0:T(8,128)(2,1)S(1)}, bf16[144,576]{1,0:T(8,128)(2,1)S(1)}, u32[]{:S(2)}, u32[]{:S(2)}) collective-permute-start(bf16[144,576]{1,0:T(8,128)(2,1)S(1)} %dynamic-slice_bitcast_fusion.13), channel_id=1, source_target_pairs={{0,8},{4,12},{8,0},{12,4},{16,24},{20,28},{24,16},{28,20},{1,9},{5... | collective-permute-start | bytes 497672 | tf_op jit(solution)/shard_map/ppermute | solution.py:246
  444.6 15.0 %collective-permute-start.44 = (bf16[144,1152]{1,0:T(8,128)(2,1)S(1)}, bf16[144,1152]{1,0:T(8,128)(2,1)S(1)}, u32[]{:S(2)}, u32[]{:S(2)}) collective-permute-start(bf16[144,1152]{1,0:T(8,128)(2,1)S(1)} %dynamic-slice_bitcast_fusion.10), channel_id=1, source_target_pairs={{0,8},{4,12},{8,0},{12,4},{16,24},{20,28},{24,16},{28,20},{1,9},{5... | collective-permute-start | bytes 995336 | tf_op jit(solution)/shard_map/ppermute | solution.py:246
  444.7 21.4 %collective-permute-start.41 = (bf16[144,1152]{1,0:T(8,128)(2,1)S(1)}, bf16[144,1152]{1,0:T(8,128)(2,1)S(1)}, u32[]{:S(2)}, u32[]{:S(2)}) collective-permute-start(bf16[144,1152]{1,0:T(8,128)(2,1)S(1)} %dynamic-slice_bitcast_fusion.11), channel_id=1, source_target_pairs={{0,8},{4,12},{8,0},{12,4},{16,24},{20,28},{24,16},{28,20},{1,9},{5... | collective-permute-start | bytes 995336 | tf_op jit(solution)/shard_map/ppermute | solution.py:246
  (95 other events, 927.5 us)

commit v3 on v1

--- a/solution.py
+++ b/solution.py
@@ -318,17 +318,15 @@
         come = after((yield sent), come)
         held = kept.astype(F32) + come.astype(F32)
         left.remove(bit)
+        if left:
+            held = held.astype(BF16)
     return held
 
 
-def scatter_data(partials):
-    joined = jnp.concatenate([partial.astype(BF16) for partial in partials], axis=1)
-    found = lax.psum_scatter(joined, "dp", scatter_dimension=0, tiled=True)
-    cuts, at = [], 0
-    for partial in partials[:-1]:
-        at += partial.shape[1]
-        cuts.append(at)
-    return joined, lambda anchor: jnp.split(after(anchor, found).astype(F32), cuts, axis=1)
+def scatter_whole(partial):
+    low = partial.astype(BF16)
+    found = lax.psum_scatter(low, "dp", scatter_dimension=0, tiled=True)
+    return low, lambda anchor: after(anchor, found).astype(F32)
 
 
 def finish(steps, anchor=None):
@@ -515,8 +513,9 @@
     grad_pre = after(next(entry_steps), grad_pre)
     grad_out_mine = mine(out_grad).astype(F32)
     grad_up_w = jnp.einsum("td,tf->df", entry_m, grad_pre, preferred_element_type=F32)
-    wide_sent, wide_sums = scatter_data([grad_down_w, grad_up_w])
-    grad_entry_m = finish(entry_steps, wide_sent)
+    down_sent, down_sum = scatter_whole(grad_down_w)
+    up_sent, up_sum = scatter_whole(grad_up_w)
+    grad_entry_m = finish(entry_steps, (down_sent, up_sent))
     grad_down_b = jnp.sum(grad_branch_m.astype(F32), axis=0)
     grad_up_b = jnp.sum(grad_pre.astype(F32), axis=0)
     grad_middle = grad_out_mine + norm_back_m(grad_entry_m * (1.0 + scale_m))[0]
@@ -579,10 +578,9 @@
     )
     early_steps = scatter_data_steps(jnp.concatenate([grad_out_w, grad_q_w], axis=1))
     next(early_steps)
-    early_sent = early_steps.send(grad_keys)
     late_steps = scatter_data_steps(jnp.concatenate([grad_k_w, grad_v_w], axis=1))
     late_sent = next(late_steps)
-    grad_proj = after((late_sent, early_sent), *grad_proj)
+    grad_proj = after(late_sent, *grad_proj)
     grad_in_b = jnp.stack([jnp.sum(grad_proj[c].astype(F32), axis=1) for c in (0, 2)])
     grad_entry = lax.dot_general(
         in_weight.reshape(width, 3 * local_width),
@@ -637,8 +635,9 @@
             for value in (grad_in_b.reshape(-1), grad_up_b, grad_down_b)
         ]
     )
-    late_sent = late_steps.send(tokens_sent)
-    tokens_sent = tokens_steps.send(late_sent)
+    early_sent = early_steps.send(input_part)
+    late_sent = late_steps.send(input_part)
+    tokens_sent = tokens_steps.send((early_sent, late_sent))
     for place, bit in enumerate(bits_of("dp")):
         come = swap(small, "dp", bit)
         if place == 0:
@@ -668,8 +667,8 @@
         )
 
     grad_tokens = finish(tokens_steps, grad_mod_w).T
-    sum_down_w, sum_up_w = wide_sums(grad_mod_w)
-    early = finish(early_steps, tokens_sent)
+    sum_down_w, sum_up_w = down_sum(grad_mod_w), up_sum(grad_mod_w)
+    early = finish(early_steps, small)
     late = finish(late_steps, small)
     sum_out_w = early[:, :local_width]
     sum_in_w = jnp.stack(

time: 423 us -> 420 us (level)
  local copies, waits for them, and re-layouts: 63.1 us -> 41.2 us
  waiting for transfers between devices: 98.1 us -> 113 us
  other arithmetic: 64.9 us -> 73.9 us
  matrix products: 74 us -> 69.7 us
    ppermute x33, waiting for transfers between devices: 92.8 us -> 106 us  [swap(): lax.ppermute(value, axis, [(i, i ^ bit) for i in range(lax.axis_size(axis...]
    unnamed x224 -> x193, local copies, waits for them, and re-layouts: 27.2 us -> 15.2 us
    convert_element_type x0 -> x6, other arithmetic: none -> 7.68 us  [the longest x4 3.97 us: scatter_data_steps(): held = held.astype(BF16)]
    dot_general x2, matrix products: 5.5 us -> 1.2 us  [onehot_sum(): first = jnp.einsum(form, select, upper, preferred_element_type=F32)]
  transfers between devices with their start and end apart: 40 -> 41, of which waited for: 17 -> 13; matrix products, arithmetic and copies ran while one was open for 33% -> 33% of each run, Pallas kernels for 8% -> 8%
where the time goes in v3:
time: 420 us; the launch traced here: 414 us
  waiting for transfers between devices  113 us (27%)
  other arithmetic  73.9 us (18%)
  matrix products  69.7 us (17%)
  starting transfers between devices  61.9 us (15%)
  local copies, waits for them, and re-layouts  41.2 us (10%)
  Pallas kernels  38.3 us (9%)
  between operations  16.6 us (4%)
    ppermute x33, waiting for transfers between devices, swap(): lax.ppermute(value, axis, [(i, i ^ bit) for i in range(lax.axis_size(axis...  106 us
    ppermute x33, starting transfers between devices, swap(): lax.ppermute(value, axis, [(i, i ^ bit) for i in range(lax.axis_size(axis...  38.6 us
    ppermute x6, starting transfers between devices, shift(): lax.ppermute(value, axis, [(i, i + distance) for i in devices if i + dist...  23 us
    pallas_call x1, Pallas kernels, attend_back(): pl.pallas_call(functools.partial(backward_kernel, bases, heads), out_shap...  16.8 us
    unnamed x193, local copies, waits for them, and re-layouts  15.2 us
    pallas_call x2, Pallas kernels, attend(): pl.pallas_call(functools.partial(forward_kernel, bases, heads, last), out...  14.6 us
    select_n x15, other arithmetic, in_order(): jnp.where(upper, jnp.stack([other, mine], axis=dim), jnp.stack([mine, oth...  11.8 us
    dot_general x3, matrix products, project(): jnp.einsum('dcf,td->cft', in_weight, entry, preferred_element_type=F32)  9.51 us
  transfers between devices with their start and end apart: 41, of which 13 were waited for; matrix products, arithmetic and copies ran while one was open for 33% of the time, Pallas kernels for 8%

profile of v3, /device:TPU:0, one launch (start us, length us, event | category | flops | bytes accessed | tf_op | source)
XLA Modules:
  0.0 414.1 jit_solution(1421385420902358689)
XLA Ops:
  7.2 2.1 constant_dynamic-slice_fusion.12
  9.3 5.7 %collective-permute-start.2 = (bf16[256,1152]{1,0:T(8,128)(2,1)}, bf16[256,1152]{1,0:T(8,128)(2,1)}, u32[]{:S(2)}, u32[]{:S(2)}) collective-permute-start(bf16[256,1152]{1,0:T(8,128)(2,1)} %constant_dynamic-slice_fusion.12), channel_id=1, source_target_pairs={{0,4},{4,8},{8,12},{12,16},{16,20},{20,24},{24,28},{1,5},{5,9},{9,... | collective-permute-start | bytes 1769480 | tf_op jit(solution)/shard_map/ppermute | solution.py:251
  17.0 3.3 fusion.60
  21.9 2.2 convert_reduce_fusion.2
  31.0 2.5 fusion.61
  33.7 6.0 %collective-permute-done.2 = bf16[256,1152]{1,0:T(8,128)(2,1)} collective-permute-done((bf16[256,1152]{1,0:T(8,128)(2,1)}, bf16[256,1152]{1,0:T(8,128)(2,1)}, u32[]{:S(2)}, u32[]{:S(2)}) %collective-permute-start.2) | collective-permute-done | bytes 589856 | tf_op jit(solution)/shard_map/ppermute | solution.py:251
  41.4 9.1 %shard_map.237 = (f32[4,72,1024]{2,1,0:T(8,128)S(1)}, f32[4,1,1024]{2,1,0:T(1,128)S(1)}, f32[4,1,1024]{2,1,0:T(1,128)S(1)}) custom-call(s32[1,2,4]{2,1,0:T(2,128)S(1)} %add_bitcast_fusion.2.bounds, s32[2,1024]{1,0:T(2,128)S(1)} %pad_add_fusion.span, bf16[4,72,1024]{2,1,0:T(8,128)(2,1)S(1)} %bitcast.387, f32[4,72,1024]{2,1,0:T(8,128)S(1)} %broadcast_in_dim.212.mixed_in, ...), custom_call_target="tpu_custom_call" | custom-call | flops 19327352832 | bytes 25165824 | tf_op jit(solution)/shard_map/pallas_call | solution.py:89
  51.1 5.1 %collective-permute-done.3 = bf16[256,1152]{1,0:T(8,128)(2,1)S(1)} collective-permute-done((bf16[256,1152]{1,0:T(8,128)(2,1)}, bf16[256,1152]{1,0:T(8,128)(2,1)S(1)}, u32[]{:S(2)}, u32[]{:S(2)}) %collective-permute-start.3) | collective-permute-done | bytes 589856 | tf_op jit(solution)/shard_map/ppermute | solution.py:246
  60.8 6.0 %collective-permute-done.6 = bf16[256,1152]{1,0:T(8,128)(2,1)S(1)} collective-permute-done((bf16[256,1152]{1,0:T(8,128)(2,1)}, bf16[256,1152]{1,0:T(8,128)(2,1)S(1)}, u32[]{:S(2)}, u32[]{:S(2)}) %collective-permute-start.6) | collective-permute-done | bytes 589856 | tf_op jit(solution)/shard_map/ppermute | solution.py:246
  74.5 3.4 fusion.62
  78.8 3.6 fusion.63
  83.5 5.5 %shard_map.238 = (bf16[4,72,1024]{2,1,0:T(8,128)(2,1)S(1)}, f32[4,1,1024]{2,1,0:T(1,128)S(1)}, f32[4,1,1024]{2,1,0:T(1,128)}) custom-call(s32[2,2,4]{2,1,0:T(2,128)S(1)} %pad_add_fusion.4.bounds, s32[2,1024]{1,0:T(2,128)S(1)} %pad_add_fusion.span, bf16[4,72,1024]{2,1,0:T(8,128)(2,1)S(1)} %bitcast.388, f32[4,72,1024]{2,1,0:T(8,128)S(1)} %get-tuple-element.46.mixed_in, ...), custom_call_target="tpu_custom_call" | custom-call | flops 19327352832 | bytes 25165824 | tf_op jit(solution)/shard_map/pallas_call | solution.py:89
  103.5 12.9 %collective-permute-done.9 = bf16[256,1152]{1,0:T(8,128)(2,1)} collective-permute-done((bf16[256,1152]{1,0:T(8,128)(2,1)}, bf16[256,1152]{1,0:T(8,128)(2,1)}, u32[]{:S(2)}, u32[]{:S(2)}) %collective-permute-start.9) | collective-permute-done | bytes 589856 | tf_op jit(solution)/shard_map/ppermute | solution.py:246
  121.9 11.9 %collective-permute-done.10 = bf16[256,1152]{1,0:T(8,128)(2,1)S(1)} collective-permute-done((bf16[256,1152]{1,0:T(8,128)(2,1)S(1)}, bf16[256,1152]{1,0:T(8,128)(2,1)S(1)}, u32[]{:S(2)}, u32[]{:S(2)}) %collective-permute-start.10) | collective-permute-done | bytes 589856 | tf_op jit(solution)/shard_map/ppermute | solution.py:246
  135.8 3.5 fusion.165
  140.0 6.1 %fusion.34 = (bf16[1024,1152]{1,0:T(8,128)(2,1)S(1)}, bf16[1024,1152]{1,0:T(8,128)(2,1)S(1)}) fusion(f32[1024,1152]{1,0:T(8,128)S(1)} %fusion.165, f32[1152]{0:T(1024)S(1)} %convert_element_type.363, bf16[1024,1152]{1,0:T(8,128)(2,1)S(1)} %bitcast.439, bf16[1152,1152]{1,0:T(8,128)(2,1)S(1)} %copy-done), kind=kOutput, calls=%fused_computation.47 | convolution fusion | flops 2745040896 | bytes 14455296 | tf_op jit(solution)/shard_map/dot_general | solution.py:503
  146.1 3.8 convolution_convert_fusion.5
  152.4 4.8 %convolution_convert_fusion.1 = bf16[1152,1152]{1,0:T(8,128)(2,1)} fusion(bf16[1024,1152]{1,0:T(8,128)(2,1)S(1)} %get-tuple-element.160, bf16[1024,1152]{1,0:T(8,128)(2,1)S(1)} %get-tuple-element.53), kind=kOutput, calls=%fused_computation.4 | convolution fusion | flops 2719236096 | bytes 7372800 | tf_op jit(solution)/shard_map/td,tf->df/dot_general | solution.py:510
  159.0 6.5 %convolution_convert_fusion = bf16[1152,1152]{1,0:T(8,128)(2,1)} fusion(bf16[1024,1152]{1,0:T(8,128)(2,1)} %bitcast.440, bf16[1024,1152]{1,0:T(8,128)(2,1)S(1)} %copy-done.55), kind=kOutput, calls=%fused_computation.3 | convolution fusion | flops 2719236096 | bytes 7372800 | tf_op jit(solution)/shard_map/td,tf->df/dot_general | solution.py:515
  170.7 14.2 %collective-permute-done.13 = bf16[256,1152]{1,0:T(8,128)(2,1)} collective-permute-done((bf16[256,1152]{1,0:T(8,128)(2,1)S(1)}, bf16[256,1152]{1,0:T(8,128)(2,1)}, u32[]{:S(2)}, u32[]{:S(2)}) %collective-permute-start.13) | collective-permute-done | bytes 589856 | tf_op jit(solution)/shard_map/ppermute | solution.py:246
  184.9 2.8 multiply_multiply_fusion.2
  191.9 3.6 convert_reduce_fusion.7
  197.0 2.5 copy.77
  199.5 2.1 convert_reduce_fusion.4
  201.7 9.2 %collective-permute-done.14 = bf16[256,1152]{1,0:T(8,128)(2,1)} collective-permute-done((bf16[256,1152]{1,0:T(8,128)(2,1)}, bf16[256,1152]{1,0:T(8,128)(2,1)}, u32[]{:S(2)}, u32[]{:S(2)}) %collective-permute-start.14) | collective-permute-done | bytes 589856 | tf_op jit(solution)/shard_map/ppermute | solution.py:246
  212.9 5.5 %convolution_convert_fusion.4 = bf16[1024,1152]{1,0:T(8,128)(2,1)S(1)} fusion(bf16[1024,1152]{1,0:T(8,128)(2,1)S(1)} %copy-done.92, bf16[1152,1152]{1,0:T(8,128)(2,1)} %param.23), kind=kOutput, calls=%fused_computation.59 | convolution fusion | flops 2719088640 | bytes 7372800 | tf_op jit(solution)/shard_map/tf,df->td/dot_general | solution.py:530
  227.0 7.0 %collective-permute-start.20 = (f32[2,4,1,1024]{3,2,1,0:T(1,128)S(1)}, f32[2,4,1,1024]{3,2,1,0:T(1,128)S(1)}, u32[]{:S(2)}, u32[]{:S(2)}) collective-permute-start(f32[2,4,1,1024]{3,2,1,0:T(1,128)S(1)} %pad_maximum_fusion.9), channel_id=1, source_target_pairs={{0,4},{4,8},{8,12},{12,16},{16,20},{20,24},{24,28},{1,5},{5,9},{9,... | collective-permute-start | bytes 98312 | tf_op jit(solution)/shard_map/ppermute | solution.py:251
  235.3 6.5 %collective-permute-start.18 = (bf16[4,72,1024]{2,1,0:T(8,128)(2,1)}, bf16[4,72,1024]{2,1,0:T(8,128)(2,1)}, u32[]{:S(2)}, u32[]{:S(2)}) collective-permute-start(bf16[4,72,1024]{2,1,0:T(8,128)(2,1)} %bitcast.71.grad), channel_id=1, source_target_pairs={{0,4},{4,8},{8,12},{12,16},{16,20},{20,24},{24,28},{1,5},{5,9},{9,... | collective-permute-start | bytes 1769480 | tf_op jit(solution)/shard_map/ppermute | solution.py:251
  244.6 4.4 %copy.80 = bf16[1152,1024]{1,0:T(8,128)(2,1)} copy(bf16[1152,1024]{0,1:T(8,128)(2,1)} %bitcast.420) | data formatting | bytes 4718592 | tf_op jit(solution)/shard_map/dot_general | solution.py:559
  251.2 16.8 %shard_map.239 = (bf16[4,72,1024]{2,1,0:T(8,128)(2,1)S(1)}, f32[4,72,1024]{2,1,0:T(8,128)S(1)}, f32[4,72,1024]{2,1,0:T(8,128)S(1)}) custom-call(s32[3,2,4]{2,1,0:T(2,128)S(1)} %pad_add_fusion.3.bounds, s32[2,1024]{1,0:T(2,128)S(1)} %pad_add_fusion.span, bf16[4,72,1024]{2,1,0:T(8,128)(2,1)S(1)} %bitcast.389, bf16[4,72,1024]{2,1,0:T(8,128)(2,1)} %bitcast.71.grad, ...), custom_call_target="tpu_custom_call" | custom-call | flops 19327352832 | bytes 25165824 | tf_op jit(solution)/shard_map/pallas_call | solution.py:171
  272.3 4.1 collective-permute-start.22
  276.5 3.0 convert_multiply_fusion
  281.2 6.8 %shard_map.240 = (bf16[4,72,1024]{2,1,0:T(8,128)(2,1)S(1)}, bf16[4,72,1024]{2,1,0:T(8,128)(2,1)S(1)}) custom-call(s32[2,2,4]{2,1,0:T(2,128)S(1)} %pad_add_fusion.4.bounds, bf16[4,72,1024]{2,1,0:T(8,128)(2,1)S(1)} %bitcast.386, bf16[4,72,1024]{2,1,0:T(8,128)(2,1)S(1)} %bitcast.383, f32[4,72,1024]{2,1,0:T(8,128)S(1)} %get-tuple-element.58.keys_in, ...), custom_call_target="tpu_custom_call" | custom-call | flops 19327352832 | bytes 25165824 | tf_op jit(solution)/shard_map/pallas_call | solution.py:234
  291.9 3.4 collective-permute-start.23
  295.5 2.9 convolution_bitcast_fusion
  300.3 3.0 fusion.11
  311.4 2.3 fusion.79
  313.7 4.2 %collective-permute-done.23 = bf16[2,2,144,576]{3,2,1,0:T(8,128)(2,1)} collective-permute-done((bf16[2,2,144,576]{3,2,1,0:T(8,128)(2,1)}, bf16[2,2,144,576]{3,2,1,0:T(8,128)(2,1)}, u32[]{:S(2)}, u32[]{:S(2)}) %collective-permute-start.23) | collective-permute-done | bytes 663584 | tf_op jit(solution)/shard_map/ppermute | solution.py:246
  317.9 2.8 fusion.90
  320.7 4.1 convert_element_type.388
  324.8 3.1 copy.79
  331.0 2.4 collective-permute-start.28
  337.9 3.8 collective-permute-start.29
  344.6 3.5 collective-permute-done.29
  351.4 32.0 %collective-permute-done.30 = f32[20,1728]{1,0:T(8,128)S(1)} collective-permute-done((f32[20,1728]{1,0:T(8,128)S(1)}, f32[20,1728]{1,0:T(8,128)S(1)}, u32[]{:S(2)}, u32[]{:S(2)}) %collective-permute-start.30) | collective-permute-done | bytes 138272 | tf_op jit(solution)/shard_map/ppermute | solution.py:246
  384.8 2.8 fusion.127
  398.4 4.3 %collective-permute-done.36 = bf16[144,576]{1,0:T(8,128)(2,1)S(1)} collective-permute-done((bf16[144,576]{1,0:T(8,128)(2,1)S(1)}, bf16[144,576]{1,0:T(8,128)(2,1)S(1)}, u32[]{:S(2)}, u32[]{:S(2)}) %collective-permute-start.36) | collective-permute-done | bytes 165920 | tf_op jit(solution)/shard_map/ppermute | solution.py:246
  404.5 2.3 fusion.89
  (428 shorter events, 128.1 us)
Async XLA Ops:
  7.2 132.8 %copy-start = (bf16[1152,1152]{1,0:T(8,128)(2,1)S(1)}, bf16[1152,1152]{1,0:T(8,128)(2,1)}, u32[]{:S(2)}) copy-start(bf16[1152,1152]{1,0:T(8,128)(2,1)} %param.21) | copy-start | bytes 7962628
  7.2 384.9 %reduce-scatter.5.cloned.1.call-start = ((), (), s32[]{:S(2)}) async-start(), calls=%async_computation.3 | async-start | bytes 2985984 | tf_op jit(solution)/shard_map/reduce_scatter | solution.py:328
  9.3 30.4 %collective-permute-start.2 = (bf16[256,1152]{1,0:T(8,128)(2,1)}, bf16[256,1152]{1,0:T(8,128)(2,1)}, u32[]{:S(2)}, u32[]{:S(2)}) collective-permute-start(bf16[256,1152]{1,0:T(8,128)(2,1)} %constant_dynamic-slice_fusion.12), channel_id=1, source_target_pairs={{0,4},{4,8},{8,12},{12,16},{16,20},{20,24},{24,28},{1,5},{5,9},{9,... | collective-permute-start | bytes 1769480 | tf_op jit(solution)/shard_map/ppermute | solution.py:251
  15.0 35.4 %collective-permute-start.5 = (bf16[256,1152]{1,0:T(8,128)(2,1)}, bf16[256,1152]{1,0:T(8,128)(2,1)}, u32[]{:S(2)}, u32[]{:S(2)}) collective-permute-start(bf16[256,1152]{1,0:T(8,128)(2,1)} %constant_dynamic-slice_fusion.12), channel_id=1, source_target_pairs={{4,0},{8,4},{12,8},{16,12},{20,16},{24,20},{28,24},{5,1},{9,5},{13... | collective-permute-start | bytes 1769480 | tf_op jit(solution)/shard_map/ppermute | solution.py:251
  20.3 5.3 %collective-permute-start = (bf16[1,16,1728]{2,1,0:T(8,128)(2,1)S(1)}, bf16[1,16,1728]{2,1,0:T(8,128)(2,1)S(1)}, u32[]{:S(2)}, u32[]{:S(2)}) collective-permute-start(bf16[1,16,1728]{2,1,0:T(8,128)(2,1)S(1)} %bitcast.448), channel_id=1, source_target_pairs={{0,2},{1,3},{2,0},{3,1},{4,6},{5,7},{6,4},{7,5},{8,10},{9,11},{10,... | collective-permute-start | bytes 165896 | tf_op jit(solution)/shard_map/ppermute | solution.py:246
  25.7 1.4 collective-permute-start.1
  33.7 49.7 %copy-start.4 = (bf16[1,288,1024]{2,1,0:T(8,128)(2,1)}, bf16[1,288,1024]{2,1,0:T(8,128)(2,1)S(1)}, u32[]{:S(2)}) copy-start(bf16[1,288,1024]{2,1,0:T(8,128)(2,1)S(1)} %get-tuple-element.130) | copy-start | bytes 1769476
  39.7 16.5 %collective-permute-start.3 = (bf16[256,1152]{1,0:T(8,128)(2,1)}, bf16[256,1152]{1,0:T(8,128)(2,1)S(1)}, u32[]{:S(2)}, u32[]{:S(2)}) collective-permute-start(bf16[256,1152]{1,0:T(8,128)(2,1)} %collective-permute-done.2), channel_id=1, source_target_pairs={{0,2},{1,3},{2,0},{3,1},{4,6},{5,7},{6,4},{7,5},{8,10},{9,11},{10,... | collective-permute-start | bytes 1769480 | tf_op jit(solution)/shard_map/ppermute | solution.py:246
  50.5 16.3 %collective-permute-start.6 = (bf16[256,1152]{1,0:T(8,128)(2,1)}, bf16[256,1152]{1,0:T(8,128)(2,1)S(1)}, u32[]{:S(2)}, u32[]{:S(2)}) collective-permute-start(bf16[256,1152]{1,0:T(8,128)(2,1)} %collective-permute-done.5), channel_id=1, source_target_pairs={{0,2},{1,3},{2,0},{3,1},{4,6},{5,7},{6,4},{7,5},{8,10},{9,11},{10,... | collective-permute-start | bytes 1769480 | tf_op jit(solution)/shard_map/ppermute | solution.py:246
  57.7 13.6 %collective-permute-start.4 = (bf16[2,256,1152]{2,1,0:T(8,128)(2,1)S(1)}, bf16[2,256,1152]{2,1,0:T(8,128)(2,1)S(1)}, u32[]{:S(2)}, u32[]{:S(2)}) collective-permute-start(bf16[2,256,1152]{2,1,0:T(8,128)(2,1)S(1)} %maximum_select_fusion.4), channel_id=1, source_target_pairs={{0,1},{1,0},{2,3},{3,2},{4,5},{5,4},{6,7},{7,6},{8,9},{9,8},{10,11... | collective-permute-start | bytes 3538952 | tf_op jit(solution)/shard_map/ppermute | solution.py:246
  68.2 4.6 %collective-permute-start.7 = (bf16[2,256,1152]{2,1,0:T(8,128)(2,1)S(1)}, bf16[2,256,1152]{2,1,0:T(8,128)(2,1)S(1)}, u32[]{:S(2)}, u32[]{:S(2)}) collective-permute-start(bf16[2,256,1152]{2,1,0:T(8,128)(2,1)S(1)} %maximum_select_fusion.6), channel_id=1, source_target_pairs={{0,1},{1,0},{2,3},{3,2},{4,5},{5,4},{6,7},{7,6},{8,9},{9,8},{10,11... | collective-permute-start | bytes 3538952 | tf_op jit(solution)/shard_map/ppermute | solution.py:246
  93.0 3.3 collective-permute-start.8
  100.5 15.9 %collective-permute-start.9 = (bf16[256,1152]{1,0:T(8,128)(2,1)}, bf16[256,1152]{1,0:T(8,128)(2,1)}, u32[]{:S(2)}, u32[]{:S(2)}) collective-permute-start(bf16[256,1152]{1,0:T(8,128)(2,1)} %fusion.105), channel_id=1, source_target_pairs={{0,2},{1,3},{2,0},{3,1},{4,6},{5,7},{6,4},{7,5},{8,10},{9,11},{10,... | collective-permute-start | bytes 1769480 | tf_op jit(solution)/shard_map/ppermute | solution.py:246
  103.5 31.7 %copy-start.25 = (f32[256,4608]{1,0:T(8,128)}, f32[256,4608]{1,0:T(8,128)S(1)}, u32[]{:S(2)}) copy-start(f32[256,4608]{1,0:T(8,128)S(1)} %convolution_convert_fusion.2) | copy-start | bytes 14155780
  119.1 14.8 %collective-permute-start.10 = (bf16[256,1152]{1,0:T(8,128)(2,1)S(1)}, bf16[256,1152]{1,0:T(8,128)(2,1)S(1)}, u32[]{:S(2)}, u32[]{:S(2)}) collective-permute-start(bf16[256,1152]{1,0:T(8,128)(2,1)S(1)} %fusion.86), channel_id=1, source_target_pairs={{0,2},{1,3},{2,0},{3,1},{4,6},{5,7},{6,4},{7,5},{8,10},{9,11},{10,... | collective-permute-start | bytes 1769480 | tf_op jit(solution)/shard_map/ppermute | solution.py:246
  134.1 5.5 %collective-permute-start.11 = (bf16[2,256,1152]{2,1,0:T(8,128)(2,1)S(1)}, bf16[2,256,1152]{2,1,0:T(8,128)(2,1)S(1)}, u32[]{:S(2)}, u32[]{:S(2)}) collective-permute-start(bf16[2,256,1152]{2,1,0:T(8,128)(2,1)S(1)} %maximum_select_fusion.8), channel_id=1, source_target_pairs={{0,1},{1,0},{2,3},{3,2},{4,5},{5,4},{6,7},{7,6},{8,9},{9,8},{10,11... | collective-permute-start | bytes 3538952 | tf_op jit(solution)/shard_map/ppermute | solution.py:246
  152.4 13.1 %collective-permute-start.12 = (bf16[2,256,1152]{2,1,0:T(8,128)(2,1)}, bf16[2,256,1152]{2,1,0:T(8,128)(2,1)}, u32[]{:S(2)}, u32[]{:S(2)}) collective-permute-start(bf16[2,256,1152]{2,1,0:T(8,128)(2,1)} %dynamic-slice_bitcast_fusion.2), channel_id=1, source_target_pairs={{0,1},{1,0},{2,3},{3,2},{4,5},{5,4},{6,7},{7,6},{8,9},{9,8},{10,11... | collective-permute-start | bytes 3538952 | tf_op jit(solution)/shard_map/ppermute | solution.py:246
  157.3 234.8 %reduce-scatter.3.cloned.1.call-start = ((), (), s32[]{:S(2)}) async-start(), calls=%async_computation.2 | async-start | bytes 2985984 | tf_op jit(solution)/shard_map/reduce_scatter | solution.py:328
  165.5 19.5 %copy-start.23 = (f32[256,1152]{1,0:T(8,128)S(1)}, f32[256,1152]{1,0:T(8,128)}, u32[]{:S(2)}) copy-start(f32[256,1152]{1,0:T(8,128)} %copy-done.22) | copy-start | bytes 3538948
  169.0 16.0 %collective-permute-start.13 = (bf16[256,1152]{1,0:T(8,128)(2,1)S(1)}, bf16[256,1152]{1,0:T(8,128)(2,1)}, u32[]{:S(2)}, u32[]{:S(2)}) collective-permute-start(bf16[256,1152]{1,0:T(8,128)(2,1)S(1)} %fusion.106), channel_id=1, source_target_pairs={{0,2},{1,3},{2,0},{3,1},{4,6},{5,7},{6,4},{7,5},{8,10},{9,11},{10,... | collective-permute-start | bytes 1769480 | tf_op jit(solution)/shard_map/ppermute | solution.py:246
  195.4 15.4 %collective-permute-start.14 = (bf16[256,1152]{1,0:T(8,128)(2,1)}, bf16[256,1152]{1,0:T(8,128)(2,1)}, u32[]{:S(2)}, u32[]{:S(2)}) collective-permute-start(bf16[256,1152]{1,0:T(8,128)(2,1)} %get-tuple-element.108), channel_id=1, source_target_pairs={{0,2},{1,3},{2,0},{3,1},{4,6},{5,7},{6,4},{7,5},{8,10},{9,11},{10,... | collective-permute-start | bytes 1769480 | tf_op jit(solution)/shard_map/ppermute | solution.py:246
  212.8 8.2 %collective-permute-start.15 = (bf16[2,256,1152]{2,1,0:T(8,128)(2,1)S(1)}, bf16[2,256,1152]{2,1,0:T(8,128)(2,1)S(1)}, u32[]{:S(2)}, u32[]{:S(2)}) collective-permute-start(bf16[2,256,1152]{2,1,0:T(8,128)(2,1)S(1)} %maximum_select_fusion.10), channel_id=1, source_target_pairs={{0,1},{1,0},{2,3},{3,2},{4,5},{5,4},{6,7},{7,6},{8,9},{9,8},{10,11... | collective-permute-start | bytes 3538952 | tf_op jit(solution)/shard_map/ppermute | solution.py:246
  218.5 23.3 %collective-permute-start.16 = (bf16[2,256,1152]{2,1,0:T(8,128)(2,1)S(1)}, bf16[2,256,1152]{2,1,0:T(8,128)(2,1)S(1)}, u32[]{:S(2)}, u32[]{:S(2)}) collective-permute-start(bf16[2,256,1152]{2,1,0:T(8,128)(2,1)S(1)} %dynamic-slice_bitcast_fusion.1), channel_id=1, source_target_pairs={{0,1},{1,0},{2,3},{3,2},{4,5},{5,4},{6,7},{7,6},{8,9},{9,8},{10,11... | collective-permute-start | bytes 3538952 | tf_op jit(solution)/shard_map/ppermute | solution.py:246
  225.7 46.7 %collective-permute-start.21 = (f32[2,4,1,1024]{3,2,1,0:T(1,128)S(1)}, f32[2,4,1,1024]{3,2,1,0:T(1,128)S(1)}, u32[]{:S(2)}, u32[]{:S(2)}) collective-permute-start(f32[2,4,1,1024]{3,2,1,0:T(1,128)S(1)} %pad_maximum_fusion.9), channel_id=1, source_target_pairs={{4,0},{8,4},{12,8},{16,12},{20,16},{24,20},{28,24},{5,1},{9,5},{13... | collective-permute-start | bytes 98312 | tf_op jit(solution)/shard_map/ppermute | solution.py:251
  227.0 49.4 %collective-permute-start.20 = (f32[2,4,1,1024]{3,2,1,0:T(1,128)S(1)}, f32[2,4,1,1024]{3,2,1,0:T(1,128)S(1)}, u32[]{:S(2)}, u32[]{:S(2)}) collective-permute-start(f32[2,4,1,1024]{3,2,1,0:T(1,128)S(1)} %pad_maximum_fusion.9), channel_id=1, source_target_pairs={{0,4},{4,8},{8,12},{12,16},{16,20},{20,24},{24,28},{1,5},{5,9},{9,... | collective-permute-start | bytes 98312 | tf_op jit(solution)/shard_map/ppermute | solution.py:251
  234.0 46.4 %collective-permute-start.19 = (bf16[4,72,1024]{2,1,0:T(8,128)(2,1)}, bf16[4,72,1024]{2,1,0:T(8,128)(2,1)}, u32[]{:S(2)}, u32[]{:S(2)}) collective-permute-start(bf16[4,72,1024]{2,1,0:T(8,128)(2,1)} %bitcast.71.grad), channel_id=1, source_target_pairs={{4,0},{8,4},{12,8},{16,12},{20,16},{24,20},{28,24},{5,1},{9,5},{13... | collective-permute-start | bytes 1769480 | tf_op jit(solution)/shard_map/ppermute | solution.py:251
  235.3 45.1 %collective-permute-start.18 = (bf16[4,72,1024]{2,1,0:T(8,128)(2,1)}, bf16[4,72,1024]{2,1,0:T(8,128)(2,1)}, u32[]{:S(2)}, u32[]{:S(2)}) collective-permute-start(bf16[4,72,1024]{2,1,0:T(8,128)(2,1)} %bitcast.71.grad), channel_id=1, source_target_pairs={{0,4},{4,8},{8,12},{12,16},{16,20},{20,24},{24,28},{1,5},{5,9},{9,... | collective-permute-start | bytes 1769480 | tf_op jit(solution)/shard_map/ppermute | solution.py:251
  243.1 33.4 %collective-permute-start.17 = (bf16[256,1152]{1,0:T(8,128)(2,1)}, bf16[256,1152]{1,0:T(8,128)(2,1)}, u32[]{:S(2)}, u32[]{:S(2)}) collective-permute-start(bf16[256,1152]{1,0:T(8,128)(2,1)} %fusion.107), channel_id=1, source_target_pairs={{0,2},{1,3},{2,0},{3,1},{4,6},{5,7},{6,4},{7,5},{8,10},{9,11},{10,... | collective-permute-start | bytes 1769480 | tf_op jit(solution)/shard_map/ppermute | solution.py:246
  251.2 16.9 %copy-start.18 = (bf16[4,72,1024]{2,1,0:T(8,128)(2,1)S(1)}, bf16[4,72,1024]{2,1,0:T(8,128)(2,1)}, u32[]{:S(2)}) copy-start(bf16[4,72,1024]{2,1,0:T(8,128)(2,1)} %copy-done.16) | copy-start | bytes 1769476
  251.2 16.9 %copy-start.58 = (bf16[1152,1024]{1,0:T(8,128)(2,1)S(1)}, bf16[1152,1024]{1,0:T(8,128)(2,1)}, u32[]{:S(2)}) copy-start(bf16[1152,1024]{1,0:T(8,128)(2,1)} %copy.80) | copy-start | bytes 7077892
  272.3 39.1 %collective-permute-start.22 = (bf16[2,2,144,576]{3,2,1,0:T(8,128)(2,1)}, bf16[2,2,144,576]{3,2,1,0:T(8,128)(2,1)}, u32[]{:S(2)}, u32[]{:S(2)}) collective-permute-start(bf16[2,2,144,576]{3,2,1,0:T(8,128)(2,1)} %fusion.95), channel_id=1, source_target_pairs={{0,4},{4,0},{8,12},{12,8},{16,20},{20,16},{24,28},{28,24},{1,5},{5... | collective-permute-start | bytes 1990664 | tf_op jit(solution)/shard_map/ppermute | solution.py:246
  291.9 26.0 %collective-permute-start.23 = (bf16[2,2,144,576]{3,2,1,0:T(8,128)(2,1)}, bf16[2,2,144,576]{3,2,1,0:T(8,128)(2,1)}, u32[]{:S(2)}, u32[]{:S(2)}) collective-permute-start(bf16[2,2,144,576]{3,2,1,0:T(8,128)(2,1)} %fusion.101), channel_id=1, source_target_pairs={{0,4},{4,0},{8,12},{12,8},{16,20},{20,16},{24,28},{28,24},{1,5},{5... | collective-permute-start | bytes 1990664 | tf_op jit(solution)/shard_map/ppermute | solution.py:246
  309.3 20.6 %collective-permute-start.27 = (f32[17,1728]{1,0:T(8,128)}, f32[17,1728]{1,0:T(8,128)}, u32[]{:S(2)}, u32[]{:S(2)}) collective-permute-start(f32[17,1728]{1,0:T(8,128)} %get-tuple-element.147), channel_id=1, source_target_pairs={{0,3},{1,2},{2,1},{3,0},{4,7},{5,6},{6,5},{7,4},{8,11},{9,10},{10,... | collective-permute-start | bytes 352520 | tf_op jit(solution)/shard_map/ppermute | solution.py:246
  309.3 20.6 %collective-permute-start.25 = (f32[17,1728]{1,0:T(8,128)}, f32[17,1728]{1,0:T(8,128)}, u32[]{:S(2)}, u32[]{:S(2)}) collective-permute-start(f32[17,1728]{1,0:T(8,128)} %get-tuple-element.148), channel_id=1, source_target_pairs={{0,1},{1,0},{2,3},{3,2},{4,5},{5,4},{6,7},{7,6},{8,9},{9,8},{10,11... | collective-permute-start | bytes 352520 | tf_op jit(solution)/shard_map/ppermute | solution.py:246
  309.9 19.9 %collective-permute-start.26 = (f32[17,1728]{1,0:T(8,128)S(1)}, f32[17,1728]{1,0:T(8,128)}, u32[]{:S(2)}, u32[]{:S(2)}) collective-permute-start(f32[17,1728]{1,0:T(8,128)S(1)} %get-tuple-element.149), channel_id=1, source_target_pairs={{0,2},{1,3},{2,0},{3,1},{4,6},{5,7},{6,4},{7,5},{8,10},{9,11},{10,... | collective-permute-start | bytes 352520 | tf_op jit(solution)/shard_map/ppermute | solution.py:246
  328.1 7.8 %collective-permute-start.24 = (bf16[2,288,1024]{2,1,0:T(8,128)(2,1)S(1)}, bf16[2,288,1024]{2,1,0:T(8,128)(2,1)S(1)}, u32[]{:S(2)}, u32[]{:S(2)}) collective-permute-start(bf16[2,288,1024]{2,1,0:T(8,128)(2,1)S(1)} %dynamic-slice_bitcast_fusion), channel_id=1, source_target_pairs={{0,1},{1,0},{2,3},{3,2},{4,5},{5,4},{6,7},{7,6},{8,9},{9,8},{10,11... | collective-permute-start | bytes 3538952 | tf_op jit(solution)/shard_map/ppermute | solution.py:246
  331.0 6.8 %collective-permute-start.28 = (f32[20,1728]{1,0:T(8,128)S(1)}, f32[20,1728]{1,0:T(8,128)S(1)}, u32[]{:S(2)}, u32[]{:S(2)}) collective-permute-start(f32[20,1728]{1,0:T(8,128)S(1)} %pad_maximum_fusion.8), channel_id=1, source_target_pairs={{0,4},{4,0},{8,12},{12,8},{16,20},{20,16},{24,28},{28,24},{1,5},{5... | collective-permute-start | bytes 414728 | tf_op jit(solution)/shard_map/ppermute | solution.py:246
  337.9 10.3 %collective-permute-start.29 = (f32[20,1728]{1,0:T(8,128)S(1)}, f32[20,1728]{1,0:T(8,128)S(1)}, u32[]{:S(2)}, u32[]{:S(2)}) collective-permute-start(f32[20,1728]{1,0:T(8,128)S(1)} %fusion.195), channel_id=1, source_target_pairs={{0,8},{4,12},{8,0},{12,4},{16,24},{20,28},{24,16},{28,20},{1,9},{5... | collective-permute-start | bytes 414728 | tf_op jit(solution)/shard_map/ppermute | solution.py:246
  341.7 41.8 %collective-permute-start.35 = (bf16[2,144,576]{2,1,0:T(8,128)(2,1)}, bf16[2,144,576]{2,1,0:T(8,128)(2,1)S(1)}, u32[]{:S(2)}, u32[]{:S(2)}) collective-permute-start(bf16[2,144,576]{2,1,0:T(8,128)(2,1)} %dynamic-slice_bitcast_fusion.5), channel_id=1, source_target_pairs={{0,16},{4,20},{8,24},{12,28},{16,0},{20,4},{24,8},{28,12},{1,17},{... | collective-permute-start | bytes 995336 | tf_op jit(solution)/shard_map/ppermute | solution.py:246
  342.7 40.7 %collective-permute-start.37 = (bf16[2,144,576]{2,1,0:T(8,128)(2,1)}, bf16[2,144,576]{2,1,0:T(8,128)(2,1)S(1)}, u32[]{:S(2)}, u32[]{:S(2)}) collective-permute-start(bf16[2,144,576]{2,1,0:T(8,128)(2,1)} %dynamic-slice_bitcast_fusion.4), channel_id=1, source_target_pairs={{0,16},{4,20},{8,24},{12,28},{16,0},{20,4},{24,8},{28,12},{1,17},{... | collective-permute-start | bytes 995336 | tf_op jit(solution)/shard_map/ppermute | solution.py:246
  348.1 35.3 %collective-permute-start.30 = (f32[20,1728]{1,0:T(8,128)S(1)}, f32[20,1728]{1,0:T(8,128)S(1)}, u32[]{:S(2)}, u32[]{:S(2)}) collective-permute-start(f32[20,1728]{1,0:T(8,128)S(1)} %add.730), channel_id=1, source_target_pairs={{0,16},{4,20},{8,24},{12,28},{16,0},{20,4},{24,8},{28,12},{1,17},{... | collective-permute-start | bytes 414728 | tf_op jit(solution)/shard_map/ppermute | solution.py:246
  350.2 39.5 %copy-start.51 = (bf16[2,2,144,576]{3,2,1,0:T(8,128)(2,1)S(1)}, bf16[2,2,144,576]{3,2,1,0:T(8,128)(2,1)}, u32[]{:S(2)}) copy-start(bf16[2,2,144,576]{3,2,1,0:T(8,128)(2,1)} %copy-done.50) | copy-start | bytes 1990660
  350.2 54.3 %collective-permute-start.31 = (bf16[288,1024]{1,0:T(8,128)(2,1)S(1)}, bf16[288,1024]{1,0:T(8,128)(2,1)}, u32[]{:S(2)}, u32[]{:S(2)}) collective-permute-start(bf16[288,1024]{1,0:T(8,128)(2,1)S(1)} %fusion.108), channel_id=1, source_target_pairs={{0,2},{1,3},{2,0},{3,1},{4,6},{5,7},{6,4},{7,5},{8,10},{9,11},{10,... | collective-permute-start | bytes 1769480 | tf_op jit(solution)/shard_map/ppermute | solution.py:246
  387.8 8.0 %collective-permute-start.32 = (f32[2,288]{1,0:T(2,128)S(1)}, f32[2,288]{1,0:T(2,128)S(1)}, u32[]{:S(2)}, u32[]{:S(2)}) collective-permute-start(f32[2,288]{1,0:T(2,128)S(1)} %bitcast.467), channel_id=1, source_target_pairs={{0,1},{1,0},{2,3},{3,2},{4,5},{5,4},{6,7},{7,6},{8,9},{9,8},{10,11... | collective-permute-start | bytes 6920 | tf_op jit(solution)/shard_map/ppermute | solution.py:246
  387.8 10.0 %collective-permute-start.33 = (f32[2,288]{1,0:T(2,128)S(1)}, f32[2,288]{1,0:T(2,128)S(1)}, u32[]{:S(2)}, u32[]{:S(2)}) collective-permute-start(f32[2,288]{1,0:T(2,128)S(1)} %bitcast.466), channel_id=1, source_target_pairs={{0,2},{1,3},{2,0},{3,1},{4,6},{5,7},{6,4},{7,5},{8,10},{9,11},{10,... | collective-permute-start | bytes 6920 | tf_op jit(solution)/shard_map/ppermute | solution.py:246
  389.1 8.8 %collective-permute-start.34 = (f32[2,288]{1,0:T(2,128)S(1)}, f32[2,288]{1,0:T(2,128)S(1)}, u32[]{:S(2)}, u32[]{:S(2)}) collective-permute-start(f32[2,288]{1,0:T(2,128)S(1)} %bitcast.465), channel_id=1, source_target_pairs={{0,3},{1,2},{2,1},{3,0},{4,7},{5,6},{6,5},{7,4},{8,11},{9,10},{10,... | collective-permute-start | bytes 6920 | tf_op jit(solution)/shard_map/ppermute | solution.py:246
  389.8 8.6 %collective-permute-start.38 = (bf16[144,576]{1,0:T(8,128)(2,1)S(1)}, bf16[144,576]{1,0:T(8,128)(2,1)S(1)}, u32[]{:S(2)}, u32[]{:S(2)}) collective-permute-start(bf16[144,576]{1,0:T(8,128)(2,1)S(1)} %dynamic-slice_bitcast_fusion.6), channel_id=1, source_target_pairs={{0,8},{4,12},{8,0},{12,4},{16,24},{20,28},{24,16},{28,20},{1,9},{5... | collective-permute-start | bytes 497672 | tf_op jit(solution)/shard_map/ppermute | solution.py:246
  395.8 6.9 %collective-permute-start.36 = (bf16[144,576]{1,0:T(8,128)(2,1)S(1)}, bf16[144,576]{1,0:T(8,128)(2,1)S(1)}, u32[]{:S(2)}, u32[]{:S(2)}) collective-permute-start(bf16[144,576]{1,0:T(8,128)(2,1)S(1)} %dynamic-slice_bitcast_fusion.7), channel_id=1, source_target_pairs={{0,8},{4,12},{8,0},{12,4},{16,24},{20,28},{24,16},{28,20},{1,9},{5... | collective-permute-start | bytes 497672 | tf_op jit(solution)/shard_map/ppermute | solution.py:246
  (86 other events, 371.1 us)
Sparse Core Ops, SparseCore 0:
  157.4 73.5 reduce-scatter.4
  235.1 93.1 reduce-scatter.2
